TPU v7x, 128 devices: a whole 4x4x4 slice. The times are simulated.
128 devices in a mesh: section: 4 (over z), expert: 4 (over y), dp: 8 (over x, core).
Axes of the slice: x: 4, y: 4, z: 4, core: 2. Of those that a mesh axis runs over, the one named last changes fastest.
Arguments:
- tokens: bfloat16 [2, 2048, 2048], P(None, ('expert', 'dp')), may hold values from -24 to 24
- expert_ids: int32 [4, 2, 2048, 4], P('section', None, ('expert', 'dp')), may hold values from 0 to 31, all different within a row; in each aligned block of 64 rows (0 to 63, 64 to 127, ..., all dimensions but the last counted through in order) at most 16 rows name the same one
- labels: int32 [2, 2048], P(None, ('expert', 'dp')), may hold values from 0 to 127
- router: bfloat16 [4, 2048, 32], P('section'), may hold values from -0.125 to 0.125
- class_head: bfloat16 [2048, 128], replicated, may hold values from -0.5 to 0.5
- w_gate: bfloat16 [4, 32, 2048, 768], P('section', ('expert', 'dp')), may hold values from -0.125 to 0.125
- w_up: bfloat16 [4, 32, 2048, 768], P('section', ('expert', 'dp')), may hold values from -0.125 to 0.125
- w_down: bfloat16 [4, 32, 768, 2048], P('section', ('expert', 'dp')), may hold values from -0.21875 to 0.21875
Outputs:
- mean_loss: float32 [], replicated
- grad_head: float32 [2048, 128], replicated
- grad_router: float32 [4, 2048, 32], P('section')
- grad_gate: bfloat16 [4, 32, 2048, 768], P('section', ('expert', 'dp'))
- grad_up: bfloat16 [4, 32, 2048, 768], P('section', ('expert', 'dp'))
- grad_down: bfloat16 [4, 32, 768, 2048], P('section', ('expert', 'dp'))
Inputs may be any that keep to these rules, and one draw needn't show every extreme that they name: `expert_ids`: each token names 4 different experts; among the 64 tokens of one device in one micro-batch and layer no expert is named more than 16 times, a bound that some block reaches.
All inputs are finite; a program needn't handle non-finite values.
Results may differ from a plain program's by a relative error of at most 0.025.
Values may be sent and summed in bfloat16 or wider, within the bound.
No kernel may reach another device: no remote copies, remote signals or barrier semaphores. Data moves between devices by JAX's collectives and lax.ppermute only.
A program may use at most 320 MiB of HBM per device.

v0:
```python
import jax
import jax.numpy as jnp
from jax import lax
from jax.sharding import PartitionSpec as P

soft_cap = 30.0
norm_eps = 1e-06
tile_rows = 128


def from_behind(block, axis, distance):
    devices = range(lax.axis_size(axis))
    route = [(i - distance, i) for i in devices if i - distance in devices]
    return lax.ppermute(block, axis, route)


def spread(array, axis, root):
    mine = lax.axis_index(axis) == root
    return lax.psum(jnp.where(mine, array, jnp.zeros_like(array)), axis)


def over_pieces(array, axis):
    parts = lax.all_gather(array, axis).astype(jnp.float32)
    return parts.sum(axis=0)


def capped(values):
    return soft_cap * jnp.tanh(values / soft_cap)


def normalize(layer_in):
    hidden_f = layer_in.astype(jnp.float32)
    inv_rms = lax.rsqrt(jnp.mean(hidden_f * hidden_f, axis=-1, keepdims=True) + norm_eps)
    return (hidden_f, inv_rms, (hidden_f * inv_rms).astype(jnp.bfloat16))


def gate_probs(normed, ids_now, router_w):
    logits = jnp.dot(normed, router_w, preferred_element_type=jnp.float32)
    one_hot = (
        ids_now[:, :, None] == jnp.arange(router_w.shape[1], dtype=jnp.int32)[None, None, :]
    ).astype(jnp.float32)
    chosen = capped(jnp.sum(one_hot * logits[:, None, :], axis=-1))
    weights = jnp.exp(chosen)
    return (one_hot, chosen, weights / jnp.sum(weights, axis=-1, keepdims=True))


def contract_first(left, right):
    return lax.dot_general(
        left, right, (((0,), (0,)), ((), ())), preferred_element_type=jnp.float32
    )


def contract_last(left, right):
    return lax.dot_general(
        left, right, (((1,), (1,)), ((), ())), preferred_element_type=jnp.float32
    )


def take_slot(stored, micro_at):
    return lax.dynamic_index_in_dim(stored, micro_at, 0, keepdims=False)


def keep_slot(stored, fresh, micro_at, active):
    return lax.dynamic_update_index_in_dim(
        stored, jnp.where(active, fresh, take_slot(stored, micro_at)), micro_at, 0
    )


def placement_rows(ids_now, active, expert_count):
    flat_ids = ids_now.reshape(-1)
    one_hot = (flat_ids[:, None] == jnp.arange(expert_count, dtype=jnp.int32)[None, :]).astype(
        jnp.int32
    )
    one_hot = one_hot * active.astype(jnp.int32)
    before = jnp.cumsum(one_hot, axis=0) - one_hot
    slot_of = jnp.sum(before * one_hot, axis=1)
    counts = jnp.sum(one_hot, axis=0)
    target = jnp.where(active, flat_ids, expert_count)
    return (target, slot_of, counts)


def packing(live_rows, slot_count, buffer_rows):
    offsets = jnp.cumsum(live_rows) - live_rows
    slot_ids = jnp.arange(slot_count, dtype=jnp.int32)
    packed_at = offsets[:, None] + slot_ids[None, :]
    dest_row = jnp.where(slot_ids[None, :] < live_rows[:, None], packed_at, buffer_rows).reshape(-1)
    fetch_row = jnp.minimum(packed_at, buffer_rows - 1).reshape(-1)
    return (dest_row, fetch_row)


def send_tokens(payload, counts):
    return (
        lax.all_to_all(payload, ("expert", "dp"), split_axis=0, concat_axis=0, tiled=True),
        lax.all_to_all(counts, ("expert", "dp"), split_axis=0, concat_axis=0, tiled=True),
    )


def route_rows(payload):
    return lax.all_to_all(payload, ("expert", "dp"), split_axis=0, concat_axis=0, tiled=True)


def expert_forward(packed, gate_w, up_w, down_w):
    gate_act = jnp.dot(packed, gate_w, preferred_element_type=jnp.float32)
    up_act = jnp.dot(packed, up_w, preferred_element_type=jnp.float32)
    hidden_act = (gate_act * jax.nn.sigmoid(gate_act) * up_act).astype(jnp.bfloat16)
    return jnp.dot(hidden_act, down_w, preferred_element_type=jnp.float32).astype(jnp.bfloat16)


def expert_backward(packed, packed_grad, gate_w, up_w, down_w, grad_sums):
    grad_gate, grad_up, grad_down = grad_sums
    gate_act = jnp.dot(packed, gate_w, preferred_element_type=jnp.float32)
    up_act = jnp.dot(packed, up_w, preferred_element_type=jnp.float32)
    sigmoid_gate = jax.nn.sigmoid(gate_act)
    silu_gate = gate_act * sigmoid_gate
    hidden_act = (silu_gate * up_act).astype(jnp.bfloat16)
    grad_down = grad_down + contract_first(hidden_act, packed_grad)
    grad_hidden = contract_last(packed_grad, down_w)
    grad_gate_act = (
        grad_hidden * up_act * sigmoid_gate * (1.0 + gate_act * (1.0 - sigmoid_gate))
    ).astype(jnp.bfloat16)
    grad_up_act = (grad_hidden * silu_gate).astype(jnp.bfloat16)
    grad_gate = grad_gate + contract_first(packed, grad_gate_act)
    grad_up = grad_up + contract_first(packed, grad_up_act)
    results = (contract_last(grad_gate_act, gate_w) + contract_last(grad_up_act, up_w)).astype(
        jnp.bfloat16
    )
    return (grad_gate, grad_up, grad_down, results)


def shards(tokens, expert_ids, labels, router, class_head, w_gate, w_up, w_down):
    section_count = lax.axis_size("section")
    section_index = lax.axis_index("section")
    expert_count = lax.axis_size(("expert", "dp"))
    micro_count, tok_rows, model_width = tokens.shape
    top_count = expert_ids.shape[3]
    slot_count = 2 * tok_rows * top_count // expert_count
    buffer_rows = (expert_count * slot_count + tile_rows - 1) // tile_rows * tile_rows
    route_ids = expert_ids[0]
    router_w = router[0]
    gate_w = w_gate[0, 0]
    up_w = w_up[0, 0]
    down_w = w_down[0, 0]
    hidden_dim = gate_w.shape[1]
    is_last = section_index == section_count - 1
    tick_count = micro_count + section_count - 1
    saved_in = jnp.zeros((micro_count, tok_rows, model_width), jnp.bfloat16)
    saved_out = jnp.zeros((micro_count, tok_rows, top_count, model_width), jnp.bfloat16)
    saved_packed = jnp.zeros((micro_count, buffer_rows, model_width), jnp.bfloat16)
    saved_live = jnp.zeros((micro_count, expert_count), jnp.int32)
    finals = jnp.zeros((micro_count, tok_rows, model_width), jnp.bfloat16)
    incoming = jnp.zeros((tok_rows, model_width), jnp.bfloat16)
    for tick_num in range(tick_count):
        micro_at = tick_num - section_index
        active = (micro_at >= 0) & (micro_at < micro_count)
        micro_at = jnp.clip(micro_at, 0, micro_count - 1)
        layer_in = jnp.where(section_index == 0, take_slot(tokens, micro_at), incoming)
        hidden_f, inv_rms, normed = normalize(layer_in)
        ids_now = take_slot(route_ids, micro_at)
        one_hot, chosen, probs = gate_probs(normed, ids_now, router_w)
        target, slot_of, counts = placement_rows(ids_now, active, expert_count)
        source_rows = jnp.broadcast_to(
            normed[:, None, :], (tok_rows, top_count, model_width)
        ).reshape(-1, model_width)
        outgoing = (
            jnp.zeros((expert_count, slot_count, model_width), jnp.bfloat16)
            .at[target, slot_of]
            .set(source_rows, mode="drop")
        )
        arrived, arrived_counts = send_tokens(
            outgoing, counts.astype(jnp.bfloat16).reshape(expert_count, 1)
        )
        live_rows = arrived_counts[:, 0].astype(jnp.int32)
        dest_row, fetch_row = packing(live_rows, slot_count, buffer_rows)
        packed = (
            jnp.zeros((buffer_rows, model_width), jnp.bfloat16)
            .at[dest_row]
            .set(arrived.reshape(-1, model_width), mode="drop")
        )
        results = expert_forward(packed, gate_w, up_w, down_w)
        returned = route_rows(results[fetch_row].reshape(expert_count, slot_count, model_width))
        expert_out = returned[jnp.minimum(target, expert_count - 1), slot_of].reshape(
            tok_rows, top_count, model_width
        )
        layer_out = (
            hidden_f + jnp.sum(probs[:, :, None] * expert_out.astype(jnp.float32), axis=1)
        ).astype(jnp.bfloat16)
        saved_in = keep_slot(saved_in, layer_in, micro_at, active)
        saved_out = keep_slot(saved_out, expert_out, micro_at, active)
        saved_packed = keep_slot(saved_packed, packed, micro_at, active)
        saved_live = keep_slot(saved_live, live_rows, micro_at, active)
        finals = keep_slot(finals, layer_out, micro_at, active & is_last)
        if tick_num + 1 < tick_count:
            incoming = from_behind(layer_out, "section", 1)
    all_rows = micro_count * tok_rows
    share_rows = all_rows // section_count
    final_all = spread(finals.reshape(-1, model_width), "section", section_count - 1)
    final_rows = lax.dynamic_slice_in_dim(final_all, section_index * share_rows, share_rows, 0)
    label_rows = lax.dynamic_slice_in_dim(
        labels.reshape(-1), section_index * share_rows, share_rows, 0
    )
    class_logits = capped(jnp.dot(final_rows, class_head, preferred_element_type=jnp.float32))
    class_weights = jnp.exp(class_logits)
    class_total = jnp.sum(class_weights, axis=-1, keepdims=True)
    label_hot = (
        label_rows[:, None] == jnp.arange(class_head.shape[1], dtype=jnp.int32)[None, :]
    ).astype(jnp.float32)
    token_loss = jnp.log(class_total[:, 0]) - jnp.sum(label_hot * class_logits, axis=-1)
    scaled = class_logits / soft_cap
    grad_logits = ((class_weights / class_total - label_hot) * (1.0 - scaled * scaled)).astype(
        jnp.bfloat16
    )
    head_term = contract_first(final_rows, grad_logits)
    loss_term = jnp.sum(token_loss)
    top_share = contract_last(grad_logits, class_head).astype(jnp.bfloat16)
    grad_top = lax.all_gather(top_share, "section", axis=0, tiled=True).reshape(
        micro_count, tok_rows, model_width
    )
    grad_gate = jnp.zeros((model_width, hidden_dim), jnp.float32)
    grad_up = jnp.zeros((model_width, hidden_dim), jnp.float32)
    grad_down = jnp.zeros((hidden_dim, model_width), jnp.float32)
    grad_router = jnp.zeros(router_w.shape, jnp.float32)
    incoming_grad = jnp.zeros((tok_rows, model_width), jnp.bfloat16)
    for tick_num in range(tick_count):
        micro_at = micro_count - 1 - tick_num + (section_count - 1 - section_index)
        active = (micro_at >= 0) & (micro_at < micro_count)
        micro_at = jnp.clip(micro_at, 0, micro_count - 1)
        grad_out = jnp.where(is_last, take_slot(grad_top, micro_at), incoming_grad)
        layer_in = take_slot(saved_in, micro_at)
        expert_out = take_slot(saved_out, micro_at)
        hidden_f, inv_rms, normed = normalize(layer_in)
        ids_now = take_slot(route_ids, micro_at)
        one_hot, chosen, probs = gate_probs(normed, ids_now, router_w)
        grad_f = grad_out.astype(jnp.float32)
        grad_prob = jnp.sum(grad_f[:, None, :] * expert_out.astype(jnp.float32), axis=-1)
        grad_rows = (
            (probs[:, :, None] * grad_f[:, None, :]).astype(jnp.bfloat16).reshape(-1, model_width)
        )
        target, slot_of, counts = placement_rows(ids_now, active, expert_count)
        outgoing = (
            jnp.zeros((expert_count, slot_count, model_width), jnp.bfloat16)
            .at[target, slot_of]
            .set(grad_rows, mode="drop")
        )
        arrived = route_rows(outgoing)
        live_rows = take_slot(saved_live, micro_at) * active.astype(jnp.int32)
        dest_row, fetch_row = packing(live_rows, slot_count, buffer_rows)
        packed_grad = (
            jnp.zeros((buffer_rows, model_width), jnp.bfloat16)
            .at[dest_row]
            .set(arrived.reshape(-1, model_width), mode="drop")
        )
        packed_in = jnp.where(
            active, take_slot(saved_packed, micro_at), jnp.zeros((), jnp.bfloat16)
        )
        grad_gate, grad_up, grad_down, results = expert_backward(
            packed_in, packed_grad, gate_w, up_w, down_w, (grad_gate, grad_up, grad_down)
        )
        returned = route_rows(results[fetch_row].reshape(expert_count, slot_count, model_width))
        grad_parts = returned[jnp.minimum(target, expert_count - 1), slot_of].reshape(
            tok_rows, top_count, model_width
        )
        scaled = chosen / soft_cap
        grad_chosen = (
            probs
            * (grad_prob - jnp.sum(probs * grad_prob, axis=-1, keepdims=True))
            * (1.0 - scaled * scaled)
        )
        grad_route = jnp.sum(grad_chosen[:, :, None] * one_hot, axis=1).astype(jnp.bfloat16)
        grad_router = grad_router + jnp.where(active, contract_first(normed, grad_route), 0.0)
        grad_normed = jnp.sum(grad_parts.astype(jnp.float32), axis=1) + contract_last(
            grad_route, router_w
        )
        normed_f = hidden_f * inv_rms
        grad_in = (
            grad_f
            + inv_rms
            * (grad_normed - normed_f * jnp.mean(grad_normed * normed_f, axis=-1, keepdims=True))
        ).astype(jnp.bfloat16)
        if tick_num + 1 < tick_count:
            incoming_grad = from_behind(grad_in, "section", -1)
    head_total, loss_total = lax.psum((head_term, loss_term), ("section", "expert", "dp"))
    router_out = over_pieces(grad_router.astype(jnp.bfloat16), ("expert", "dp")).astype(
        jnp.float32
    )[None]
    mean_loss = loss_total / (micro_count * tok_rows * expert_count)
    return (
        mean_loss,
        head_total,
        router_out,
        grad_gate.astype(jnp.bfloat16)[None, None],
        grad_up.astype(jnp.bfloat16)[None, None],
        grad_down.astype(jnp.bfloat16)[None, None],
    )


def solution(mesh):
    return jax.shard_map(
        shards,
        mesh=mesh,
        in_specs=(
            P(None, ("expert", "dp"), None),
            P("section", None, ("expert", "dp"), None),
            P(None, ("expert", "dp")),
            P("section", None, None),
            P(),
            P("section", ("expert", "dp"), None, None),
            P("section", ("expert", "dp"), None, None),
            P("section", ("expert", "dp"), None, None),
        ),
        out_specs=(
            P(),
            P(),
            P("section", None, None),
            P("section", ("expert", "dp"), None, None),
            P("section", ("expert", "dp"), None, None),
            P("section", ("expert", "dp"), None, None),
        ),
        check_vma=False,
    )
```

profile of v0, /device:TPU:1, one launch (start us, length us, event | category | flops | bytes accessed | tf_op | source)
XLA Modules:
  0.0 1967.2 jit_solution(12000700485298113830)
XLA Ops:
  11.3 8.6 all-to-all-start
  27.6 46.2 %scatter_fusion = bf16[32,16,2048]{2,1,0:T(8,128)(2,1)} fusion(bf16[32,16,2048]{2,1,0:T(8,128)(2,1)} %broadcast.1924.clone, s32[256]{0:T(256)S(1)} %bitcast.733, bf16[256,2048]{1,0:T(8,128)(2,1)} %reshape.2808), kind=kCustom, calls=%fused_computation.18 | custom fusion | bytes 3147776 | tf_op jit(solution)/shard_map/scatter | solution.py:167
  73.8 7.4 all-to-all-start.1
  82.9 26.2 %all-to-all-done.1 = bf16[32,16,2048]{2,1,0:T(8,128)(2,1)} async-done(((bf16[32,16,2048]{2,1,0:T(8,128)(2,1)}), bf16[32,16,2048]{2,1,0:T(8,128)(2,1)}, u32[]{:S(2)}, u32[]{:S(2)}) %all-to-all-start.1) | async-done | bytes 2097184 | tf_op jit(solution)/shard_map/all_to_all | solution.py:93
  121.1 8.3 fusion.76
  129.4 7.1 gather_fusion
  148.3 23.1 %all-to-all-done.2 = bf16[32,16,2048]{2,1,0:T(8,128)(2,1)} async-done(((bf16[32,16,2048]{2,1,0:T(8,128)(2,1)}), bf16[32,16,2048]{2,1,0:T(8,128)(2,1)}, u32[]{:S(2)}, u32[]{:S(2)}) %all-to-all-start.2) | async-done | bytes 2097184 | tf_op jit(solution)/shard_map/all_to_all | solution.py:99
  210.6 46.2 %scatter_fusion.1 = bf16[32,16,2048]{2,1,0:T(8,128)(2,1)} fusion(bf16[32,16,2048]{2,1,0:T(8,128)(2,1)} %broadcast.1924.clone.1, s32[256]{0:T(256)S(1)} %bitcast.737, bf16[256,2048]{1,0:T(8,128)(2,1)} %reshape.2822), kind=kCustom, calls=%fused_computation.20 | custom fusion | bytes 3147776 | tf_op jit(solution)/shard_map/scatter | solution.py:167
  256.8 8.6 all-to-all-start.4
  269.6 23.6 %all-to-all-done.4 = bf16[32,16,2048]{2,1,0:T(8,128)(2,1)} async-done(((bf16[32,16,2048]{2,1,0:T(8,128)(2,1)}), bf16[32,16,2048]{2,1,0:T(8,128)(2,1)}, u32[]{:S(2)}, u32[]{:S(2)}) %all-to-all-start.4) | async-done | bytes 2097184 | tf_op jit(solution)/shard_map/all_to_all | solution.py:93
  305.0 8.3 fusion.79
  313.3 7.1 gather_fusion.2
  331.8 23.2 %all-to-all-done.5 = bf16[32,16,2048]{2,1,0:T(8,128)(2,1)} async-done(((bf16[32,16,2048]{2,1,0:T(8,128)(2,1)}), bf16[32,16,2048]{2,1,0:T(8,128)(2,1)}, u32[]{:S(2)}, u32[]{:S(2)}) %all-to-all-start.5) | async-done | bytes 2097184 | tf_op jit(solution)/shard_map/all_to_all | solution.py:99
  386.8 8.2 all-to-all-start.9
  408.5 40.3 %scatter_fusion.2 = bf16[32,16,2048]{2,1,0:T(8,128)(2,1)} fusion(bf16[32,16,2048]{2,1,0:T(8,128)(2,1)} %broadcast.1924.clone.2, s32[256]{0:T(256)S(1)} %bitcast.741, bf16[256,2048]{1,0:T(8,128)(2,1)} %reshape.2836), kind=kCustom, calls=%fused_computation.22 | custom fusion | bytes 3147776 | tf_op jit(solution)/shard_map/scatter | solution.py:167
  448.8 7.4 all-to-all-start.7
  458.7 25.5 %all-to-all-done.7 = bf16[32,16,2048]{2,1,0:T(8,128)(2,1)} async-done(((bf16[32,16,2048]{2,1,0:T(8,128)(2,1)}), bf16[32,16,2048]{2,1,0:T(8,128)(2,1)}, u32[]{:S(2)}, u32[]{:S(2)}) %all-to-all-start.7) | async-done | bytes 2097184 | tf_op jit(solution)/shard_map/all_to_all | solution.py:93
  495.8 8.3 fusion.82
  504.1 7.1 gather_fusion.4
  522.7 23.2 %all-to-all-done.8 = bf16[32,16,2048]{2,1,0:T(8,128)(2,1)} async-done(((bf16[32,16,2048]{2,1,0:T(8,128)(2,1)}), bf16[32,16,2048]{2,1,0:T(8,128)(2,1)}, u32[]{:S(2)}, u32[]{:S(2)}) %all-to-all-start.8) | async-done | bytes 2097184 | tf_op jit(solution)/shard_map/all_to_all | solution.py:99
  545.9 13.1 gather_fusion.5
  581.8 40.3 %scatter_fusion.3 = bf16[32,16,2048]{2,1,0:T(8,128)(2,1)} fusion(bf16[32,16,2048]{2,1,0:T(8,128)(2,1)} %broadcast.1924.clone.3, s32[256]{0:T(256)S(1)} %bitcast.745, bf16[256,2048]{1,0:T(8,128)(2,1)} %reshape.2850), kind=kCustom, calls=%fused_computation.24 | custom fusion | bytes 3147776 | tf_op jit(solution)/shard_map/scatter | solution.py:167
  622.1 8.1 all-to-all-start.10
  631.9 26.2 %all-to-all-done.10 = bf16[32,16,2048]{2,1,0:T(8,128)(2,1)} async-done(((bf16[32,16,2048]{2,1,0:T(8,128)(2,1)}), bf16[32,16,2048]{2,1,0:T(8,128)(2,1)}, u32[]{:S(2)}, u32[]{:S(2)}) %all-to-all-start.10) | async-done | bytes 2097184 | tf_op jit(solution)/shard_map/all_to_all | solution.py:93
  669.7 8.3 fusion.85
  685.1 7.1 all-to-all-start.11
  699.9 20.1 %all-to-all-done.11 = bf16[32,16,2048]{2,1,0:T(8,128)(2,1)} async-done(((bf16[32,16,2048]{2,1,0:T(8,128)(2,1)}), bf16[32,16,2048]{2,1,0:T(8,128)(2,1)}, u32[]{:S(2)}, u32[]{:S(2)}) %all-to-all-start.11) | async-done | bytes 2097184 | tf_op jit(solution)/shard_map/all_to_all | solution.py:99
  720.1 13.1 gather_fusion.7
  757.8 40.3 %scatter_fusion.4 = bf16[32,16,2048]{2,1,0:T(8,128)(2,1)} fusion(bf16[32,16,2048]{2,1,0:T(8,128)(2,1)} %broadcast.1924.clone.4, s32[256]{0:T(256)S(1)} %bitcast.749, bf16[256,2048]{1,0:T(8,128)(2,1)} %reshape.2864), kind=kCustom, calls=%fused_computation.26 | custom fusion | bytes 3147776 | tf_op jit(solution)/shard_map/scatter | solution.py:167
  798.1 7.4 all-to-all-start.13
  845.2 8.3 fusion.88
  880.8 14.5 all-to-all-done.14
  895.3 13.1 gather_fusion.9
  921.4 35.3 %all-reduce.3.cloned.1.call-done = bf16[128,2048]{1,0:T(8,128)(2,1)} async-done(((bf16[128,2048]{1,0:T(8,128)(2,1)}), bf16[128,2048]{1,0:T(8,128)(2,1)}) %all-reduce.3.cloned.1.call-update) | async-done | bytes 524304 | tf_op jit(solution)/shard_map/psum | solution.py:19
  960.0 10.1 all_gather.9
  983.2 40.3 %scatter_fusion.5 = bf16[32,16,2048]{2,1,0:T(8,128)(2,1)} fusion(bf16[32,16,2048]{2,1,0:T(8,128)(2,1)} %broadcast.1924.clone.5, s32[256]{0:T(256)S(1)} %bitcast.750, bf16[256,2048]{1,0:T(8,128)(2,1)} %multiply_convert_fusion.4), kind=kCustom, calls=%fused_computation.28 | custom fusion | bytes 3147776 | tf_op jit(solution)/shard_map/scatter | solution.py:242
  1023.5 13.3 all-to-all-start.15
  1047.9 16.8 all-to-all-done.15
  1091.6 7.2 all-to-all-start.16
  1098.8 27.8 %all-to-all-done.16 = bf16[32,16,2048]{2,1,0:T(8,128)(2,1)} async-done(((bf16[32,16,2048]{2,1,0:T(8,128)(2,1)}), bf16[32,16,2048]{2,1,0:T(8,128)(2,1)}, u32[]{:S(2)}, u32[]{:S(2)}) %all-to-all-start.16) | async-done | bytes 2097184 | tf_op jit(solution)/shard_map/all_to_all | solution.py:99
  1126.6 13.1 gather_fusion.11
  1167.7 40.3 %scatter_fusion.6 = bf16[32,16,2048]{2,1,0:T(8,128)(2,1)} fusion(bf16[32,16,2048]{2,1,0:T(8,128)(2,1)} %broadcast.1924.clone.6, s32[256]{0:T(256)S(1)} %bitcast.746, bf16[256,2048]{1,0:T(8,128)(2,1)} %multiply_convert_fusion.3), kind=kCustom, calls=%fused_computation.30 | custom fusion | bytes 3147776 | tf_op jit(solution)/shard_map/scatter | solution.py:242
  1208.0 9.0 all-to-all-start.17
  1222.1 22.6 %all-to-all-done.17 = bf16[32,16,2048]{2,1,0:T(8,128)(2,1)} async-done(((bf16[32,16,2048]{2,1,0:T(8,128)(2,1)}), bf16[32,16,2048]{2,1,0:T(8,128)(2,1)}, u32[]{:S(2)}, u32[]{:S(2)}) %all-to-all-start.17) | async-done | bytes 2097184 | tf_op jit(solution)/shard_map/all_to_all | solution.py:99
  1264.5 7.1 gather_fusion.12
  1278.7 27.8 %all-to-all-done.18 = bf16[32,16,2048]{2,1,0:T(8,128)(2,1)} async-done(((bf16[32,16,2048]{2,1,0:T(8,128)(2,1)}), bf16[32,16,2048]{2,1,0:T(8,128)(2,1)}, u32[]{:S(2)}, u32[]{:S(2)}) %all-to-all-start.18) | async-done | bytes 2097184 | tf_op jit(solution)/shard_map/all_to_all | solution.py:99
  1306.5 13.1 gather_fusion.13
  1347.8 40.3 %scatter_fusion.7 = bf16[32,16,2048]{2,1,0:T(8,128)(2,1)} fusion(bf16[32,16,2048]{2,1,0:T(8,128)(2,1)} %broadcast.1924.clone.7, s32[256]{0:T(256)S(1)} %bitcast.742, bf16[256,2048]{1,0:T(8,128)(2,1)} %multiply_convert_fusion.2), kind=kCustom, calls=%fused_computation.32 | custom fusion | bytes 3147776 | tf_op jit(solution)/shard_map/scatter | solution.py:242
  1388.1 8.8 all-to-all-start.19
  1402.0 22.6 %all-to-all-done.19 = bf16[32,16,2048]{2,1,0:T(8,128)(2,1)} async-done(((bf16[32,16,2048]{2,1,0:T(8,128)(2,1)}), bf16[32,16,2048]{2,1,0:T(8,128)(2,1)}, u32[]{:S(2)}, u32[]{:S(2)}) %all-to-all-start.19) | async-done | bytes 2097184 | tf_op jit(solution)/shard_map/all_to_all | solution.py:99
  1444.7 7.1 gather_fusion.14
  1451.8 7.2 all-to-all-start.20
  1459.0 27.8 %all-to-all-done.20 = bf16[32,16,2048]{2,1,0:T(8,128)(2,1)} async-done(((bf16[32,16,2048]{2,1,0:T(8,128)(2,1)}), bf16[32,16,2048]{2,1,0:T(8,128)(2,1)}, u32[]{:S(2)}, u32[]{:S(2)}) %all-to-all-start.20) | async-done | bytes 2097184 | tf_op jit(solution)/shard_map/all_to_all | solution.py:99
  1486.8 13.1 gather_fusion.15
  1528.1 46.3 %scatter_fusion.8 = bf16[32,16,2048]{2,1,0:T(8,128)(2,1)} fusion(bf16[32,16,2048]{2,1,0:T(8,128)(2,1)} %broadcast.1924.clone.8, s32[256]{0:T(256)S(1)} %bitcast.738, bf16[256,2048]{1,0:T(8,128)(2,1)} %multiply_convert_fusion.1), kind=kCustom, calls=%fused_computation.34 | custom fusion | bytes 3147776 | tf_op jit(solution)/shard_map/scatter | solution.py:242
  1574.4 8.9 all-to-all-start.21
  1588.4 22.6 %all-to-all-done.21 = bf16[32,16,2048]{2,1,0:T(8,128)(2,1)} async-done(((bf16[32,16,2048]{2,1,0:T(8,128)(2,1)}), bf16[32,16,2048]{2,1,0:T(8,128)(2,1)}, u32[]{:S(2)}, u32[]{:S(2)}) %all-to-all-start.21) | async-done | bytes 2097184 | tf_op jit(solution)/shard_map/all_to_all | solution.py:99
  1631.0 7.1 gather_fusion.16
  1651.0 21.9 %all-to-all-done.22 = bf16[32,16,2048]{2,1,0:T(8,128)(2,1)} async-done(((bf16[32,16,2048]{2,1,0:T(8,128)(2,1)}), bf16[32,16,2048]{2,1,0:T(8,128)(2,1)}, u32[]{:S(2)}, u32[]{:S(2)}) %all-to-all-start.22) | async-done | bytes 2097184 | tf_op jit(solution)/shard_map/all_to_all | solution.py:99
  1708.2 66.2 %psum.22 = f32[]{:T(128)} all-reduce(f32[]{:T(128)} %subtract_reduce_fusion), channel_id=1, replica_groups=mesh['section'=4,'expert'=4,'dp'=8] {'section','expert','dp'}, use_global_device_ids=true, to_apply=%region_59.60 | all-reduce | flops 1 | bytes 8 | tf_op jit(solution)/shard_map/psum | solution.py:281
  1821.8 46.2 %scatter_fusion.9 = bf16[32,16,2048]{2,1,0:T(8,128)(2,1)} fusion(bf16[32,16,2048]{2,1,0:T(8,128)(2,1)} %broadcast.1924, s32[256]{0:T(256)S(1)} %bitcast.734, bf16[256,2048]{1,0:T(8,128)(2,1)} %multiply_convert_fusion), kind=kCustom, calls=%fused_computation.36 | custom fusion | bytes 3147776 | tf_op jit(solution)/shard_map/scatter | solution.py:242
  1912.8 11.6 fusion.93
  1924.4 11.6 fusion.91
  1936.0 11.5 fusion.92
  (728 shorter events, 700.9 us)
Async XLA Ops:
  7.2 114.0 %copy-start = (bf16[1,1,2048,768]{3,2,1,0:T(8,128)(2,1)S(1)}, bf16[1,1,2048,768]{3,2,1,0:T(8,128)(2,1)}, u32[]{:S(2)}) copy-start(bf16[1,1,2048,768]{3,2,1,0:T(8,128)(2,1)} %param.14) | copy-start | bytes 9437188
  8.1 136.5 %copy-start.67 = (s32[1,1,64,4]{2,3,1,0:T(4,128)}, s32[1,1,64,4]{2,3,1,0:T(4,128)S(1)}, u32[]{:S(2)}) copy-start(s32[1,1,64,4]{2,3,1,0:T(4,128)S(1)} %get-tuple-element.78) | copy-start | bytes 3076
  8.1 321.8 %copy-start.69 = (s32[1,1,64,4]{2,3,1,0:T(4,128)}, s32[1,1,64,4]{2,3,1,0:T(4,128)S(1)}, u32[]{:S(2)}) copy-start(s32[1,1,64,4]{2,3,1,0:T(4,128)S(1)} %get-tuple-element.76) | copy-start | bytes 3076
  8.1 514.4 %copy-start.71 = (s32[1,1,64,4]{2,3,1,0:T(4,128)}, s32[1,1,64,4]{2,3,1,0:T(4,128)S(1)}, u32[]{:S(2)}) copy-start(s32[1,1,64,4]{2,3,1,0:T(4,128)S(1)} %get-tuple-element.74) | copy-start | bytes 3076
  11.3 62.4 %all-to-all-start = ((bf16[32,1,1]{2,1,0:T(2,128)(2,1)}), bf16[32,1,1]{2,1,0:T(2,128)(2,1)S(1)}, u32[]{:S(2)}, u32[]{:S(2)}) async-start(bf16[32,1,1]{2,1,0:T(2,128)(2,1)} %copy.226), calls=%async_computation | async-start | bytes 32768 | tf_op jit(solution)/shard_map/all_to_all | solution.py:94
  26.0 47.8 %copy-start.1 = (s32[256,1]{0,1:T(1,128)}, s32[256,1]{0,1:T(1,128)S(1)}, u32[]{:S(2)}) copy-start(s32[256,1]{0,1:T(1,128)S(1)} %get-tuple-element.90) | copy-start | bytes 3076
  73.8 35.3 %all-to-all-start.1 = ((bf16[32,16,2048]{2,1,0:T(8,128)(2,1)}), bf16[32,16,2048]{2,1,0:T(8,128)(2,1)}, u32[]{:S(2)}, u32[]{:S(2)}) async-start(bf16[32,16,2048]{2,1,0:T(8,128)(2,1)} %scatter_fusion), calls=%async_computation.1 | async-start | bytes 4194304 | tf_op jit(solution)/shard_map/all_to_all | solution.py:93
  136.5 6.9 copy-start.35
  136.5 34.8 %all-to-all-start.2 = ((bf16[32,16,2048]{2,1,0:T(8,128)(2,1)}), bf16[32,16,2048]{2,1,0:T(8,128)(2,1)}, u32[]{:S(2)}, u32[]{:S(2)}) async-start(bf16[32,16,2048]{2,1,0:T(8,128)(2,1)} %bitcast.763), calls=%async_computation.2 | async-start | bytes 4194304 | tf_op jit(solution)/shard_map/all_to_all | solution.py:99
  171.3 85.5 %all-to-all-start.3 = ((bf16[32,1,1]{2,1,0:T(2,128)(2,1)}), bf16[32,1,1]{2,1,0:T(2,128)(2,1)S(1)}, u32[]{:S(2)}, u32[]{:S(2)}) async-start(bf16[32,1,1]{2,1,0:T(2,128)(2,1)} %copy.233), calls=%async_computation.3 | async-start | bytes 32768 | tf_op jit(solution)/shard_map/all_to_all | solution.py:94
  188.6 7.2 copy-start.42
  189.4 11.4 collective-permute-start
  195.8 14.8 copy-start.5
  195.8 165.7 %copy-start.3 = (s32[256,1]{0,1:T(1,128)}, s32[256,1]{0,1:T(1,128)S(1)}, u32[]{:S(2)}) copy-start(s32[256,1]{0,1:T(1,128)S(1)} %get-tuple-element.87) | copy-start | bytes 3076
  256.8 36.4 %all-to-all-start.4 = ((bf16[32,16,2048]{2,1,0:T(8,128)(2,1)}), bf16[32,16,2048]{2,1,0:T(8,128)(2,1)}, u32[]{:S(2)}, u32[]{:S(2)}) async-start(bf16[32,16,2048]{2,1,0:T(8,128)(2,1)} %scatter_fusion.1), calls=%async_computation.4 | async-start | bytes 4194304 | tf_op jit(solution)/shard_map/all_to_all | solution.py:93
  320.4 34.7 %all-to-all-start.5 = ((bf16[32,16,2048]{2,1,0:T(8,128)(2,1)}), bf16[32,16,2048]{2,1,0:T(8,128)(2,1)}, u32[]{:S(2)}, u32[]{:S(2)}) async-start(bf16[32,16,2048]{2,1,0:T(8,128)(2,1)} %bitcast.760), calls=%async_computation.5 | async-start | bytes 4194304 | tf_op jit(solution)/shard_map/all_to_all | solution.py:99
  328.8 79.7 %copy-start.9 = (s32[256,1]{0,1:T(1,128)}, s32[256,1]{0,1:T(1,128)S(1)}, u32[]{:S(2)}) copy-start(s32[256,1]{0,1:T(1,128)S(1)} %get-tuple-element.86) | copy-start | bytes 3076
  328.8 217.1 %copy-start.7 = (s32[256,1]{0,1:T(1,128)}, s32[256,1]{0,1:T(1,128)S(1)}, u32[]{:S(2)}) copy-start(s32[256,1]{0,1:T(1,128)S(1)} %get-tuple-element.85) | copy-start | bytes 3076
  355.1 31.7 %all-to-all-start.6 = ((bf16[32,1,1]{2,1,0:T(2,128)(2,1)}), bf16[32,1,1]{2,1,0:T(2,128)(2,1)S(1)}, u32[]{:S(2)}, u32[]{:S(2)}) async-start(bf16[32,1,1]{2,1,0:T(2,128)(2,1)} %copy.240), calls=%async_computation.6 | async-start | bytes 32768 | tf_op jit(solution)/shard_map/all_to_all | solution.py:94
  373.6 10.0 collective-permute-start.1
  386.8 15.1 all-to-all-start.9
  401.9 46.9 %all-to-all-start.12 = ((bf16[32,1,1]{2,1,0:T(2,128)(2,1)}), bf16[32,1,1]{2,1,0:T(2,128)(2,1)S(1)}, u32[]{:S(2)}, u32[]{:S(2)}) async-start(bf16[32,1,1]{2,1,0:T(2,128)(2,1)} %copy.254), calls=%async_computation.12 | async-start | bytes 32768 | tf_op jit(solution)/shard_map/all_to_all | solution.py:94
  448.8 7.9 copy-start.86
  448.8 35.3 %all-to-all-start.7 = ((bf16[32,16,2048]{2,1,0:T(8,128)(2,1)}), bf16[32,16,2048]{2,1,0:T(8,128)(2,1)}, u32[]{:S(2)}, u32[]{:S(2)}) async-start(bf16[32,16,2048]{2,1,0:T(8,128)(2,1)} %scatter_fusion.2), calls=%async_computation.7 | async-start | bytes 4194304 | tf_op jit(solution)/shard_map/all_to_all | solution.py:93
  456.9 501.8 %copy-start.73 = (s32[32]{0:T(128)}, s32[32]{0:T(128)S(1)}, u32[]{:S(2)}) copy-start(s32[32]{0:T(128)S(1)} %dynamic_slice.201) | copy-start | bytes 388
  511.2 34.7 %all-to-all-start.8 = ((bf16[32,16,2048]{2,1,0:T(8,128)(2,1)}), bf16[32,16,2048]{2,1,0:T(8,128)(2,1)}, u32[]{:S(2)}, u32[]{:S(2)}) async-start(bf16[32,16,2048]{2,1,0:T(8,128)(2,1)} %bitcast.759), calls=%async_computation.8 | async-start | bytes 4194304 | tf_op jit(solution)/shard_map/all_to_all | solution.py:99
  565.9 7.4 collective-permute-start.2
  622.1 36.0 %all-to-all-start.10 = ((bf16[32,16,2048]{2,1,0:T(8,128)(2,1)}), bf16[32,16,2048]{2,1,0:T(8,128)(2,1)}, u32[]{:S(2)}, u32[]{:S(2)}) async-start(bf16[32,16,2048]{2,1,0:T(8,128)(2,1)} %scatter_fusion.3), calls=%async_computation.10 | async-start | bytes 4194304 | tf_op jit(solution)/shard_map/all_to_all | solution.py:93
  685.1 34.9 %all-to-all-start.11 = ((bf16[32,16,2048]{2,1,0:T(8,128)(2,1)}), bf16[32,16,2048]{2,1,0:T(8,128)(2,1)}, u32[]{:S(2)}, u32[]{:S(2)}) async-start(bf16[32,16,2048]{2,1,0:T(8,128)(2,1)} %bitcast.764), calls=%async_computation.11 | async-start | bytes 4194304 | tf_op jit(solution)/shard_map/all_to_all | solution.py:99
  735.9 9.1 copy-start.26
  740.1 9.2 collective-permute-start.3
  798.1 35.2 %all-to-all-start.13 = ((bf16[32,16,2048]{2,1,0:T(8,128)(2,1)}), bf16[32,16,2048]{2,1,0:T(8,128)(2,1)}, u32[]{:S(2)}, u32[]{:S(2)}) async-start(bf16[32,16,2048]{2,1,0:T(8,128)(2,1)} %scatter_fusion.4), calls=%async_computation.13 | async-start | bytes 4194304 | tf_op jit(solution)/shard_map/all_to_all | solution.py:93
  860.6 34.7 %all-to-all-start.14 = ((bf16[32,16,2048]{2,1,0:T(8,128)(2,1)}), bf16[32,16,2048]{2,1,0:T(8,128)(2,1)}, u32[]{:S(2)}, u32[]{:S(2)}) async-start(bf16[32,16,2048]{2,1,0:T(8,128)(2,1)} %bitcast.761), calls=%async_computation.14 | async-start | bytes 4194304 | tf_op jit(solution)/shard_map/all_to_all | solution.py:99
  867.3 89.4 %all-reduce.3.cloned.1.call-start = ((), (), s32[]{:S(2)}) async-start(), calls=%async_computation.24 | async-start | bytes 1048576 | tf_op jit(solution)/shard_map/psum | solution.py:19
  873.2 7.2 copy-start.56
  958.6 11.4 copy-start.65
  958.6 15.0 copy-start.75
  1023.5 41.2 %all-to-all-start.15 = ((bf16[32,16,2048]{2,1,0:T(8,128)(2,1)}), bf16[32,16,2048]{2,1,0:T(8,128)(2,1)}, u32[]{:S(2)}, u32[]{:S(2)}) async-start(bf16[32,16,2048]{2,1,0:T(8,128)(2,1)} %scatter_fusion.5), calls=%async_computation.15 | async-start | bytes 4194304 | tf_op jit(solution)/shard_map/all_to_all | solution.py:99
  1091.6 35.0 %all-to-all-start.16 = ((bf16[32,16,2048]{2,1,0:T(8,128)(2,1)}), bf16[32,16,2048]{2,1,0:T(8,128)(2,1)}, u32[]{:S(2)}, u32[]{:S(2)}) async-start(bf16[32,16,2048]{2,1,0:T(8,128)(2,1)} %bitcast.765), calls=%async_computation.16 | async-start | bytes 4194304 | tf_op jit(solution)/shard_map/all_to_all | solution.py:99
  1146.1 10.0 copy-start.28
  1149.0 7.1 collective-permute-start.4
  1208.0 36.7 %all-to-all-start.17 = ((bf16[32,16,2048]{2,1,0:T(8,128)(2,1)}), bf16[32,16,2048]{2,1,0:T(8,128)(2,1)}, u32[]{:S(2)}, u32[]{:S(2)}) async-start(bf16[32,16,2048]{2,1,0:T(8,128)(2,1)} %scatter_fusion.6), calls=%async_computation.17 | async-start | bytes 4194304 | tf_op jit(solution)/shard_map/all_to_all | solution.py:99
  1271.6 34.9 %all-to-all-start.18 = ((bf16[32,16,2048]{2,1,0:T(8,128)(2,1)}), bf16[32,16,2048]{2,1,0:T(8,128)(2,1)}, u32[]{:S(2)}, u32[]{:S(2)}) async-start(bf16[32,16,2048]{2,1,0:T(8,128)(2,1)} %bitcast.766), calls=%async_computation.18 | async-start | bytes 4194304 | tf_op jit(solution)/shard_map/all_to_all | solution.py:99
  1326.0 10.1 copy-start.29
  1329.0 7.1 collective-permute-start.5
  1388.1 8.8 copy-start.78
  1388.1 36.5 %all-to-all-start.19 = ((bf16[32,16,2048]{2,1,0:T(8,128)(2,1)}), bf16[32,16,2048]{2,1,0:T(8,128)(2,1)}, u32[]{:S(2)}, u32[]{:S(2)}) async-start(bf16[32,16,2048]{2,1,0:T(8,128)(2,1)} %scatter_fusion.7), calls=%async_computation.19 | async-start | bytes 4194304 | tf_op jit(solution)/shard_map/all_to_all | solution.py:99
  1451.8 35.0 %copy-start.8 = (s32[256,1]{0,1:T(1,128)S(1)}, s32[256,1]{0,1:T(1,128)}, u32[]{:S(2)}) copy-start(s32[256,1]{0,1:T(1,128)} %copy-done.7) | copy-start | bytes 3076
  1451.8 35.0 %all-to-all-start.20 = ((bf16[32,16,2048]{2,1,0:T(8,128)(2,1)}), bf16[32,16,2048]{2,1,0:T(8,128)(2,1)}, u32[]{:S(2)}, u32[]{:S(2)}) async-start(bf16[32,16,2048]{2,1,0:T(8,128)(2,1)} %bitcast.767), calls=%async_computation.20 | async-start | bytes 4194304 | tf_op jit(solution)/shard_map/all_to_all | solution.py:99
  1506.4 10.1 copy-start.30
  1509.3 7.1 collective-permute-start.6
  1574.4 8.9 copy-start.77
  1574.4 36.6 %all-to-all-start.21 = ((bf16[32,16,2048]{2,1,0:T(8,128)(2,1)}), bf16[32,16,2048]{2,1,0:T(8,128)(2,1)}, u32[]{:S(2)}, u32[]{:S(2)}) async-start(bf16[32,16,2048]{2,1,0:T(8,128)(2,1)} %scatter_fusion.8), calls=%async_computation.21 | async-start | bytes 4194304 | tf_op jit(solution)/shard_map/all_to_all | solution.py:99
  1638.2 34.7 %all-to-all-start.22 = ((bf16[32,16,2048]{2,1,0:T(8,128)(2,1)}), bf16[32,16,2048]{2,1,0:T(8,128)(2,1)}, u32[]{:S(2)}, u32[]{:S(2)}) async-start(bf16[32,16,2048]{2,1,0:T(8,128)(2,1)} %bitcast.762), calls=%async_computation.22 | async-start | bytes 4194304 | tf_op jit(solution)/shard_map/all_to_all | solution.py:99
  1644.9 28.0 %copy-start.4 = (s32[256,1]{0,1:T(1,128)S(1)}, s32[256,1]{0,1:T(1,128)}, u32[]{:S(2)}) copy-start(s32[256,1]{0,1:T(1,128)} %copy-done.3) | copy-start | bytes 3076
  1644.9 302.7 %all-gather.3.cloned.1.call-start = ((), (), s32[]{:S(2)}) async-start(), calls=%async_computation.26 | async-start | bytes 4325376 | tf_op jit(solution)/shard_map/all_gather | solution.py:23
  1684.4 10.1 copy-start.31
  1687.4 12.0 copy-start.79
  1687.4 7.1 collective-permute-start.7
  1699.3 257.8 %all-reduce.5.cloned.1.call-start = ((), (), s32[]{:S(2)}) async-start(), calls=%async_computation.25 | async-start | bytes 2097152 | tf_op jit(solution)/shard_map/psum | solution.py:281
  1705.2 69.1 %copy-start.66 = (f32[32,128]{1,0:T(8,128)S(1)}, f32[32,128]{1,0:T(8,128)}, u32[]{:S(2)}) copy-start(f32[32,128]{1,0:T(8,128)} %copy-done.65) | copy-start | bytes 49156
  1705.2 69.1 %copy-start.74 = (s32[32]{0:T(128)S(1)}, s32[32]{0:T(128)}, u32[]{:S(2)}) copy-start(s32[32]{0:T(128)} %copy-done.73) | copy-start | bytes 388
  1868.1 33.8 %all-to-all-start.23 = ((bf16[32,16,2048]{2,1,0:T(8,128)(2,1)}), bf16[32,16,2048]{2,1,0:T(8,128)(2,1)}, u32[]{:S(2)}, u32[]{:S(2)}) async-start(bf16[32,16,2048]{2,1,0:T(8,128)(2,1)} %scatter_fusion.9), calls=%async_computation.23 | async-start | bytes 4194304 | tf_op jit(solution)/shard_map/all_to_all | solution.py:99
  1912.8 11.7 copy-start.23
  (84 other events, 301.8 us)
Sparse Core Ops, SparseCore 0:
  916.1 40.5 all-reduce.2
  1699.5 46.2 all-gather.2
  1776.8 155.3 all-reduce.4
where the time goes:
time: 1990 us; the launch traced here: 1970 us
  local copies, waits for them, and re-layouts  805 us (40%)
  waiting for transfers between devices  468 us (24%)
  matrix products  272 us (14%)
  starting transfers between devices  208 us (10%)
  other arithmetic  121 us (6%)
  blocking collectives  76.2 us (4%)
    scatter x10, local copies, waits for them, and re-layouts, shards(): outgoing = jnp.zeros((expert_count, slot_count, model_width), jnp.bfloat1...  427 us
    all_to_all x14, waiting for transfers between devices, route_rows(): lax.all_to_all(payload, ('expert', 'dp'), split_axis=0, concat_axis=0, ti...  298 us
    all_to_all x14, starting transfers between devices, route_rows(): lax.all_to_all(payload, ('expert', 'dp'), split_axis=0, concat_axis=0, ti...  108 us
    all_to_all x5, waiting for transfers between devices, send_tokens(): lax.all_to_all(payload, ('expert', 'dp'), split_axis=0, concat_axis=0, ti...  106 us
    dot_general x21, matrix products, contract_first(): lax.dot_general(left, right, (((0,), (0,)), ((), ())), preferred_element_...  103 us
    gather x9, local copies, waits for them, and re-layouts, shards(): returned[jnp.minimum(target, expert_count - 1), slot_of]  94.2 us
    psum x1, blocking collectives, shards(): lax.psum((head_term, loss_term), ('section', 'expert', 'dp'))  66.2 us
    gather x9, local copies, waits for them, and re-layouts, shards(): results[fetch_row].reshape(expert_count, slot_count, model_width)  63.9 us
  transfers between devices with their start and end apart: 35, of which 28 were waited for; matrix products, arithmetic and copies ran while one was open for 24% of the time, Pallas kernels for 0%

commit v1 on v0

v1 whole, which is shorter than its diff:
```python
import functools

import jax
import jax.numpy as jnp
from jax import lax
from jax.experimental import pallas as pl
from jax.experimental.pallas import tpu as pltpu
from jax.sharding import PartitionSpec as P

soft_cap = 30.0
norm_eps = 1e-06
BF = jnp.bfloat16
F32 = jnp.float32
plane = ("expert", "dp")
MIB = 1 << 20


def dot(left, right, dims):
    return lax.dot_general(left, right, (dims, ((), ())), preferred_element_type=F32)


def nn(left, right):
    return dot(left, right, ((1,), (0,)))


def nt(left, right):
    return dot(left, right, ((1,), (1,)))


def tn(left, right):
    return dot(left, right, ((0,), (0,)))


def sds(shape, dtype):
    return jax.ShapeDtypeStruct(shape, dtype)


def whole(array):
    rank = len(array.shape)
    return pl.BlockSpec(array.shape, lambda *_: (0,) * rank)


def run(kernel, args, in_specs, outs, out_specs, grid=(1,), scratch=(), aliases=None, cost=1e9):
    moved = sum(a.size * a.dtype.itemsize for a in args[1:])
    return pl.pallas_call(
        kernel,
        grid_spec=pltpu.PrefetchScalarGridSpec(
            num_scalar_prefetch=1,
            grid=grid,
            in_specs=in_specs,
            out_specs=out_specs,
            scratch_shapes=list(scratch),
        ),
        out_shape=outs,
        input_output_aliases=aliases or {},
        compiler_params=pltpu.CompilerParams(vmem_limit_bytes=40 * MIB),
        cost_estimate=pl.CostEstimate(flops=int(cost), bytes_accessed=moved, transcendentals=0),
    )(*args)


def normalize(layer_in):
    hidden_f = layer_in.astype(F32)
    inv_rms = lax.rsqrt(jnp.mean(hidden_f * hidden_f, axis=-1, keepdims=True) + norm_eps)
    return hidden_f, inv_rms, (hidden_f * inv_rms).astype(BF)


def hi_lo(values):
    high = values.astype(BF)
    return high, (values - high.astype(F32)).astype(BF)


def spreading(experts, slots):
    shape = (experts, experts * slots)
    column = lax.broadcasted_iota(jnp.int32, shape, 1)
    row = lax.broadcasted_iota(jnp.int32, shape, 0)
    return ((column // slots) == row).astype(F32).astype(BF)


def pick(flag, refs):
    if len(refs) == 1:
        return refs[0][...]
    return jnp.where(flag, refs[0][...], refs[1][...])


def place_kernel(slots, sec, ids_ref, pt_ref):
    micros, rows, width = pt_ref.shape
    column = lax.broadcasted_iota(jnp.int32, (rows, width), 1)
    expert = column // slots
    slot = (column - expert * slots).astype(F32)
    below = (
        lax.broadcasted_iota(jnp.int32, (rows, rows), 0)
        > lax.broadcasted_iota(jnp.int32, (rows, rows), 1)
    ).astype(F32).astype(BF)
    for micro in range(micros):
        ids = ids_ref[micro]
        named = jnp.zeros((rows, width), F32)
        for k in range(ids.shape[1]):
            named = named + (ids[:, k : k + 1] == expert).astype(F32)
        before = nn(below, named.astype(BF))
        here = (named > 0.5) & (before == slot)
        pt_ref[micro] = here.astype(F32).astype(BF)


def prep_fwd_kernel(both, sec, *refs):
    ins, (pt_ref, h_ref, n_ref, out_ref) = refs[:-4], refs[-4:]
    step = pl.program_id(0)
    chunk = out_ref.shape[1]

    @pl.when(step == 0)
    def _():
        layer_in = pick(sec[0] == 0, ins)
        h_ref[...] = layer_in
        n_ref[...] = normalize(layer_in)[2]

    cols = n_ref[:, pl.ds(pl.multiple_of(step * chunk, chunk), chunk)]
    out_ref[...] = tn(pt_ref[0], cols).astype(BF)


def route_fwd_kernel(slots, sec, n_ref, router_ref, pt_ref, phl_ref, p_ref, c2_ref):
    logits = nn(n_ref[...], router_ref[...])
    spread = spreading(logits.shape[1], slots)
    high, low = hi_lo(logits)
    lowest = (logits - high.astype(F32) - low.astype(F32)).astype(BF)
    wide = nn(high, spread) + nn(low, spread) + nn(lowest, spread)
    tanh = jnp.tanh(wide / soft_cap)
    weights = pt_ref[0].astype(F32) * jnp.exp(soft_cap * tanh)
    probs = weights / jnp.sum(weights, axis=-1, keepdims=True)
    high, low = hi_lo(probs)
    rows = probs.shape[0]
    phl_ref[:rows] = high
    phl_ref[rows:] = low
    p_ref[...] = probs
    c2_ref[...] = 1.0 - tanh * tanh


def expert_fwd_kernel(sec, x_ref, wg_ref, wu_ref, wd_ref, out_ref, acc_ref):
    step = pl.program_id(0)
    packed = x_ref[...]
    gate = nn(packed, wg_ref[...])
    up = nn(packed, wu_ref[...])
    hidden = (gate * jax.nn.sigmoid(gate) * up).astype(BF)
    part = nn(hidden, wd_ref[...])

    @pl.when(step == 0)
    def _():
        acc_ref[...] = part

    @pl.when((step > 0) & (step < pl.num_programs(0) - 1))
    def _():
        acc_ref[...] += part

    @pl.when(step == pl.num_programs(0) - 1)
    def _():
        out_ref[...] = (acc_ref[...] + part).astype(BF)


def combine_fwd_kernel(sec, ret_ref, h_ref, phl_ref, out_ref):
    rows = h_ref.shape[0]
    both = nn(phl_ref[...], ret_ref[...])
    out_ref[...] = (h_ref[...].astype(F32) + (both[:rows] + both[rows:])).astype(BF)


def head_kernel(sec, final_ref, head_ref, label_ref, gtop_ref, glog_ref, loss_ref):
    class_logits = soft_cap * jnp.tanh(nn(final_ref[...], head_ref[...]) / soft_cap)
    weights = jnp.exp(class_logits)
    total = jnp.sum(weights, axis=-1, keepdims=True)
    hot = (lax.broadcasted_iota(jnp.int32, weights.shape, 1) == label_ref[...]).astype(F32)
    token_loss = jnp.log(total) - jnp.sum(hot * class_logits, axis=-1, keepdims=True)
    scaled = class_logits / soft_cap
    glog = ((weights / total - hot) * (1.0 - scaled * scaled)).astype(BF)
    glog_ref[...] = glog
    gtop_ref[...] = nt(glog, head_ref[...]).astype(BF)
    loss_ref[...] = jnp.broadcast_to(jnp.sum(token_loss, axis=0, keepdims=True), loss_ref.shape)


def prep_bwd_kernel(tick, n_g, n_p, sec, *refs):
    g_refs, phl_refs, (g_ref, out_ref) = refs[:n_g], refs[n_g : n_g + n_p], refs[n_g + n_p :]
    flag = sec[0] == sec[1] - tick
    step = pl.program_id(0)
    chunk = out_ref.shape[1]

    @pl.when(step == 0)
    def _():
        g_ref[...] = pick(flag, g_refs)

    cols = g_ref[:, pl.ds(pl.multiple_of(step * chunk, chunk), chunk)]
    probs = pick(flag, phl_refs)
    out_ref[...] = tn(probs, jnp.concatenate([cols, cols], axis=0)).astype(BF)


def route_bwd_kernel(tick, slots, n, micros, sec, g_ref, *refs):
    r_refs, h_refs, p_refs, c_refs = (refs[i * n : (i + 1) * n] for i in range(4))
    router_t_ref, acc_in_ref, gn_ref, acc_ref = refs[4 * n :]
    flag = sec[0] == sec[1] - tick
    micro = tick - (sec[1] - 1 - sec[0])
    active = (micro >= 0) & (micro < micros)
    grad = g_ref[...]
    grad_prob = nt(grad, pick(flag, r_refs))
    probs = pick(flag, p_refs)
    mean = jnp.sum(probs * grad_prob, axis=-1, keepdims=True)
    grad_chosen = (probs * (grad_prob - mean) * pick(flag, c_refs)).astype(BF)
    experts = router_t_ref.shape[0]
    grad_route = nt(grad_chosen, spreading(experts, slots)).astype(BF)
    gn_ref[...] = nn(grad_route, router_t_ref[...])
    normed = normalize(pick(flag, h_refs))[2]
    acc_ref[...] = acc_in_ref[...] + jnp.where(active, tn(grad_route, normed), 0.0)


def again_kernel(tick, n, sec, *refs):
    x_refs = refs[:n]
    wg_ref, wu_ref = refs[n : n + 2]
    a1_ref, a2_ref, ht_ref, xt_ref = refs[-4:]
    packed = pick(sec[0] == sec[1] - tick, x_refs)
    gate = nn(packed, wg_ref[...])
    up = nn(packed, wu_ref[...])
    sigmoid = jax.nn.sigmoid(gate)
    silu = gate * sigmoid
    a1_ref[...] = up * sigmoid * (1.0 + gate * (1.0 - sigmoid))
    a2_ref[...] = silu
    ht_ref[0] = (silu * up).astype(BF).T

    @pl.when(pl.program_id(0) == 0)
    def _():
        xt_ref[0] = packed.T


def expert_bwd_kernel(last, sec, dy_ref, wd_ref, a1_ref, a2_ref, *refs):
    step = pl.program_id(0)
    if last:
        gg_ref, gu_ref, dys_ref = refs[-3:]
    else:
        wg_ref, wu_ref = refs[:2]
        gg_ref, gu_ref, dys_ref, out_ref, acc_ref = refs[-5:]
    rows = dy_ref[...]
    grad_hidden = nt(rows, wd_ref[...])
    gg = (grad_hidden * a1_ref[...]).astype(BF)
    gu = (grad_hidden * a2_ref[...]).astype(BF)
    gg_ref[0] = gg
    gu_ref[0] = gu

    @pl.when(step == 0)
    def _():
        dys_ref[0] = rows

    if last:
        return
    part = nt(gg, wg_ref[...]) + nt(gu, wu_ref[...])

    @pl.when(step == 0)
    def _():
        acc_ref[...] = part

    @pl.when((step > 0) & (step < pl.num_programs(0) - 1))
    def _():
        acc_ref[...] += part

    @pl.when(step == pl.num_programs(0) - 1)
    def _():
        out_ref[...] = (acc_ref[...] + part).astype(BF)


def combine_bwd_kernel(tick, n, sec, ret_ref, pt_ref, gn_ref, g_ref, *refs):
    h_refs, (out_ref, sum_ref) = refs[:n], refs[n:]
    step = pl.program_id(0)
    chunk = ret_ref.shape[1]
    cols = pl.ds(pl.multiple_of(step * chunk, chunk), chunk)
    sum_ref[:, cols] = nn(pt_ref[0], ret_ref[...])

    @pl.when(step == pl.num_programs(0) - 1)
    def _():
        hidden_f, inv_rms, _ = normalize(pick(sec[0] == sec[1] - tick, h_refs))
        grad_normed = sum_ref[...] + gn_ref[...]
        normed_f = hidden_f * inv_rms
        mean = jnp.mean(grad_normed * normed_f, axis=-1, keepdims=True)
        out_ref[...] = (
            g_ref[...].astype(F32) + inv_rms * (grad_normed - normed_f * mean)
        ).astype(BF)


def weights_kernel(sec, xt_ref, gg_ref, gu_ref, ht_ref, dy_ref, gate_ref, up_ref, down_ref):
    gate_ref[...] = (nn(xt_ref[0], gg_ref[0]) + nn(xt_ref[1], gg_ref[1])).astype(BF)
    up_ref[...] = (nn(xt_ref[0], gu_ref[0]) + nn(xt_ref[1], gu_ref[1])).astype(BF)
    down_ref[...] = (nn(ht_ref[0], dy_ref[0]) + nn(ht_ref[1], dy_ref[1])).astype(BF)


def to_owners(rows):
    return lax.all_to_all(rows, plane, split_axis=0, concat_axis=0, tiled=True)


def from_behind(block, axis, distance):
    devices = range(lax.axis_size(axis))
    route = [(i - distance, i) for i in devices if i - distance in devices]
    return lax.ppermute(block, axis, route)


def shards(tokens, expert_ids, labels, router, class_head, w_gate, w_up, w_down):
    sections = lax.axis_size("section")
    section = lax.axis_index("section")
    experts = lax.axis_size(plane)
    micros, rows, width = tokens.shape
    top = expert_ids.shape[3]
    slots = 2 * rows * top // experts
    packed = experts * slots
    router_w = router[0]
    router_t = router_w.T
    gate_w, up_w, down_w = w_gate[0, 0], w_up[0, 0], w_down[0, 0]
    ffe = gate_w.shape[1]
    ticks = micros + sections - 1
    sec = jnp.stack([section, jnp.int32(sections)]).astype(jnp.int32)
    tile = 256
    chunk = 512
    steps = ffe // tile
    col_steps = width // chunk
    row_block = pl.BlockSpec((rows, chunk), lambda i, s: (0, i))
    buf_block = pl.BlockSpec((packed, chunk), lambda i, s: (0, i))
    in_block = pl.BlockSpec((width, tile), lambda i, s: (0, i))
    down_block = pl.BlockSpec((tile, width), lambda i, s: (i, 0))
    act_block = pl.BlockSpec((packed, tile), lambda i, s: (0, i))
    row_full = sds((rows, width), BF)
    buf_full = sds((packed, width), BF)
    matmul = 2.0 * packed * width * ffe

    [places] = run(
        functools.partial(place_kernel, slots),
        (sec, expert_ids[0]),
        [whole(expert_ids[0])],
        [sds((micros, rows, packed), BF)],
        [whole(sds((micros, rows, packed), BF))],
    )

    def place_block(micro_of):
        return pl.BlockSpec(
            (1, rows, packed), lambda i, s: (jnp.clip(micro_of(s), 0, micros - 1), 0, 0)
        )

    saved = []
    finals = []
    incoming = None
    for tick in range(ticks):
        if tick == 0:
            ins = (tokens[0],)
        elif tick < micros:
            ins = (tokens[tick], incoming)
        else:
            ins = (incoming,)
        micro_spec = place_block(lambda s, tick=tick: tick - s[0])
        layer_in, normed, outgoing = run(
            functools.partial(prep_fwd_kernel, len(ins) == 2),
            (sec, *ins, places),
            [whole(row_full)] * len(ins) + [micro_spec],
            [row_full, row_full, buf_full],
            [whole(row_full), whole(row_full), buf_block],
            grid=(col_steps,),
            cost=2 * rows * packed * width,
        )
        arrived = to_owners(outgoing)
        wide = sds((rows, packed), F32)
        two = sds((2 * rows, packed), BF)
        probs_two, probs, slope = run(
            functools.partial(route_fwd_kernel, slots),
            (sec, normed, router_w, places),
            [whole(row_full), whole(router_w), micro_spec],
            [two, wide, wide],
            [whole(two), whole(wide), whole(wide)],
            cost=2 * rows * width * experts,
        )
        [results] = run(
            expert_fwd_kernel,
            (sec, arrived, gate_w, up_w, down_w),
            [whole(buf_full), in_block, in_block, down_block],
            [buf_full],
            [whole(buf_full)],
            grid=(steps,),
            scratch=[pltpu.VMEM((packed, width), F32)],
            cost=3 * matmul,
        )
        returned = to_owners(results)
        [layer_out] = run(
            combine_fwd_kernel,
            (sec, returned, layer_in, probs_two),
            [buf_block, row_block, whole(two)],
            [row_full],
            [row_block],
            grid=(col_steps,),
            cost=4 * rows * packed * width,
        )
        saved.append((arrived, returned, layer_in, probs_two, probs, slope))
        if tick + 1 < ticks:
            incoming = from_behind(layer_out, "section", 1)
        micro = tick - (sections - 1)
        if micro >= 0:
            label_col = labels[micro][:, None]
            glog_full, loss_full = sds((rows, class_head.shape[1]), BF), sds((8, 128), F32)
            finals.append(
                (
                    layer_out,
                    *run(
                        head_kernel,
                        (sec, layer_out, class_head, label_col),
                        [whole(row_full), whole(class_head), whole(label_col)],
                        [row_full, glog_full, loss_full],
                        [whole(row_full), whole(glog_full), whole(loss_full)],
                        cost=4 * rows * width * class_head.shape[1],
                    ),
                )
            )

    head_term = sum(
        dot(final, glog, ((0,), (0,))) for final, _, glog, _ in finals
    )
    loss_term = sum(loss for _, _, _, loss in finals)
    share = width // experts
    head_parts = jnp.concatenate(
        [
            head_term.reshape(experts, share, -1),
            jnp.broadcast_to(loss_term[None], (experts, *loss_term.shape)),
        ],
        axis=1,
    )
    head_parts = lax.psum_scatter(head_parts, plane, scatter_dimension=0, tiled=True)
    head_all = lax.all_gather(head_parts, ("section", *plane), axis=0, tiled=True)
    head_all = head_all[(sections - 1) * experts :]
    head_total = head_all[:, :share].reshape(width, -1)
    mean_loss = head_all[0, share, 0] / (micros * rows * experts)

    router_sum = jnp.zeros((experts, width), F32)
    store = None
    for tick in range(ticks):
        at = [
            s_num + tick - (sections - 1 - s_num)
            for s_num in reversed(range(sections))
            if 0 <= tick - (sections - 1 - s_num) < micros
        ]
        cands = [saved[t] for t in at]
        if tick == 0:
            grads = (finals[0][1],)
        elif tick < micros:
            grads = (finals[tick][1], incoming)
        else:
            grads = (incoming,)
        micro_of = lambda s, tick=tick: tick - (s[1] - 1 - s[0])
        last = tick + 1 == ticks

        def slot_block(shape, place, micro_of=micro_of):
            def index(i, s):
                micro = micro_of(s)
                return (jnp.where((micro >= 0) & (micro < micros), micro, micros), *place(i))

            return pl.BlockSpec((1, *shape), index)

        count = len(cands)
        gsel, outgoing = run(
            functools.partial(prep_bwd_kernel, tick, len(grads), count),
            (sec, *grads, *[c[3] for c in cands]),
            [whole(row_full)] * len(grads) + [whole(c[3]) for c in cands],
            [row_full, buf_full],
            [whole(row_full), buf_block],
            grid=(col_steps,),
            cost=4 * rows * packed * width,
        )
        arrived = to_owners(outgoing)
        route_args = (
            gsel,
            *[c[1] for c in cands],
            *[c[2] for c in cands],
            *[c[4] for c in cands],
            *[c[5] for c in cands],
            router_t,
            router_sum,
        )
        wide_f = sds((rows, width), F32)
        grad_normed, router_sum = run(
            functools.partial(route_bwd_kernel, tick, slots, count, micros),
            (sec, *route_args),
            [whole(a) for a in route_args],
            [wide_f, router_sum],
            [whole(wide_f), whole(router_sum)],
            cost=2 * rows * packed * width,
        )
        act = sds((packed, ffe), F32)
        stores = [
            sds((micros + 1, ffe, packed), BF),
            sds((micros + 1, width, packed), BF),
            sds((micros + 1, packed, ffe), BF),
            sds((micros + 1, packed, ffe), BF),
            sds((micros + 1, packed, width), BF),
        ]
        anywhere = pl.BlockSpec(memory_space=pl.ANY)
        old = [] if store is None else list(store[:2])
        a1, a2, hidden_t, packed_t = run(
            functools.partial(again_kernel, tick, count),
            (sec, *[c[0] for c in cands], gate_w, up_w, *old),
            [whole(buf_full)] * count + [in_block, in_block] + [anywhere] * len(old),
            [act, act, *stores[:2]],
            [
                act_block,
                act_block,
                slot_block((tile, packed), lambda i: (i, 0)),
                slot_block((width, packed), lambda i: (0, 0)),
            ],
            grid=(steps,),
            aliases={3 + count + i: 2 + i for i in range(len(old))},
            cost=2 * matmul,
        )
        old = [] if store is None else list(store[2:])
        args = [arrived, down_w, a1, a2] + ([] if last else [gate_w, up_w])
        specs = [whole(buf_full), down_block, act_block, act_block]
        specs += [] if last else [in_block, in_block]
        outs = stores[2:] + ([] if last else [buf_full])
        out_specs = [
            slot_block((packed, tile), lambda i: (0, i)),
            slot_block((packed, tile), lambda i: (0, i)),
            slot_block((packed, width), lambda i: (0, 0)),
        ] + ([] if last else [whole(buf_full)])
        got = run(
            functools.partial(expert_bwd_kernel, last),
            (sec, *args, *old),
            specs + [anywhere] * len(old),
            outs,
            out_specs,
            grid=(steps,),
            scratch=[] if last else [pltpu.VMEM((packed, width), F32)],
            aliases={1 + len(args) + i: i for i in range(len(old))},
            cost=matmul if last else 3 * matmul,
        )
        store = (hidden_t, packed_t, *got[:3])
        if last:
            break
        returned = to_owners(got[3])
        [grad_in] = run(
            functools.partial(combine_bwd_kernel, tick, count),
            (sec, returned, places, grad_normed, gsel, *[c[2] for c in cands]),
            [buf_block, place_block(micro_of), whole(wide_f), whole(row_full)]
            + [whole(row_full)] * count,
            [row_full],
            [whole(row_full)],
            grid=(col_steps,),
            scratch=[pltpu.VMEM((rows, width), F32)],
            cost=2 * rows * packed * width,
        )
        incoming = from_behind(grad_in, "section", -1)

    router_parts = lax.all_gather(router_sum.astype(BF), plane, axis=0, tiled=False)
    router_out = jnp.sum(router_parts.astype(F32), axis=0).T[None]

    hidden_t, packed_t, gate_rows, up_rows, out_rows = store
    act_pair = pl.BlockSpec((micros, packed, ffe), lambda i, s: (0, 0, 0))
    grad_gate, grad_up, grad_down = run(
        weights_kernel,
        (sec, packed_t, gate_rows, up_rows, hidden_t, out_rows),
        [
            pl.BlockSpec((micros, chunk, packed), lambda i, s: (0, i, 0)),
            act_pair,
            act_pair,
            pl.BlockSpec((micros, ffe, packed), lambda i, s: (0, 0, 0)),
            pl.BlockSpec((micros, packed, chunk), lambda i, s: (0, 0, i)),
        ],
        [sds((width, ffe), BF), sds((width, ffe), BF), sds((ffe, width), BF)],
        [
            pl.BlockSpec((chunk, ffe), lambda i, s: (i, 0)),
            pl.BlockSpec((chunk, ffe), lambda i, s: (i, 0)),
            pl.BlockSpec((ffe, chunk), lambda i, s: (0, i)),
        ],
        grid=(col_steps,),
        cost=6 * matmul,
    )
    return (
        mean_loss,
        head_total,
        router_out,
        grad_gate[None, None],
        grad_up[None, None],
        grad_down[None, None],
    )


def solution(mesh):
    experts = P("section", plane, None, None)
    return jax.shard_map(
        shards,
        mesh=mesh,
        in_specs=(
            P(None, plane, None),
            P("section", None, plane, None),
            P(None, plane),
            P("section", None, None),
            P(),
            experts,
            experts,
            experts,
        ),
        out_specs=(P(), P(), P("section", None, None), experts, experts, experts),
        check_vma=False,
    )
```

time: 1990 us -> 1010 us (0.51)
  local copies, waits for them, and re-layouts: 805 us -> 169 us
  matrix products: 272 us -> 0.67 us
  Pallas kernels: 0 us -> 237 us
  waiting for transfers between devices: 468 us -> 303 us
  other arithmetic: 121 us -> 5.59 us
  starting transfers between devices: 208 us -> 119 us
  blocking collectives: 76.2 us -> 147 us
    scatter x20 -> x0, local copies, waits for them, and re-layouts: 490 us -> none  [the longest x10 427 us: shards(): outgoing = jnp.zeros((expert_count, slot_count, model_width), jnp.bfloat1...]
    dot_general x70 -> x2, matrix products: 272 us -> 0.67 us  [dot(): lax.dot_general(left, right, (dims, ((), ())), preferred_element_type=F32)]
    pallas_call x0 -> x48, Pallas kernels: none -> 237 us  [run(): pl.pallas_call(kernel, grid_spec=pltpu.PrefetchScalarGridSpec(num_scalar_...]
    all_to_all x24 -> x15, waiting for transfers between devices: 406 us -> 222 us  [to_owners(): return lax.all_to_all(rows, plane, split_axis=0, concat_axis=0, tiled=True)]
    gather x18 -> x0, local copies, waits for them, and re-layouts: 158 us -> none  [the longest x9 94.2 us: shards(): returned[jnp.minimum(target, expert_count - 1), slot_of]]
    all_to_all x0 -> x4, blocking collectives: none -> 147 us  [to_owners(): return lax.all_to_all(rows, plane, split_axis=0, concat_axis=0, tiled=True)]
    unnamed x228 -> x399, local copies, waits for them, and re-layouts: 25.6 us -> 161 us
    all_to_all x24 -> x15, starting transfers between devices: 181 us -> 97.7 us  [to_owners(): return lax.all_to_all(rows, plane, split_axis=0, concat_axis=0, tiled=True)]
  transfers between devices with their start and end apart: 35 -> 26, of which waited for: 28 -> 21; matrix products, arithmetic and copies ran while one was open for 24% -> 1% of each run, Pallas kernels for 0% -> 16%
where the time goes in v1:
time: 1010 us; the launch traced here: 998 us
  waiting for transfers between devices  303 us (30%)
  Pallas kernels  237 us (23%)
  local copies, waits for them, and re-layouts  169 us (17%)
  blocking collectives  147 us (15%)
  starting transfers between devices  119 us (12%)
  between operations  17.4 us (2%)
    pallas_call x48, Pallas kernels, run(): pl.pallas_call(kernel, grid_spec=pltpu.PrefetchScalarGridSpec(num_scalar_...  237 us
    all_to_all x15, waiting for transfers between devices, to_owners(): return lax.all_to_all(rows, plane, split_axis=0, concat_axis=0, tiled=True)  222 us
    unnamed x399, local copies, waits for them, and re-layouts  161 us
    all_to_all x4, blocking collectives, to_owners(): return lax.all_to_all(rows, plane, split_axis=0, concat_axis=0, tiled=True)  147 us
    all_to_all x15, starting transfers between devices, to_owners(): return lax.all_to_all(rows, plane, split_axis=0, concat_axis=0, tiled=True)  97.7 us
    unnamed x4, waiting for transfers between devices  44.9 us
    ppermute x8, waiting for transfers between devices, from_behind(): return lax.ppermute(block, axis, route)  36.3 us
    ppermute x8, starting transfers between devices, from_behind(): return lax.ppermute(block, axis, route)  21.1 us
  transfers between devices with their start and end apart: 26, of which 21 were waited for; matrix products, arithmetic and copies ran while one was open for 1% of the time, Pallas kernels for 16%

profile of v1, /device:TPU:1, one launch (start us, length us, event | category | flops | bytes accessed | tf_op | source)
XLA Modules:
  0.0 998.5 jit_solution(6677893847616258412)
XLA Ops:
  13.0 37.1 %all_to_all.209 = bf16[32,16,2048]{2,1,0:T(8,128)(2,1)S(1)} all-to-all(bf16[32,16,2048]{2,1,0:T(8,128)(2,1)S(1)} %bitcast.146), channel_id=1, replica_groups=mesh['section'=4,'expert'=4,'dp'=8] {'expert','dp'}, dimensions={0} | all-to-all | bytes 4194304 | tf_op jit(solution)/shard_map/all_to_all | solution.py:287
  50.1 7.4 shard_map.129
  58.9 4.9 all-to-all-start.1
  69.1 22.6 %all-to-all-done.1 = bf16[32,16,2048]{2,1,0:T(8,128)(2,1)} async-done(((bf16[32,16,2048]{2,1,0:T(8,128)(2,1)}), bf16[32,16,2048]{2,1,0:T(8,128)(2,1)}, u32[]{:S(2)}, u32[]{:S(2)}) %all-to-all-start.1) | async-done | bytes 2097184 | tf_op jit(solution)/shard_map/all_to_all | solution.py:287
  92.7 3.7 shard_map.131
  107.1 36.5 %all_to_all.210 = bf16[32,16,2048]{2,1,0:T(8,128)(2,1)S(1)} all-to-all(bf16[32,16,2048]{2,1,0:T(8,128)(2,1)S(1)} %bitcast.145), channel_id=1, replica_groups=mesh['section'=4,'expert'=4,'dp'=8] {'expert','dp'}, dimensions={0} | all-to-all | bytes 4194304 | tf_op jit(solution)/shard_map/all_to_all | solution.py:287
  143.6 7.4 shard_map.133
  152.4 4.7 all-to-all-start.3
  162.1 23.0 %all-to-all-done.3 = bf16[32,16,2048]{2,1,0:T(8,128)(2,1)} async-done(((bf16[32,16,2048]{2,1,0:T(8,128)(2,1)}), bf16[32,16,2048]{2,1,0:T(8,128)(2,1)}, u32[]{:S(2)}, u32[]{:S(2)}) %all-to-all-start.3) | async-done | bytes 2097184 | tf_op jit(solution)/shard_map/all_to_all | solution.py:287
  186.0 3.7 shard_map.135
  189.7 4.1 collective-permute-start.1
  200.0 36.7 %all_to_all.211 = bf16[32,16,2048]{2,1,0:T(8,128)(2,1)S(1)} all-to-all(bf16[32,16,2048]{2,1,0:T(8,128)(2,1)S(1)} %bitcast.147), channel_id=1, replica_groups=mesh['section'=4,'expert'=4,'dp'=8] {'expert','dp'}, dimensions={0} | all-to-all | bytes 4194304 | tf_op jit(solution)/shard_map/all_to_all | solution.py:287
  236.8 7.4 shard_map.137
  245.5 4.7 all-to-all-start.5
  255.3 23.0 %all-to-all-done.5 = bf16[32,16,2048]{2,1,0:T(8,128)(2,1)} async-done(((bf16[32,16,2048]{2,1,0:T(8,128)(2,1)}), bf16[32,16,2048]{2,1,0:T(8,128)(2,1)}, u32[]{:S(2)}, u32[]{:S(2)}) %all-to-all-start.5) | async-done | bytes 2097184 | tf_op jit(solution)/shard_map/all_to_all | solution.py:287
  279.2 3.7 shard_map.139
  282.9 4.1 collective-permute-start.2
  293.8 36.5 %all_to_all.212 = bf16[32,16,2048]{2,1,0:T(8,128)(2,1)S(1)} all-to-all(bf16[32,16,2048]{2,1,0:T(8,128)(2,1)S(1)} %bitcast.148), channel_id=1, replica_groups=mesh['section'=4,'expert'=4,'dp'=8] {'expert','dp'}, dimensions={0} | all-to-all | bytes 4194304 | tf_op jit(solution)/shard_map/all_to_all | solution.py:287
  330.4 7.4 shard_map.141
  339.1 4.9 all-to-all-start.7
  349.7 22.2 %all-to-all-done.7 = bf16[32,16,2048]{2,1,0:T(8,128)(2,1)} async-done(((bf16[32,16,2048]{2,1,0:T(8,128)(2,1)}), bf16[32,16,2048]{2,1,0:T(8,128)(2,1)}, u32[]{:S(2)}, u32[]{:S(2)}) %all-to-all-start.7) | async-done | bytes 2097184 | tf_op jit(solution)/shard_map/all_to_all | solution.py:287
  383.7 6.7 all-to-all-start.10
  390.4 4.1 collective-permute-start.3
  394.6 5.5 collective-permute-done.3.refs_0_
  405.0 13.4 %all-to-all-done.10 = bf16[32,16,2048]{2,1,0:T(8,128)(2,1)} async-done(((bf16[32,16,2048]{2,1,0:T(8,128)(2,1)}), bf16[32,16,2048]{2,1,0:T(8,128)(2,1)}, u32[]{:S(2)}, u32[]{:S(2)}) %all-to-all-start.10) | async-done | bytes 2097184 | tf_op jit(solution)/shard_map/all_to_all | solution.py:287
  418.4 7.3 all-to-all-start.8
  429.3 7.2 shard_map.151
  437.9 15.4 %shard_map.152 = (bf16[3,512,768]{2,1,0:T(8,128)(2,1)S(1)}, bf16[3,512,768]{2,1,0:T(8,128)(2,1)S(1)}, bf16[3,512,2048]{2,1,0:T(8,128)(2,1)}, bf16[512,2048]{1,0:T(8,128)(2,1)S(1)}) custom-call(s32[2]{0:T(128)S(1)} %pad_add_fusion.sec, bf16[512,2048]{1,0:T(8,128)(2,1)} %bitcast.34.dy_ref, bf16[768,2048]{1,0:T(8,128)(2,1)} %bitcast.100, ...), custom_call_target="tpu_custom_call" | custom-call | flops 4831838208 | bytes 14680064 | tf_op jit(solution)/shard_map/pallas_call | solution.py:45
  457.4 7.8 all-to-all-start.11
  469.0 8.9 shard_map.146
  479.2 13.9 %all-to-all-done.11 = bf16[32,16,2048]{2,1,0:T(8,128)(2,1)} async-done(((bf16[32,16,2048]{2,1,0:T(8,128)(2,1)}), bf16[32,16,2048]{2,1,0:T(8,128)(2,1)}, u32[]{:S(2)}, u32[]{:S(2)}) %all-to-all-start.11) | async-done | bytes 2097184 | tf_op jit(solution)/shard_map/all_to_all | solution.py:287
  493.1 6.7 all-to-all-start.9
  507.8 4.3 shard_map.154
  519.2 8.7 all-to-all-done.9
  540.6 7.1 all-to-all-start.12
  551.0 8.9 shard_map.156
  563.7 11.9 %all-to-all-done.12 = bf16[32,16,2048]{2,1,0:T(8,128)(2,1)} async-done(((bf16[32,16,2048]{2,1,0:T(8,128)(2,1)}), bf16[32,16,2048]{2,1,0:T(8,128)(2,1)}, u32[]{:S(2)}, u32[]{:S(2)}) %all-to-all-start.12) | async-done | bytes 2097184 | tf_op jit(solution)/shard_map/all_to_all | solution.py:287
  581.7 15.4 %shard_map.157 = (bf16[3,512,768]{2,1,0:T(8,128)(2,1)S(1)}, bf16[3,512,768]{2,1,0:T(8,128)(2,1)S(1)}, bf16[3,512,2048]{2,1,0:T(8,128)(2,1)}, bf16[512,2048]{1,0:T(8,128)(2,1)S(1)}) custom-call(s32[2]{0:T(128)S(1)} %pad_add_fusion.sec, bf16[512,2048]{1,0:T(8,128)(2,1)} %bitcast.39.dy_ref, ...), custom_call_target="tpu_custom_call", output_to_operand_aliasing={{0}: (7, {}), {1}: (8, {}), {2}: (9, {})} | custom-call | flops 4831838208 | bytes 25690112 | tf_op jit(solution)/shard_map/pallas_call | solution.py:45
  601.2 6.2 all-to-all-start.13
  612.4 4.0 shard_map.158
  617.9 17.4 %all-to-all-done.13 = bf16[32,16,2048]{2,1,0:T(8,128)(2,1)S(1)} async-done(((bf16[32,16,2048]{2,1,0:T(8,128)(2,1)}), bf16[32,16,2048]{2,1,0:T(8,128)(2,1)S(1)}, u32[]{:S(2)}, u32[]{:S(2)}) %all-to-all-start.13) | async-done | bytes 2097184 | tf_op jit(solution)/shard_map/all_to_all | solution.py:287
  639.6 7.0 collective-permute-done.5.refs_0_
  651.6 7.6 all-to-all-start.14
  659.5 44.8 %reduce-scatter.4.cloned.1.call-done = f32[1,72,128]{2,1,0:T(8,128)} async-done(((f32[32,72,128]{2,1,0:T(8,128)}), f32[1,72,128]{2,1,0:T(8,128)}) %reduce-scatter.4.cloned.1.call-update) | async-done | bytes 36880
  709.2 8.2 shard_map.161
  727.3 15.4 %shard_map.162 = (bf16[3,512,768]{2,1,0:T(8,128)(2,1)S(1)}, bf16[3,512,768]{2,1,0:T(8,128)(2,1)S(1)}, bf16[3,512,2048]{2,1,0:T(8,128)(2,1)}, bf16[512,2048]{1,0:T(8,128)(2,1)S(1)}) custom-call(s32[2]{0:T(128)S(1)} %pad_add_fusion.sec, bf16[512,2048]{1,0:T(8,128)(2,1)} %bitcast.44.dy_ref, ...), custom_call_target="tpu_custom_call", output_to_operand_aliasing={{0}: (7, {}), {1}: (8, {}), {2}: (9, {})} | custom-call | flops 4831838208 | bytes 25690112 | tf_op jit(solution)/shard_map/pallas_call | solution.py:45
  746.9 7.4 all-to-all-start.15
  758.0 4.0 shard_map.163
  763.5 25.7 %all-to-all-done.15 = bf16[32,16,2048]{2,1,0:T(8,128)(2,1)S(1)} async-done(((bf16[32,16,2048]{2,1,0:T(8,128)(2,1)}), bf16[32,16,2048]{2,1,0:T(8,128)(2,1)S(1)}, u32[]{:S(2)}, u32[]{:S(2)}) %all-to-all-start.15) | async-done | bytes 2097184 | tf_op jit(solution)/shard_map/all_to_all | solution.py:287
  793.4 8.1 collective-permute-done.6.refs_0_
  807.4 6.3 all-to-all-start.16
  818.6 8.2 shard_map.166
  830.4 11.1 %all-to-all-done.16 = bf16[32,16,2048]{2,1,0:T(8,128)(2,1)} async-done(((bf16[32,16,2048]{2,1,0:T(8,128)(2,1)}), bf16[32,16,2048]{2,1,0:T(8,128)(2,1)}, u32[]{:S(2)}, u32[]{:S(2)}) %all-to-all-start.16) | async-done | bytes 2097184 | tf_op jit(solution)/shard_map/all_to_all | solution.py:287
  847.7 15.3 %shard_map.167 = (bf16[3,512,768]{2,1,0:T(8,128)(2,1)S(1)}, bf16[3,512,768]{2,1,0:T(8,128)(2,1)S(1)}, bf16[3,512,2048]{2,1,0:T(8,128)(2,1)}, bf16[512,2048]{1,0:T(8,128)(2,1)S(1)}) custom-call(s32[2]{0:T(128)S(1)} %pad_add_fusion.sec, bf16[512,2048]{1,0:T(8,128)(2,1)} %bitcast.48.dy_ref, ...), custom_call_target="tpu_custom_call", output_to_operand_aliasing={{0}: (7, {}), {1}: (8, {}), {2}: (9, {})} | custom-call | flops 4831838208 | bytes 25690112 | tf_op jit(solution)/shard_map/pallas_call | solution.py:45
  867.1 6.2 all-to-all-start.17
  875.3 4.0 shard_map.168
  880.8 20.5 %all-to-all-done.17 = bf16[32,16,2048]{2,1,0:T(8,128)(2,1)S(1)} async-done(((bf16[32,16,2048]{2,1,0:T(8,128)(2,1)}), bf16[32,16,2048]{2,1,0:T(8,128)(2,1)S(1)}, u32[]{:S(2)}, u32[]{:S(2)}) %all-to-all-start.17) | async-done | bytes 2097184 | tf_op jit(solution)/shard_map/all_to_all | solution.py:287
  905.5 5.8 collective-permute-done.7.refs_0_
  915.7 4.1 shard_map.171
  920.5 9.1 all-to-all-start.18
  934.8 7.3 shard_map.172
  950.1 8.4 all-to-all-done.18
  966.6 6.6 shard_map.173
  973.2 13.4 %shard_map.174 = (bf16[2048,768]{1,0:T(8,128)(2,1)}, bf16[2048,768]{1,0:T(8,128)(2,1)}, bf16[768,2048]{1,0:T(8,128)(2,1)}) custom-call(s32[2]{0:T(128)S(1)} %pad_add_fusion.sec, bf16[3,2048,512]{2,1,0:T(8,128)(2,1)S(1)} %bitcast.99, bf16[3,512,768]{2,1,0:T(8,128)(2,1)S(1)} %get-tuple-element.193.gg_ref, bf16[3,512,768]{2,1,0:T(8,128)(2,1)S(1)} %get-tuple-element.194.gu_ref, ...), custom_call_target="tpu_custom_call" | custom-call | flops 9663676416 | bytes 19660800 | tf_op jit(solution)/shard_map/pallas_call | solution.py:45
  (459 shorter events, 239.9 us)
Async XLA Ops:
  8.0 42.1 %copy-start.12 = (bf16[1,1,768,2048]{3,2,1,0:T(8,128)(2,1)S(1)}, bf16[1,1,768,2048]{3,2,1,0:T(8,128)(2,1)}, u32[]{:S(2)}) copy-start(bf16[1,1,768,2048]{3,2,1,0:T(8,128)(2,1)} %param.15) | copy-start | bytes 9437188
  10.0 40.1 %copy-start.5 = (bf16[1,1,2048,768]{3,2,1,0:T(8,128)(2,1)S(1)}, bf16[1,1,2048,768]{3,2,1,0:T(8,128)(2,1)}, u32[]{:S(2)}) copy-start(bf16[1,1,2048,768]{3,2,1,0:T(8,128)(2,1)} %param.14) | copy-start | bytes 9437188
  13.0 37.1 %copy-start.72 = (bf16[64,2048]{1,0:T(8,128)(2,1)}, bf16[64,2048]{1,0:T(8,128)(2,1)S(1)}, u32[]{:S(2)}) copy-start(bf16[64,2048]{1,0:T(8,128)(2,1)S(1)} %get-tuple-element.104.h_ref.refs_3_.refs_1_) | copy-start | bytes 786436
  13.0 37.1 %copy-start.158 = (bf16[64,2048]{1,0:T(8,128)(2,1)}, bf16[64,2048]{1,0:T(8,128)(2,1)S(1)}, u32[]{:S(2)}) copy-start(bf16[64,2048]{1,0:T(8,128)(2,1)S(1)} %get-tuple-element.105.n_ref) | copy-start | bytes 786436
  13.0 37.1 %copy-start = (bf16[1,1,2048,768]{3,2,1,0:T(8,128)(2,1)S(1)}, bf16[1,1,2048,768]{3,2,1,0:T(8,128)(2,1)}, u32[]{:S(2)}) copy-start(bf16[1,1,2048,768]{3,2,1,0:T(8,128)(2,1)} %param.13) | copy-start | bytes 9437188
  50.1 7.5 copy-start.55
  58.9 32.9 %all-to-all-start.1 = ((bf16[32,16,2048]{2,1,0:T(8,128)(2,1)}), bf16[32,16,2048]{2,1,0:T(8,128)(2,1)}, u32[]{:S(2)}, u32[]{:S(2)}) async-start(bf16[32,16,2048]{2,1,0:T(8,128)(2,1)} %bitcast.142), calls=%async_computation.1 | async-start | bytes 4194304 | tf_op jit(solution)/shard_map/all_to_all | solution.py:287
  69.1 34.1 %copy-start.174 = (bf16[128,512]{1,0:T(8,128)(2,1)}, bf16[128,512]{1,0:T(8,128)(2,1)S(1)}, u32[]{:S(2)}) copy-start(bf16[128,512]{1,0:T(8,128)(2,1)S(1)} %get-tuple-element.106.phl_ref.refs_2_) | copy-start | bytes 393220
  92.7 50.9 %copy-start.13 = (bf16[1,1,768,2048]{3,2,1,0:T(8,128)(2,1)S(1)}, bf16[1,1,768,2048]{3,2,1,0:T(8,128)(2,1)}, u32[]{:S(2)}) copy-start(bf16[1,1,768,2048]{3,2,1,0:T(8,128)(2,1)} %param.15) | copy-start | bytes 9437188
  96.4 6.9 collective-permute-start
  107.1 78.0 %copy-start.69 = (bf16[64,2048]{1,0:T(8,128)(2,1)}, bf16[64,2048]{1,0:T(8,128)(2,1)S(1)}, u32[]{:S(2)}) copy-start(bf16[64,2048]{1,0:T(8,128)(2,1)S(1)} %get-tuple-element.108.h_ref.refs_3_.refs_1_) | copy-start | bytes 786436
  107.1 36.5 %copy-start.6 = (bf16[1,1,2048,768]{3,2,1,0:T(8,128)(2,1)S(1)}, bf16[1,1,2048,768]{3,2,1,0:T(8,128)(2,1)}, u32[]{:S(2)}) copy-start(bf16[1,1,2048,768]{3,2,1,0:T(8,128)(2,1)} %param.14) | copy-start | bytes 9437188
  143.6 7.4 copy-start.49
  152.4 32.7 %all-to-all-start.3 = ((bf16[32,16,2048]{2,1,0:T(8,128)(2,1)}), bf16[32,16,2048]{2,1,0:T(8,128)(2,1)}, u32[]{:S(2)}, u32[]{:S(2)}) async-start(bf16[32,16,2048]{2,1,0:T(8,128)(2,1)} %bitcast.143), calls=%async_computation.3 | async-start | bytes 4194304 | tf_op jit(solution)/shard_map/all_to_all | solution.py:287
  186.0 50.7 %copy-start.14 = (bf16[1,1,768,2048]{3,2,1,0:T(8,128)(2,1)S(1)}, bf16[1,1,768,2048]{3,2,1,0:T(8,128)(2,1)}, u32[]{:S(2)}) copy-start(bf16[1,1,768,2048]{3,2,1,0:T(8,128)(2,1)} %param.15) | copy-start | bytes 9437188
  189.7 7.4 collective-permute-start.1
  200.0 36.8 %copy-start.7 = (bf16[1,1,2048,768]{3,2,1,0:T(8,128)(2,1)S(1)}, bf16[1,1,2048,768]{3,2,1,0:T(8,128)(2,1)}, u32[]{:S(2)}) copy-start(bf16[1,1,2048,768]{3,2,1,0:T(8,128)(2,1)} %param.14) | copy-start | bytes 9437188
  236.7 7.4 copy-start.52
  245.5 32.7 %all-to-all-start.5 = ((bf16[32,16,2048]{2,1,0:T(8,128)(2,1)}), bf16[32,16,2048]{2,1,0:T(8,128)(2,1)}, u32[]{:S(2)}, u32[]{:S(2)}) async-start(bf16[32,16,2048]{2,1,0:T(8,128)(2,1)} %bitcast.144), calls=%async_computation.5 | async-start | bytes 4194304 | tf_op jit(solution)/shard_map/all_to_all | solution.py:287
  279.2 51.2 %copy-start.15 = (bf16[1,1,768,2048]{3,2,1,0:T(8,128)(2,1)S(1)}, bf16[1,1,768,2048]{3,2,1,0:T(8,128)(2,1)}, u32[]{:S(2)}) copy-start(bf16[1,1,768,2048]{3,2,1,0:T(8,128)(2,1)} %param.15) | copy-start | bytes 9437188
  282.9 7.4 collective-permute-start.2
  293.8 36.5 %copy-start.8 = (bf16[1,1,2048,768]{3,2,1,0:T(8,128)(2,1)S(1)}, bf16[1,1,2048,768]{3,2,1,0:T(8,128)(2,1)}, u32[]{:S(2)}) copy-start(bf16[1,1,2048,768]{3,2,1,0:T(8,128)(2,1)} %param.14) | copy-start | bytes 9437188
  330.3 7.4 copy-start.57
  339.1 32.9 %all-to-all-start.7 = ((bf16[32,16,2048]{2,1,0:T(8,128)(2,1)}), bf16[32,16,2048]{2,1,0:T(8,128)(2,1)}, u32[]{:S(2)}, u32[]{:S(2)}) async-start(bf16[32,16,2048]{2,1,0:T(8,128)(2,1)} %bitcast.141), calls=%async_computation.7 | async-start | bytes 4194304 | tf_op jit(solution)/shard_map/all_to_all | solution.py:287
  383.7 34.7 %all-to-all-start.10 = ((bf16[32,16,2048]{2,1,0:T(8,128)(2,1)}), bf16[32,16,2048]{2,1,0:T(8,128)(2,1)}, u32[]{:S(2)}, u32[]{:S(2)}) async-start(bf16[32,16,2048]{2,1,0:T(8,128)(2,1)} %bitcast.137), calls=%async_computation.10 | async-start | bytes 4194304 | tf_op jit(solution)/shard_map/all_to_all | solution.py:287
  390.4 9.7 collective-permute-start.3
  418.4 39.0 %all-to-all-start.8 = ((bf16[32,16,2048]{2,1,0:T(8,128)(2,1)}), bf16[32,16,2048]{2,1,0:T(8,128)(2,1)}, u32[]{:S(2)}, u32[]{:S(2)}) async-start(bf16[32,16,2048]{2,1,0:T(8,128)(2,1)} %bitcast.135), calls=%async_computation.8 | async-start | bytes 4194304 | tf_op jit(solution)/shard_map/all_to_all | solution.py:287
  457.4 7.8 copy-start.1
  457.4 35.7 %all-to-all-start.11 = ((bf16[32,16,2048]{2,1,0:T(8,128)(2,1)}), bf16[32,16,2048]{2,1,0:T(8,128)(2,1)}, u32[]{:S(2)}, u32[]{:S(2)}) async-start(bf16[32,16,2048]{2,1,0:T(8,128)(2,1)} %bitcast.140), calls=%async_computation.11 | async-start | bytes 4194304 | tf_op jit(solution)/shard_map/all_to_all | solution.py:287
  493.1 34.7 %all-to-all-start.9 = ((bf16[32,16,2048]{2,1,0:T(8,128)(2,1)}), bf16[32,16,2048]{2,1,0:T(8,128)(2,1)}, u32[]{:S(2)}, u32[]{:S(2)}) async-start(bf16[32,16,2048]{2,1,0:T(8,128)(2,1)} %bitcast.132), calls=%async_computation.9 | async-start | bytes 4194304 | tf_op jit(solution)/shard_map/all_to_all | solution.py:287
  512.2 23.4 %collective-permute-start.4 = (bf16[64,2048]{1,0:T(8,128)(2,1)}, bf16[64,2048]{1,0:T(8,128)(2,1)}, u32[]{:S(2)}, u32[]{:S(2)}) collective-permute-start(bf16[64,2048]{1,0:T(8,128)(2,1)} %shard_map.154), channel_id=1, source_target_pairs={{32,0},{64,32},{96,64},{33,1},{65,33},{97,65},{34,2},{66,34},{98,6... | collective-permute-start | bytes 786440 | tf_op jit(solution)/shard_map/ppermute | solution.py:293
  540.6 34.9 %all-to-all-start.12 = ((bf16[32,16,2048]{2,1,0:T(8,128)(2,1)}), bf16[32,16,2048]{2,1,0:T(8,128)(2,1)}, u32[]{:S(2)}, u32[]{:S(2)}) async-start(bf16[32,16,2048]{2,1,0:T(8,128)(2,1)} %bitcast.139), calls=%async_computation.12 | async-start | bytes 4194304 | tf_op jit(solution)/shard_map/all_to_all | solution.py:287
  601.2 6.6 copy-start.79
  601.2 6.6 copy-start.193
  601.2 34.1 %all-to-all-start.13 = ((bf16[32,16,2048]{2,1,0:T(8,128)(2,1)}), bf16[32,16,2048]{2,1,0:T(8,128)(2,1)S(1)}, u32[]{:S(2)}, u32[]{:S(2)}) async-start(bf16[32,16,2048]{2,1,0:T(8,128)(2,1)} %bitcast.130), calls=%async_computation.13 | async-start | bytes 4194304 | tf_op jit(solution)/shard_map/all_to_all | solution.py:287
  607.4 96.9 %reduce-scatter.4.cloned.1.call-start = ((), (), s32[]{:S(2)}) async-start(), calls=%async_computation.22 | async-start | bytes 1216512
  612.4 34.2 %copy-start.172 = (bf16[128,512]{1,0:T(8,128)(2,1)S(1)}, bf16[128,512]{1,0:T(8,128)(2,1)}, u32[]{:S(2)}) copy-start(bf16[128,512]{1,0:T(8,128)(2,1)} %copy-done.170) | copy-start | bytes 393220
  638.3 8.3 collective-permute-start.5
  651.6 52.7 %copy-start.2 = (bf16[1,1,2048,768]{3,2,1,0:T(8,128)(2,1)S(1)}, bf16[1,1,2048,768]{3,2,1,0:T(8,128)(2,1)}, u32[]{:S(2)}) copy-start(bf16[1,1,2048,768]{3,2,1,0:T(8,128)(2,1)} %param.13) | copy-start | bytes 9437188
  651.6 69.6 %all-to-all-start.14 = ((bf16[32,16,2048]{2,1,0:T(8,128)(2,1)}), bf16[32,16,2048]{2,1,0:T(8,128)(2,1)}, u32[]{:S(2)}, u32[]{:S(2)}) async-start(bf16[32,16,2048]{2,1,0:T(8,128)(2,1)} %bitcast.133), calls=%async_computation.14 | async-start | bytes 4194304 | tf_op jit(solution)/shard_map/all_to_all | solution.py:287
  659.2 286.5 %all-gather.4.cloned.1.call-start = ((), (), s32[]{:S(2)}) async-start(), calls=%async_computation.20 | async-start | bytes 4755456 | tf_op jit(solution)/shard_map/all_gather | solution.py:421
  746.9 7.4 copy-start.63
  746.9 7.4 copy-start.67
  746.9 7.4 copy-start.70
  746.9 7.4 copy-start.118
  746.9 7.4 copy-start.125
  746.9 42.3 %all-to-all-start.15 = ((bf16[32,16,2048]{2,1,0:T(8,128)(2,1)}), bf16[32,16,2048]{2,1,0:T(8,128)(2,1)S(1)}, u32[]{:S(2)}, u32[]{:S(2)}) async-start(bf16[32,16,2048]{2,1,0:T(8,128)(2,1)} %bitcast.136), calls=%async_computation.15 | async-start | bytes 4194304 | tf_op jit(solution)/shard_map/all_to_all | solution.py:287
  792.1 9.4 collective-permute-start.6
  807.4 6.3 copy-start.3
  807.4 34.1 %all-to-all-start.16 = ((bf16[32,16,2048]{2,1,0:T(8,128)(2,1)}), bf16[32,16,2048]{2,1,0:T(8,128)(2,1)}, u32[]{:S(2)}, u32[]{:S(2)}) async-start(bf16[32,16,2048]{2,1,0:T(8,128)(2,1)} %bitcast.138), calls=%async_computation.16 | async-start | bytes 4194304 | tf_op jit(solution)/shard_map/all_to_all | solution.py:287
  867.1 6.3 copy-start.135
  867.1 6.3 copy-start.167
  867.1 34.1 %all-to-all-start.17 = ((bf16[32,16,2048]{2,1,0:T(8,128)(2,1)}), bf16[32,16,2048]{2,1,0:T(8,128)(2,1)S(1)}, u32[]{:S(2)}, u32[]{:S(2)}) async-start(bf16[32,16,2048]{2,1,0:T(8,128)(2,1)} %bitcast.134), calls=%async_computation.17 | async-start | bytes 4194304 | tf_op jit(solution)/shard_map/all_to_all | solution.py:287
  873.3 113.3 %all-gather.6.cloned.1.call-start = ((), (), s32[]{:S(2)}) async-start(), calls=%async_computation.21 | async-start | bytes 4325376 | tf_op jit(solution)/shard_map/all_gather | solution.py:543
  902.3 13.3 %copy-start.71 = (bf16[64,2048]{1,0:T(8,128)(2,1)S(1)}, bf16[64,2048]{1,0:T(8,128)(2,1)}, u32[]{:S(2)}) copy-start(bf16[64,2048]{1,0:T(8,128)(2,1)} %copy-done.69) | copy-start | bytes 786436
  902.3 13.3 %copy-start.126 = (f32[64,512]{1,0:T(8,128)S(1)}, f32[64,512]{1,0:T(8,128)}, u32[]{:S(2)}) copy-start(f32[64,512]{1,0:T(8,128)} %copy-done.124) | copy-start | bytes 393220
  902.3 13.3 %copy-start.129 = (f32[64,512]{1,0:T(8,128)S(1)}, f32[64,512]{1,0:T(8,128)}, u32[]{:S(2)}) copy-start(f32[64,512]{1,0:T(8,128)} %copy-done.127) | copy-start | bytes 393220
  902.3 13.3 %copy-start.165 = (f32[32,2048]{1,0:T(8,128)S(1)}, f32[32,2048]{1,0:T(8,128)}, u32[]{:S(2)}) copy-start(f32[32,2048]{1,0:T(8,128)} %copy-done.164) | copy-start | bytes 786436
  904.2 7.1 collective-permute-start.7
  920.5 9.1 copy-start.4
  920.5 38.0 %all-to-all-start.18 = ((bf16[32,16,2048]{2,1,0:T(8,128)(2,1)}), bf16[32,16,2048]{2,1,0:T(8,128)(2,1)}, u32[]{:S(2)}, u32[]{:S(2)}) async-start(bf16[32,16,2048]{2,1,0:T(8,128)(2,1)} %bitcast.131), calls=%async_computation.18 | async-start | bytes 4194304 | tf_op jit(solution)/shard_map/all_to_all | solution.py:287
  947.6 25.6 %slice-start = ((s8[6291456]{0:T(1024)(128)(4,1)}), s8[2097152]{0:T(1024)(128)(4,1)S(1)}, s32[]{:S(2)}) async-start(s8[6291456]{0:T(1024)(128)(4,1)} %bitcast.98), calls=%async_computation.23 | async-start | bytes 4194304
  966.6 6.6 slice-start.1
  966.6 6.6 copy-start.27
  (161 other events, 243.9 us)
Sparse Core Ops, SparseCore 0:
  611.8 92.4 reduce-scatter.3
  707.3 79.9 all-gather.3
  920.6 61.7 all-gather.5

commit v2 on v1

--- a/solution.py
+++ b/solution.py
@@ -40,7 +40,21 @@
     return pl.BlockSpec(array.shape, lambda *_: (0,) * rank)
 
 
-def run(kernel, args, in_specs, outs, out_specs, grid=(1,), scratch=(), aliases=None, cost=1e9):
+class Far:
+    def __init__(self, array):
+        self.value = pltpu.with_memory_space_constraint(array, pltpu.HBM)
+
+
+def far(arrays):
+    return [Far(a) for a in arrays]
+
+
+def far_out(shape):
+    return pltpu.HBM(shape.shape, shape.dtype)
+
+
+def run(kernel, args, in_specs, outs, out_specs, grid=(1,), scratch=(), aliases=None, cost=1e9, room=20):
+    args = [a.value if isinstance(a, Far) else a for a in args]
     moved = sum(a.size * a.dtype.itemsize for a in args[1:])
     return pl.pallas_call(
         kernel,
@@ -53,7 +67,7 @@
         ),
         out_shape=outs,
         input_output_aliases=aliases or {},
-        compiler_params=pltpu.CompilerParams(vmem_limit_bytes=40 * MIB),
+        compiler_params=pltpu.CompilerParams(vmem_limit_bytes=room * MIB),
         cost_estimate=pl.CostEstimate(flops=int(cost), bytes_accessed=moved, transcendentals=0),
     )(*args)
 
@@ -133,25 +147,29 @@
     c2_ref[...] = 1.0 - tanh * tanh
 
 
-def expert_fwd_kernel(sec, x_ref, wg_ref, wu_ref, wd_ref, out_ref, acc_ref):
+def expert_fwd_kernel(first, sec, x_ref, wg_ref, wu_ref, wd_ref, *refs):
+    out_ref, hidden_ref = refs[-2:]
     step = pl.program_id(0)
-    packed = x_ref[...]
-    gate = nn(packed, wg_ref[...])
-    up = nn(packed, wu_ref[...])
-    hidden = (gate * jax.nn.sigmoid(gate) * up).astype(BF)
-    part = nn(hidden, wd_ref[...])
-
-    @pl.when(step == 0)
-    def _():
-        acc_ref[...] = part
-
-    @pl.when((step > 0) & (step < pl.num_programs(0) - 1))
-    def _():
-        acc_ref[...] += part
-
-    @pl.when(step == pl.num_programs(0) - 1)
-    def _():
-        out_ref[...] = (acc_ref[...] + part).astype(BF)
+    tile = wg_ref.shape[1]
+
+    @pl.when(step < first)
+    def _():
+        packed = x_ref[...]
+        gate = nn(packed, wg_ref[...])
+        up = nn(packed, wu_ref[...])
+        cols = pl.ds(pl.multiple_of(step * tile, tile), tile)
+        hidden_ref[:, cols] = (gate * jax.nn.sigmoid(gate) * up).astype(BF)
+
+    @pl.when(step >= first)
+    def _():
+        out_ref[...] = nn(hidden_ref[...], wd_ref[...]).astype(BF)
+
+
+def turn_kernel(sec, wg_ref, wu_ref, wd_ref, dep_ref, gu_ref, down_ref):
+    tile = wg_ref.shape[1]
+    gu_ref[:tile] = wg_ref[...].T
+    gu_ref[tile:] = wu_ref[...].T
+    down_ref[...] = wd_ref[...].T
 
 
 def combine_fwd_kernel(sec, ret_ref, h_ref, phl_ref, out_ref):
@@ -173,6 +191,23 @@
     loss_ref[...] = jnp.broadcast_to(jnp.sum(token_loss, axis=0, keepdims=True), loss_ref.shape)
 
 
+def head_sum_kernel(sec, *refs):
+    ins, out_ref = refs[:-2], refs[-1]
+    out_ref[...] = sum(
+        tn(ins[i][...], ins[i + 1][...]) for i in range(0, len(ins), 2)
+    ).astype(BF)
+
+
+def piece_kernel(experts, sec, in_ref, out_ref):
+    share = in_ref.shape[0] // experts
+    total = in_ref[:share].astype(F32)
+    for part in range(1, experts):
+        total = total + in_ref[part * share : (part + 1) * share].astype(F32)
+    high, low = hi_lo(total)
+    out_ref[:share] = high
+    out_ref[share:] = low
+
+
 def prep_bwd_kernel(tick, n_g, n_p, sec, *refs):
     g_refs, phl_refs, (g_ref, out_ref) = refs[:n_g], refs[n_g : n_g + n_p], refs[n_g + n_p :]
     flag = sec[0] == sec[1] - tick
@@ -181,7 +216,8 @@
 
     @pl.when(step == 0)
     def _():
-        g_ref[...] = pick(flag, g_refs)
+        found = [ref[: g_ref.shape[0]] for ref in g_refs]
+        g_ref[...] = found[0] if n_g == 1 else jnp.where(flag, found[0], found[1])
 
     cols = g_ref[:, pl.ds(pl.multiple_of(step * chunk, chunk), chunk)]
     probs = pick(flag, phl_refs)
@@ -190,7 +226,8 @@
 
 def route_bwd_kernel(tick, slots, n, micros, sec, g_ref, *refs):
     r_refs, h_refs, p_refs, c_refs = (refs[i * n : (i + 1) * n] for i in range(4))
-    router_t_ref, acc_in_ref, gn_ref, acc_ref = refs[4 * n :]
+    router_t_ref, acc_in_ref = refs[4 * n : 4 * n + 2]
+    carry_refs, (gn_ref, acc_ref) = refs[4 * n + 2 : -2], refs[-2:]
     flag = sec[0] == sec[1] - tick
     micro = tick - (sec[1] - 1 - sec[0])
     active = (micro >= 0) & (micro < micros)
@@ -203,7 +240,12 @@
     grad_route = nt(grad_chosen, spreading(experts, slots)).astype(BF)
     gn_ref[...] = nn(grad_route, router_t_ref[...])
     normed = normalize(pick(flag, h_refs))[2]
-    acc_ref[...] = acc_in_ref[...] + jnp.where(active, tn(grad_route, normed), 0.0)
+    total = acc_in_ref[...] + jnp.where(active, tn(grad_route, normed), 0.0)
+    if carry_refs:
+        acc_ref[:experts] = total.astype(BF)
+        acc_ref[experts:] = carried(sec, grad.shape[0], carry_refs)
+    else:
+        acc_ref[...] = total
 
 
 def again_kernel(tick, n, sec, *refs):
@@ -215,8 +257,8 @@
     up = nn(packed, wu_ref[...])
     sigmoid = jax.nn.sigmoid(gate)
     silu = gate * sigmoid
-    a1_ref[...] = up * sigmoid * (1.0 + gate * (1.0 - sigmoid))
-    a2_ref[...] = silu
+    a1_ref[...] = (up * sigmoid * (1.0 + gate * (1.0 - sigmoid))).astype(BF)
+    a2_ref[...] = silu.astype(BF)
     ht_ref[0] = (silu * up).astype(BF).T
 
     @pl.when(pl.program_id(0) == 0)
@@ -224,43 +266,93 @@
         xt_ref[0] = packed.T
 
 
-def expert_bwd_kernel(last, sec, dy_ref, wd_ref, a1_ref, a2_ref, *refs):
+def expert_bwd_kernel(first, sec, dy_ref, wd_ref, a1_ref, a2_ref, wgu_ref, *refs):
+    gg_ref, gu_ref, dys_ref, out_ref, both_ref = refs[-5:]
     step = pl.program_id(0)
-    if last:
-        gg_ref, gu_ref, dys_ref = refs[-3:]
-    else:
-        wg_ref, wu_ref = refs[:2]
-        gg_ref, gu_ref, dys_ref, out_ref, acc_ref = refs[-5:]
-    rows = dy_ref[...]
-    grad_hidden = nt(rows, wd_ref[...])
-    gg = (grad_hidden * a1_ref[...]).astype(BF)
-    gu = (grad_hidden * a2_ref[...]).astype(BF)
-    gg_ref[0] = gg
-    gu_ref[0] = gu
+    tile = wd_ref.shape[1]
 
     @pl.when(step == 0)
     def _():
-        dys_ref[0] = rows
-
-    if last:
-        return
-    part = nt(gg, wg_ref[...]) + nt(gu, wu_ref[...])
+        dys_ref[0] = dy_ref[...]
+
+    @pl.when(step < first)
+    def _():
+        grad_hidden = nn(dy_ref[...], wd_ref[...])
+        gg = (grad_hidden * a1_ref[...].astype(F32)).astype(BF)
+        gu = (grad_hidden * a2_ref[...].astype(F32)).astype(BF)
+        gg_ref[0] = gg
+        gu_ref[0] = gu
+        at = pl.multiple_of(step * 2 * tile, tile)
+        both_ref[:, pl.ds(at, tile)] = gg
+        both_ref[:, pl.ds(pl.multiple_of(at + tile, tile), tile)] = gu
+
+    @pl.when(step >= first)
+    def _():
+        out_ref[...] = nn(both_ref[...], wgu_ref[...]).astype(BF)
+
+
+def earlier_kernel(sec, xt_ref, gg_ref, gu_ref, ht_ref, dy_ref, gate_ref, up_ref, down_ref, dy_now):
+    done = sec[0] != 0
+
+    @pl.when(pl.program_id(0) == 0)
+    def _():
+        dy_now[...] = jnp.where(done, dy_ref[1], jnp.zeros((), BF))
+
+    gg = jnp.where(done, gg_ref[1], jnp.zeros((), BF))
+    gu = jnp.where(done, gu_ref[1], jnp.zeros((), BF))
+    gate_ref[...] = (nn(xt_ref[0], gg_ref[0]) + nn(xt_ref[1], gg)).astype(BF)
+    up_ref[...] = (nn(xt_ref[0], gu_ref[0]) + nn(xt_ref[1], gu)).astype(BF)
+    down_ref[...] = (nn(ht_ref[0], dy_ref[0]) + nn(ht_ref[1], dy_now[...])).astype(BF)
+
+
+def final_kernel(sec, dy_ref, wd_ref, a1_ref, a2_ref, xt_ref, ht_ref, *refs):
+    gate_old, up_old, down_old, gate_ref, up_ref, down_ref, dy_now = refs
+    mine = sec[0] == 0
+
+    @pl.when(pl.program_id(0) == 0)
+    def _():
+        dy_now[...] = jnp.where(mine, dy_ref[...], jnp.zeros((), BF))
+
+    grad_hidden = nn(dy_now[...], wd_ref[...])
+    gg = (grad_hidden * a1_ref[...].astype(F32)).astype(BF)
+    gu = (grad_hidden * a2_ref[...].astype(F32)).astype(BF)
+    gate_ref[...] = (gate_old[...].astype(F32) + nn(xt_ref[0], gg)).astype(BF)
+    up_ref[...] = (up_old[...].astype(F32) + nn(xt_ref[0], gu)).astype(BF)
+    down_ref[...] = (down_old[...].astype(F32) + nn(ht_ref[0], dy_now[...])).astype(BF)
+
+
+def tail_kernel(held, sec, in_ref, router_ref, head_ref, loss_ref):
+    blocks = in_ref.shape[0]
+    experts = router_ref.shape[0]
+    total = in_ref[0, :experts].astype(F32)
+    for block in range(1, blocks):
+        total = total + in_ref[block, :experts].astype(F32)
+    step = pl.program_id(0)
 
     @pl.when(step == 0)
     def _():
-        acc_ref[...] = part
-
-    @pl.when((step > 0) & (step < pl.num_programs(0) - 1))
-    def _():
-        acc_ref[...] += part
-
-    @pl.when(step == pl.num_programs(0) - 1)
-    def _():
-        out_ref[...] = (acc_ref[...] + part).astype(BF)
+        router_ref[...] = total
+
+    @pl.when(step > 0)
+    def _():
+        router_ref[...] += total
+
+    for block in range(blocks):
+        rest = in_ref[block, experts:].astype(F32)
+        head_ref[block] = rest[:held] + rest[held : 2 * held]
+        loss_ref[block : block + 1] = rest[2 * held : 2 * held + 1, : loss_ref.shape[1]]
+
+
+def carried(sec, rows, refs):
+    own = refs[0][...]
+    if len(refs) == 1:
+        return own
+    return jnp.where(sec[0] == sec[1] - 1, own, refs[1][rows:])
 
 
 def combine_bwd_kernel(tick, n, sec, ret_ref, pt_ref, gn_ref, g_ref, *refs):
-    h_refs, (out_ref, sum_ref) = refs[:n], refs[n:]
+    h_refs, carry_refs, (out_ref, sum_ref) = refs[:n], refs[n:-2], refs[-2:]
+    rows = g_ref.shape[0]
     step = pl.program_id(0)
     chunk = ret_ref.shape[1]
     cols = pl.ds(pl.multiple_of(step * chunk, chunk), chunk)
@@ -272,15 +364,11 @@
         grad_normed = sum_ref[...] + gn_ref[...]
         normed_f = hidden_f * inv_rms
         mean = jnp.mean(grad_normed * normed_f, axis=-1, keepdims=True)
-        out_ref[...] = (
+        out_ref[:rows] = (
             g_ref[...].astype(F32) + inv_rms * (grad_normed - normed_f * mean)
         ).astype(BF)
-
-
-def weights_kernel(sec, xt_ref, gg_ref, gu_ref, ht_ref, dy_ref, gate_ref, up_ref, down_ref):
-    gate_ref[...] = (nn(xt_ref[0], gg_ref[0]) + nn(xt_ref[1], gg_ref[1])).astype(BF)
-    up_ref[...] = (nn(xt_ref[0], gu_ref[0]) + nn(xt_ref[1], gu_ref[1])).astype(BF)
-    down_ref[...] = (nn(ht_ref[0], dy_ref[0]) + nn(ht_ref[1], dy_ref[1])).astype(BF)
+        if carry_refs:
+            out_ref[rows:] = carried(sec, rows, carry_refs)
 
 
 def to_owners(rows):
@@ -308,7 +396,7 @@
     ticks = micros + sections - 1
     sec = jnp.stack([section, jnp.int32(sections)]).astype(jnp.int32)
     tile = 256
-    chunk = 512
+    chunk = 1024
     steps = ffe // tile
     col_steps = width // chunk
     row_block = pl.BlockSpec((rows, chunk), lambda i, s: (0, i))
@@ -318,6 +406,10 @@
     act_block = pl.BlockSpec((packed, tile), lambda i, s: (0, i))
     row_full = sds((rows, width), BF)
     buf_full = sds((packed, width), BF)
+    buf_out = pltpu.HBM((packed, width), BF)
+    wide_chunk = 1024
+    late_block = pl.BlockSpec((packed, wide_chunk), lambda i, s: (0, jnp.maximum(i - steps, 0)))
+    anywhere = pl.BlockSpec(memory_space=pl.ANY)
     matmul = 2.0 * packed * width * ffe
 
     [places] = run(
@@ -348,7 +440,7 @@
             functools.partial(prep_fwd_kernel, len(ins) == 2),
             (sec, *ins, places),
             [whole(row_full)] * len(ins) + [micro_spec],
-            [row_full, row_full, buf_full],
+            [far_out(row_full), row_full, buf_out],
             [whole(row_full), whole(row_full), buf_block],
             grid=(col_steps,),
             cost=2 * rows * packed * width,
@@ -360,24 +452,44 @@
             functools.partial(route_fwd_kernel, slots),
             (sec, normed, router_w, places),
             [whole(row_full), whole(router_w), micro_spec],
-            [two, wide, wide],
+            [far_out(two), far_out(wide), far_out(wide)],
             [whole(two), whole(wide), whole(wide)],
             cost=2 * rows * width * experts,
         )
+        if tick == 1:
+            turned_gu, turned_down = run(
+                turn_kernel,
+                (sec, *far([gate_w, up_w, down_w, outgoing])),
+                [in_block, in_block, down_block, anywhere],
+                [pltpu.HBM((2 * ffe, width), BF), pltpu.HBM((width, ffe), BF)],
+                [pl.BlockSpec((2 * tile, width), lambda i, s: (i, 0)), in_block],
+                grid=(steps,),
+                cost=matmul,
+            )
+            after = (turned_gu,)
+        else:
+            after = ()
         [results] = run(
-            expert_fwd_kernel,
-            (sec, arrived, gate_w, up_w, down_w),
-            [whole(buf_full), in_block, in_block, down_block],
-            [buf_full],
-            [whole(buf_full)],
-            grid=(steps,),
-            scratch=[pltpu.VMEM((packed, width), F32)],
+            functools.partial(expert_fwd_kernel, steps),
+            (sec, arrived, gate_w, up_w, down_w, *far(after)),
+            [
+                whole(buf_full),
+                pl.BlockSpec((width, tile), lambda i, s: (0, jnp.minimum(i, steps - 1))),
+                pl.BlockSpec((width, tile), lambda i, s: (0, jnp.minimum(i, steps - 1))),
+                pl.BlockSpec((ffe, wide_chunk), lambda i, s: (0, jnp.maximum(i - steps, 0))),
+                *[anywhere for _ in after],
+            ],
+            [buf_out],
+            [late_block],
+            grid=(steps + width // wide_chunk,),
+            scratch=[pltpu.VMEM((packed, ffe), BF)],
             cost=3 * matmul,
+            room=24,
         )
         returned = to_owners(results)
         [layer_out] = run(
             combine_fwd_kernel,
-            (sec, returned, layer_in, probs_two),
+            (sec, returned, *far([layer_in, probs_two])),
             [buf_block, row_block, whole(two)],
             [row_full],
             [row_block],
@@ -398,31 +510,16 @@
                         head_kernel,
                         (sec, layer_out, class_head, label_col),
                         [whole(row_full), whole(class_head), whole(label_col)],
-                        [row_full, glog_full, loss_full],
+                        [far_out(row_full), far_out(glog_full), far_out(loss_full)],
                         [whole(row_full), whole(glog_full), whole(loss_full)],
                         cost=4 * rows * width * class_head.shape[1],
                     ),
                 )
             )
 
-    head_term = sum(
-        dot(final, glog, ((0,), (0,))) for final, _, glog, _ in finals
-    )
-    loss_term = sum(loss for _, _, _, loss in finals)
     share = width // experts
-    head_parts = jnp.concatenate(
-        [
-            head_term.reshape(experts, share, -1),
-            jnp.broadcast_to(loss_term[None], (experts, *loss_term.shape)),
-        ],
-        axis=1,
-    )
-    head_parts = lax.psum_scatter(head_parts, plane, scatter_dimension=0, tiled=True)
-    head_all = lax.all_gather(head_parts, ("section", *plane), axis=0, tiled=True)
-    head_all = head_all[(sections - 1) * experts :]
-    head_total = head_all[:, :share].reshape(width, -1)
-    mean_loss = head_all[0, share, 0] / (micros * rows * experts)
-
+    carry_rows = 16
+    classes = class_head.shape[1]
     router_sum = jnp.zeros((experts, width), F32)
     store = None
     for tick in range(ticks):
@@ -451,9 +548,9 @@
         count = len(cands)
         gsel, outgoing = run(
             functools.partial(prep_bwd_kernel, tick, len(grads), count),
-            (sec, *grads, *[c[3] for c in cands]),
-            [whole(row_full)] * len(grads) + [whole(c[3]) for c in cands],
-            [row_full, buf_full],
+            (sec, *grads, *far([c[3] for c in cands])),
+            [whole(a) for a in grads] + [whole(c[3]) for c in cands],
+            [far_out(row_full), buf_out],
             [whole(row_full), buf_block],
             grid=(col_steps,),
             cost=4 * rows * packed * width,
@@ -469,15 +566,19 @@
             router_sum,
         )
         wide_f = sds((rows, width), F32)
+        acc_full = sds((experts, width), F32)
+        if last:
+            route_args = (*route_args, own, incoming)
+            acc_full = sds((experts + carry_rows, width), BF)
         grad_normed, router_sum = run(
             functools.partial(route_bwd_kernel, tick, slots, count, micros),
-            (sec, *route_args),
+            (sec, *far(route_args)),
             [whole(a) for a in route_args],
-            [wide_f, router_sum],
-            [whole(wide_f), whole(router_sum)],
+            [far_out(wide_f), far_out(acc_full)],
+            [whole(wide_f), whole(acc_full)],
             cost=2 * rows * packed * width,
         )
-        act = sds((packed, ffe), F32)
+        act = sds((packed, ffe), BF)
         stores = [
             sds((micros + 1, ffe, packed), BF),
             sds((micros + 1, width, packed), BF),
@@ -485,13 +586,12 @@
             sds((micros + 1, packed, ffe), BF),
             sds((micros + 1, packed, width), BF),
         ]
-        anywhere = pl.BlockSpec(memory_space=pl.ANY)
         old = [] if store is None else list(store[:2])
         a1, a2, hidden_t, packed_t = run(
             functools.partial(again_kernel, tick, count),
-            (sec, *[c[0] for c in cands], gate_w, up_w, *old),
+            (sec, *far([c[0] for c in cands]), *far([gate_w, up_w]), *far(old)),
             [whole(buf_full)] * count + [in_block, in_block] + [anywhere] * len(old),
-            [act, act, *stores[:2]],
+            [far_out(act), far_out(act), *[far_out(a) for a in stores[:2]]],
             [
                 act_block,
                 act_block,
@@ -501,68 +601,147 @@
             grid=(steps,),
             aliases={3 + count + i: 2 + i for i in range(len(old))},
             cost=2 * matmul,
-        )
-        old = [] if store is None else list(store[2:])
-        args = [arrived, down_w, a1, a2] + ([] if last else [gate_w, up_w])
-        specs = [whole(buf_full), down_block, act_block, act_block]
-        specs += [] if last else [in_block, in_block]
-        outs = stores[2:] + ([] if last else [buf_full])
-        out_specs = [
-            slot_block((packed, tile), lambda i: (0, i)),
-            slot_block((packed, tile), lambda i: (0, i)),
-            slot_block((packed, width), lambda i: (0, 0)),
-        ] + ([] if last else [whole(buf_full)])
-        got = run(
-            functools.partial(expert_bwd_kernel, last),
-            (sec, *args, *old),
-            specs + [anywhere] * len(old),
-            outs,
-            out_specs,
-            grid=(steps,),
-            scratch=[] if last else [pltpu.VMEM((packed, width), F32)],
-            aliases={1 + len(args) + i: i for i in range(len(old))},
-            cost=matmul if last else 3 * matmul,
-        )
-        store = (hidden_t, packed_t, *got[:3])
+            room=28,
+        )
+        if tick == 1:
+            head_full = sds((width, classes), BF)
+            head_args = [part for final in finals for part in (final[0], final[2])]
+            [head_term] = run(
+                head_sum_kernel,
+                (sec, *far(head_args), *far([a1])),
+                [*[whole(a) for a in head_args], anywhere],
+                [far_out(head_full)],
+                [whole(head_full)],
+                cost=4 * rows * width * classes,
+            )
+            pieces = to_owners(head_term)
+            piece_full = sds((2 * share, classes), BF)
+            [piece] = run(
+                functools.partial(piece_kernel, experts),
+                (sec, pieces),
+                [whole(pieces)],
+                [piece_full],
+                [whole(piece_full)],
+            )
+            loss_pair = jnp.stack(hi_lo(sum(final[3][0, 0] for final in finals)))
+            flat = jnp.concatenate([piece.reshape(-1), loss_pair])
+            own = jnp.pad(flat, (0, carry_rows * width - flat.size)).reshape(carry_rows, width)
         if last:
             break
+        old = [] if store is None else list(store[2:])
+        args = [arrived, turned_down, a1, a2, turned_gu]
+        early = lambda i: jnp.minimum(i, steps - 1)
+        got = run(
+            functools.partial(expert_bwd_kernel, steps),
+            (sec, arrived, *far([turned_down, a1, a2, turned_gu, *old])),
+            [
+                whole(buf_full),
+                pl.BlockSpec((width, tile), lambda i, s: (0, early(i))),
+                pl.BlockSpec((packed, tile), lambda i, s: (0, early(i))),
+                pl.BlockSpec((packed, tile), lambda i, s: (0, early(i))),
+                pl.BlockSpec(
+                    (2 * ffe, wide_chunk), lambda i, s: (0, jnp.maximum(i - steps, 0))
+                ),
+                *[anywhere] * len(old),
+            ],
+            [*[far_out(a) for a in stores[2:]], buf_out],
+            [
+                slot_block((packed, tile), lambda i: (0, early(i))),
+                slot_block((packed, tile), lambda i: (0, early(i))),
+                slot_block((packed, width), lambda i: (0, 0)),
+                late_block,
+            ],
+            grid=(steps + width // wide_chunk,),
+            scratch=[pltpu.VMEM((packed, 2 * ffe), BF)],
+            room=32,
+            aliases={1 + len(args) + i: i for i in range(len(old))},
+            cost=3 * matmul,
+        )
+        store = (hidden_t, packed_t, *got[:3])
         returned = to_owners(got[3])
+        carry = [] if tick == 0 else [own] if tick == 1 else [own, incoming]
+        grad_full = sds((rows + (carry_rows if carry else 0), width), BF)
         [grad_in] = run(
             functools.partial(combine_bwd_kernel, tick, count),
-            (sec, returned, places, grad_normed, gsel, *[c[2] for c in cands]),
+            (sec, returned, places, *far([grad_normed, gsel, *[c[2] for c in cands]]), *carry),
             [buf_block, place_block(micro_of), whole(wide_f), whole(row_full)]
-            + [whole(row_full)] * count,
-            [row_full],
-            [whole(row_full)],
+            + [whole(row_full)] * count
+            + [whole(a) for a in carry],
+            [grad_full],
+            [whole(grad_full)],
             grid=(col_steps,),
             scratch=[pltpu.VMEM((rows, width), F32)],
             cost=2 * rows * packed * width,
         )
         incoming = from_behind(grad_in, "section", -1)
 
-    router_parts = lax.all_gather(router_sum.astype(BF), plane, axis=0, tiled=False)
-    router_out = jnp.sum(router_parts.astype(F32), axis=0).T[None]
-
-    hidden_t, packed_t, gate_rows, up_rows, out_rows = store
-    act_pair = pl.BlockSpec((micros, packed, ffe), lambda i, s: (0, 0, 0))
+    everyone = lax.all_gather(router_sum, plane, axis=0, tiled=False)
+    held = share * classes // width
+    router_full, head_full = sds((experts, width), F32), sds((experts, held, width), F32)
+    loss_full = sds((experts, 128), F32)
+    router_rows, head_rows, loss_rows = run(
+        functools.partial(tail_kernel, held),
+        (sec, everyone),
+        [pl.BlockSpec((8, *everyone.shape[1:]), lambda i, s: (i, 0, 0))],
+        [router_full, head_full, loss_full],
+        [
+            whole(router_full),
+            pl.BlockSpec((8, held, width), lambda i, s: (i, 0, 0)),
+            pl.BlockSpec((8, 128), lambda i, s: (i, 0)),
+        ],
+        grid=(experts // 8,),
+    )
+    router_out = router_rows.T[None]
+    head_total = head_rows.reshape(width, classes)
+    mean_loss = jnp.sum(loss_rows[:, :2]) / (micros * rows * experts)
+
+    both_slots = lambda shape, place: pl.BlockSpec((micros, *shape), lambda i, s: (0, *place(i)))
+    next_slot = lambda shape, place: pl.BlockSpec((1, *shape), lambda i, s: (1, *place(i)))
+    up_tile = lambda i: (i, 0)
+    side_tile = lambda i: (0, i)
+    stay = lambda i: (0, 0)
+    grad_shapes = [sds((width, ffe), BF), sds((width, ffe), BF), sds((ffe, width), BF)]
+    earlier = run(
+        earlier_kernel,
+        (sec, *far([packed_t, store[2], store[3], hidden_t, store[4]])),
+        [
+            both_slots((width, packed), stay),
+            both_slots((packed, tile), side_tile),
+            both_slots((packed, tile), side_tile),
+            both_slots((tile, packed), up_tile),
+            both_slots((packed, width), stay),
+        ],
+        [far_out(a) for a in grad_shapes],
+        [in_block, in_block, down_block],
+        grid=(steps,),
+        scratch=[pltpu.VMEM((packed, width), BF)],
+        cost=6 * matmul,
+        room=32,
+    )
     grad_gate, grad_up, grad_down = run(
-        weights_kernel,
-        (sec, packed_t, gate_rows, up_rows, hidden_t, out_rows),
+        final_kernel,
+        (
+            sec,
+            arrived,
+            *far([turned_down, a1, a2, packed_t, hidden_t, *earlier]),
+        ),
         [
-            pl.BlockSpec((micros, chunk, packed), lambda i, s: (0, i, 0)),
-            act_pair,
-            act_pair,
-            pl.BlockSpec((micros, ffe, packed), lambda i, s: (0, 0, 0)),
-            pl.BlockSpec((micros, packed, chunk), lambda i, s: (0, 0, i)),
+            whole(buf_full),
+            in_block,
+            act_block,
+            act_block,
+            next_slot((width, packed), stay),
+            next_slot((tile, packed), up_tile),
+            in_block,
+            in_block,
+            down_block,
         ],
-        [sds((width, ffe), BF), sds((width, ffe), BF), sds((ffe, width), BF)],
-        [
-            pl.BlockSpec((chunk, ffe), lambda i, s: (i, 0)),
-            pl.BlockSpec((chunk, ffe), lambda i, s: (i, 0)),
-            pl.BlockSpec((ffe, chunk), lambda i, s: (0, i)),
-        ],
-        grid=(col_steps,),
-        cost=6 * matmul,
+        grad_shapes,
+        [in_block, in_block, down_block],
+        grid=(steps,),
+        scratch=[pltpu.VMEM((packed, width), BF)],
+        cost=4 * matmul,
+        room=32,
     )
     return (
         mean_loss,

time: 1010 us -> 920 us (0.911)
  local copies, waits for them, and re-layouts: 169 us -> 27.8 us
  Pallas kernels: 237 us -> 282 us
  waiting for transfers between devices: 303 us -> 340 us
  blocking collectives: 147 us -> 111 us
    unnamed x399 -> x91, local copies, waits for them, and re-layouts: 161 us -> 20.2 us
    all_to_all x15 -> x17, waiting for transfers between devices: 222 us -> 289 us  [to_owners(): return lax.all_to_all(rows, plane, split_axis=0, concat_axis=0, tiled=True)]
    unnamed x4 -> x1, waiting for transfers between devices: 44.9 us -> 0.02 us
    pallas_call x48 -> x52, Pallas kernels: 237 us -> 282 us  [run(): pl.pallas_call(kernel, grid_spec=pltpu.PrefetchScalarGridSpec(num_scalar_...]
    all_to_all x4 -> x3, blocking collectives: 147 us -> 111 us  [to_owners(): return lax.all_to_all(rows, plane, split_axis=0, concat_axis=0, tiled=True)]
    all_gather x2 -> x1, waiting for transfers between devices: 0.01 us -> 12.2 us  [shards(): everyone = lax.all_gather(router_sum, plane, axis=0, tiled=False)]
    all_to_all x15 -> x17, starting transfers between devices: 97.7 us -> 108 us  [to_owners(): return lax.all_to_all(rows, plane, split_axis=0, concat_axis=0, tiled=True)]
  transfers between devices with their start and end apart: 26 -> 26, of which waited for: 21 -> 24; matrix products, arithmetic and copies ran while one was open for 1% -> 1% of each run, Pallas kernels for 16% -> 19%
where the time goes in v2:
time: 920 us; the launch traced here: 908 us
  waiting for transfers between devices  340 us (37%)
  Pallas kernels  282 us (31%)
  starting transfers between devices  129 us (14%)
  blocking collectives  111 us (12%)
  local copies, waits for them, and re-layouts  27.8 us (3%)
  between operations  18.1 us (2%)
    all_to_all x17, waiting for transfers between devices, to_owners(): return lax.all_to_all(rows, plane, split_axis=0, concat_axis=0, tiled=True)  289 us
    pallas_call x52, Pallas kernels, run(): pl.pallas_call(kernel, grid_spec=pltpu.PrefetchScalarGridSpec(num_scalar_...  282 us
    all_to_all x3, blocking collectives, to_owners(): return lax.all_to_all(rows, plane, split_axis=0, concat_axis=0, tiled=True)  111 us
    all_to_all x17, starting transfers between devices, to_owners(): return lax.all_to_all(rows, plane, split_axis=0, concat_axis=0, tiled=True)  108 us
    ppermute x8, waiting for transfers between devices, from_behind(): return lax.ppermute(block, axis, route)  39.4 us
    ppermute x8, starting transfers between devices, from_behind(): return lax.ppermute(block, axis, route)  21.5 us
    unnamed x91, local copies, waits for them, and re-layouts  20.2 us
  transfers between devices with their start and end apart: 26, of which 24 were waited for; matrix products, arithmetic and copies ran while one was open for 1% of the time, Pallas kernels for 19%

profile of v2, /device:TPU:1, one launch (start us, length us, event | category | flops | bytes accessed | tf_op | source)
XLA Modules:
  0.0 908.4 jit_solution(17576679492037021002)
XLA Ops:
  12.8 37.3 %all_to_all.220 = bf16[32,16,2048]{2,1,0:T(8,128)(2,1)S(1)} all-to-all(bf16[32,16,2048]{2,1,0:T(8,128)(2,1)} %bitcast.146), channel_id=1, replica_groups=mesh['section'=4,'expert'=4,'dp'=8] {'expert','dp'}, dimensions={0} | all-to-all | bytes 4194304 | tf_op jit(solution)/shard_map/all_to_all | solution.py:375
  50.1 8.1 shard_map.129
  58.2 4.2 all-to-all-start.1
  64.5 25.8 %all-to-all-done.1 = bf16[32,16,2048]{2,1,0:T(8,128)(2,1)S(1)} async-done(((bf16[32,16,2048]{2,1,0:T(8,128)(2,1)}), bf16[32,16,2048]{2,1,0:T(8,128)(2,1)S(1)}, u32[]{:S(2)}, u32[]{:S(2)}) %all-to-all-start.1) | async-done | bytes 2097184 | tf_op jit(solution)/shard_map/all_to_all | solution.py:375
  102.9 8.0 all-to-all-start.2
  110.9 9.8 %shard_map.133 = (bf16[1536,2048]{1,0:T(8,128)(2,1)}, bf16[2048,768]{1,0:T(8,128)(2,1)}) custom-call(s32[2]{0:T(128)S(1)} %pad_add_fusion.sec, bf16[2048,768]{1,0:T(8,128)(2,1)} %bitcast.67, bf16[2048,768]{1,0:T(8,128)(2,1)} %bitcast.78, bf16[768,2048]{1,0:T(8,128)(2,1)} %bitcast.99, bf16[512,2048]{1,0:T(8,128)(2,1)} %get-tuple-element.112.dep_ref), custom_call_target="tpu_custom_call" | custom-call | flops 1610612736 | bytes 11534336 | tf_op jit(solution)/shard_map/pallas_call | solution.py:59
  120.7 18.1 %all-to-all-done.2 = bf16[32,16,2048]{2,1,0:T(8,128)(2,1)} async-done(((bf16[32,16,2048]{2,1,0:T(8,128)(2,1)}), bf16[32,16,2048]{2,1,0:T(8,128)(2,1)}, u32[]{:S(2)}, u32[]{:S(2)}) %all-to-all-start.2) | async-done | bytes 2097184 | tf_op jit(solution)/shard_map/all_to_all | solution.py:375
  142.6 9.5 %shard_map.134 = bf16[512,2048]{1,0:T(8,128)(2,1)} custom-call(s32[2]{0:T(128)S(1)} %pad_add_fusion.sec, bf16[512,2048]{1,0:T(8,128)(2,1)} %bitcast.13.x_ref.refs_1_.refs_0_, bf16[2048,768]{1,0:T(8,128)(2,1)S(1)} %bitcast.74, bf16[2048,768]{1,0:T(8,128)(2,1)S(1)} %bitcast.85, bf16[768,2048]{1,0:T(8,128)(2,1)S(1)} %bitcast.101, ...), custom_call_target="tpu_custom_call" | custom-call | flops 4831838208 | bytes 17825792 | tf_op jit(solution)/shard_map/pallas_call | solution.py:59
  152.1 6.9 all-to-all-start.3
  161.9 25.1 %all-to-all-done.3 = bf16[32,16,2048]{2,1,0:T(8,128)(2,1)} async-done(((bf16[32,16,2048]{2,1,0:T(8,128)(2,1)}), bf16[32,16,2048]{2,1,0:T(8,128)(2,1)}, u32[]{:S(2)}, u32[]{:S(2)}) %all-to-all-start.3) | async-done | bytes 2097184 | tf_op jit(solution)/shard_map/all_to_all | solution.py:375
  199.8 36.7 %all_to_all.221 = bf16[32,16,2048]{2,1,0:T(8,128)(2,1)S(1)} all-to-all(bf16[32,16,2048]{2,1,0:T(8,128)(2,1)} %bitcast.147), channel_id=1, replica_groups=mesh['section'=4,'expert'=4,'dp'=8] {'expert','dp'}, dimensions={0} | all-to-all | bytes 4194304 | tf_op jit(solution)/shard_map/all_to_all | solution.py:375
  236.5 8.1 shard_map.138
  244.6 5.4 all-to-all-start.5
  252.9 24.9 %all-to-all-done.5 = bf16[32,16,2048]{2,1,0:T(8,128)(2,1)} async-done(((bf16[32,16,2048]{2,1,0:T(8,128)(2,1)}), bf16[32,16,2048]{2,1,0:T(8,128)(2,1)}, u32[]{:S(2)}, u32[]{:S(2)}) %all-to-all-start.5) | async-done | bytes 2097184 | tf_op jit(solution)/shard_map/all_to_all | solution.py:375
  290.7 36.6 %all_to_all.222 = bf16[32,16,2048]{2,1,0:T(8,128)(2,1)S(1)} all-to-all(bf16[32,16,2048]{2,1,0:T(8,128)(2,1)} %bitcast.148), channel_id=1, replica_groups=mesh['section'=4,'expert'=4,'dp'=8] {'expert','dp'}, dimensions={0} | all-to-all | bytes 4194304 | tf_op jit(solution)/shard_map/all_to_all | solution.py:375
  327.4 8.1 shard_map.142
  335.5 4.2 all-to-all-start.7
  342.2 25.4 %all-to-all-done.7 = bf16[32,16,2048]{2,1,0:T(8,128)(2,1)S(1)} async-done(((bf16[32,16,2048]{2,1,0:T(8,128)(2,1)}), bf16[32,16,2048]{2,1,0:T(8,128)(2,1)S(1)}, u32[]{:S(2)}, u32[]{:S(2)}) %all-to-all-start.7) | async-done | bytes 2097184 | tf_op jit(solution)/shard_map/all_to_all | solution.py:375
  376.2 6.0 all-to-all-start.10
  382.2 4.1 collective-permute-start.3
  386.4 5.3 collective-permute-done.3.refs_0_
  394.3 15.9 %all-to-all-done.10 = bf16[32,16,2048]{2,1,0:T(8,128)(2,1)S(1)} async-done(((bf16[32,16,2048]{2,1,0:T(8,128)(2,1)}), bf16[32,16,2048]{2,1,0:T(8,128)(2,1)S(1)}, u32[]{:S(2)}, u32[]{:S(2)}) %all-to-all-start.10) | async-done | bytes 2097184 | tf_op jit(solution)/shard_map/all_to_all | solution.py:375
  411.5 6.0 all-to-all-start.8
  417.6 9.7 %shard_map.152 = (bf16[512,768]{1,0:T(8,128)(2,1)}, bf16[512,768]{1,0:T(8,128)(2,1)}, bf16[3,768,512]{2,1,0:T(8,128)(2,1)}, bf16[3,2048,512]{2,1,0:T(8,128)(2,1)}) custom-call(s32[2]{0:T(128)S(1)} %pad_add_fusion.sec, bf16[512,2048]{1,0:T(8,128)(2,1)} %bitcast.111, bf16[2048,768]{1,0:T(8,128)(2,1)} %bitcast.68, bf16[2048,768]{1,0:T(8,128)(2,1)} %bitcast.79), custom_call_target="tpu_custom_call" | custom-call | flops 3221225472 | bytes 8388608 | tf_op jit(solution)/shard_map/pallas_call | solution.py:59
  427.3 11.8 %shard_map.153 = (bf16[3,512,768]{2,1,0:T(8,128)(2,1)}, bf16[3,512,768]{2,1,0:T(8,128)(2,1)}, bf16[3,512,2048]{2,1,0:T(8,128)(2,1)}, bf16[512,2048]{1,0:T(8,128)(2,1)}) custom-call(s32[2]{0:T(128)S(1)} %pad_add_fusion.sec, bf16[512,2048]{1,0:T(8,128)(2,1)S(1)} %bitcast.120, bf16[2048,768]{1,0:T(8,128)(2,1)} %get-tuple-element.132.wd_ref, ...), custom_call_target="tpu_custom_call" | custom-call | flops 4831838208 | bytes 13107200 | tf_op jit(solution)/shard_map/pallas_call | solution.py:59
  439.1 6.4 all-to-all-done.8
  446.8 7.0 all-to-all-start.11
  459.2 8.2 shard_map.146
  467.4 14.4 %all-to-all-done.11 = bf16[32,16,2048]{2,1,0:T(8,128)(2,1)} async-done(((bf16[32,16,2048]{2,1,0:T(8,128)(2,1)}), bf16[32,16,2048]{2,1,0:T(8,128)(2,1)}, u32[]{:S(2)}, u32[]{:S(2)}) %all-to-all-start.11) | async-done | bytes 2097184 | tf_op jit(solution)/shard_map/all_to_all | solution.py:375
  481.8 6.2 all-to-all-start.9
  488.8 4.5 shard_map.154
  500.9 15.1 %all-to-all-done.9 = bf16[32,16,2048]{2,1,0:T(8,128)(2,1)S(1)} async-done(((bf16[32,16,2048]{2,1,0:T(8,128)(2,1)}), bf16[32,16,2048]{2,1,0:T(8,128)(2,1)S(1)}, u32[]{:S(2)}, u32[]{:S(2)}) %all-to-all-start.9) | async-done | bytes 2097184 | tf_op jit(solution)/shard_map/all_to_all | solution.py:375
  524.8 6.0 all-to-all-start.12
  530.8 10.3 %shard_map.157 = (bf16[512,768]{1,0:T(8,128)(2,1)}, bf16[512,768]{1,0:T(8,128)(2,1)}, bf16[3,768,512]{2,1,0:T(8,128)(2,1)}, bf16[3,2048,512]{2,1,0:T(8,128)(2,1)}) custom-call(s32[2]{0:T(128)S(1)} %pad_add_fusion.sec, bf16[512,2048]{1,0:T(8,128)(2,1)} %bitcast.113, bf16[512,2048]{1,0:T(8,128)(2,1)} %bitcast.97, ...), custom_call_target="tpu_custom_call", output_to_operand_aliasing={{2}: (5, {}), {3}: (6, {})} | custom-call | flops 3221225472 | bytes 19136512 | tf_op jit(solution)/shard_map/pallas_call | solution.py:59
  544.0 14.8 %all-to-all-done.12 = bf16[32,16,2048]{2,1,0:T(8,128)(2,1)S(1)} async-done(((bf16[32,16,2048]{2,1,0:T(8,128)(2,1)}), bf16[32,16,2048]{2,1,0:T(8,128)(2,1)S(1)}, u32[]{:S(2)}, u32[]{:S(2)}) %all-to-all-start.12) | async-done | bytes 2097184 | tf_op jit(solution)/shard_map/all_to_all | solution.py:375
  558.8 5.9 all-to-all-start.14
  564.7 11.8 %shard_map.158 = (bf16[3,512,768]{2,1,0:T(8,128)(2,1)}, bf16[3,512,768]{2,1,0:T(8,128)(2,1)}, bf16[3,512,2048]{2,1,0:T(8,128)(2,1)}, bf16[512,2048]{1,0:T(8,128)(2,1)}) custom-call(s32[2]{0:T(128)S(1)} %pad_add_fusion.sec, bf16[512,2048]{1,0:T(8,128)(2,1)S(1)} %bitcast.115, ...), custom_call_target="tpu_custom_call", output_to_operand_aliasing={{0}: (6, {}), {1}: (7, {}), {2}: (8, {})} | custom-call | flops 4831838208 | bytes 24117248 | tf_op jit(solution)/shard_map/pallas_call | solution.py:59
  576.5 7.5 all-to-all-start.13
  587.7 5.3 shard_map.159
  593.8 18.1 %all-to-all-done.13 = bf16[32,16,2048]{2,1,0:T(8,128)(2,1)S(1)} async-done(((bf16[32,16,2048]{2,1,0:T(8,128)(2,1)}), bf16[32,16,2048]{2,1,0:T(8,128)(2,1)S(1)}, u32[]{:S(2)}, u32[]{:S(2)}) %all-to-all-start.13) | async-done | bytes 2097184 | tf_op jit(solution)/shard_map/all_to_all | solution.py:375
  616.0 8.4 collective-permute-done.5.refs_0_.refs_3_
  628.0 7.6 all-to-all-start.15
  635.6 10.3 %shard_map.164 = (bf16[512,768]{1,0:T(8,128)(2,1)}, bf16[512,768]{1,0:T(8,128)(2,1)}, bf16[3,768,512]{2,1,0:T(8,128)(2,1)}, bf16[3,2048,512]{2,1,0:T(8,128)(2,1)}) custom-call(s32[2]{0:T(128)S(1)} %pad_add_fusion.sec, bf16[512,2048]{1,0:T(8,128)(2,1)} %bitcast.112, ...), custom_call_target="tpu_custom_call", output_to_operand_aliasing={{2}: (5, {}), {3}: (6, {})} | custom-call | flops 3221225472 | bytes 19136512 | tf_op jit(solution)/shard_map/pallas_call | solution.py:59
  645.9 17.4 %all-to-all-done.15 = bf16[32,16,2048]{2,1,0:T(8,128)(2,1)S(1)} async-done(((bf16[32,16,2048]{2,1,0:T(8,128)(2,1)}), bf16[32,16,2048]{2,1,0:T(8,128)(2,1)S(1)}, u32[]{:S(2)}, u32[]{:S(2)}) %all-to-all-start.15) | async-done | bytes 2097184 | tf_op jit(solution)/shard_map/all_to_all | solution.py:375
  663.3 11.8 %shard_map.165 = (bf16[3,512,768]{2,1,0:T(8,128)(2,1)}, bf16[3,512,768]{2,1,0:T(8,128)(2,1)}, bf16[3,512,2048]{2,1,0:T(8,128)(2,1)}, bf16[512,2048]{1,0:T(8,128)(2,1)}) custom-call(s32[2]{0:T(128)S(1)} %pad_add_fusion.sec, bf16[512,2048]{1,0:T(8,128)(2,1)S(1)} %bitcast.118, ...), custom_call_target="tpu_custom_call", output_to_operand_aliasing={{0}: (6, {}), {1}: (7, {}), {2}: (8, {})} | custom-call | flops 4831838208 | bytes 24117248 | tf_op jit(solution)/shard_map/pallas_call | solution.py:59
  675.1 6.0 all-to-all-start.16
  681.1 5.3 shard_map.166
  686.4 22.7 %all-to-all-done.16 = bf16[32,16,2048]{2,1,0:T(8,128)(2,1)S(1)} async-done(((bf16[32,16,2048]{2,1,0:T(8,128)(2,1)}), bf16[32,16,2048]{2,1,0:T(8,128)(2,1)S(1)}, u32[]{:S(2)}, u32[]{:S(2)}) %all-to-all-start.16) | async-done | bytes 2097184 | tf_op jit(solution)/shard_map/all_to_all | solution.py:375
  713.3 8.0 collective-permute-done.6.refs_0_.refs_3_
  724.7 7.3 all-to-all-start.17
  732.1 10.3 %shard_map.169 = (bf16[512,768]{1,0:T(8,128)(2,1)}, bf16[512,768]{1,0:T(8,128)(2,1)}, bf16[3,768,512]{2,1,0:T(8,128)(2,1)}, bf16[3,2048,512]{2,1,0:T(8,128)(2,1)}) custom-call(s32[2]{0:T(128)S(1)} %pad_add_fusion.sec, bf16[512,2048]{1,0:T(8,128)(2,1)} %bitcast.98, bf16[512,2048]{1,0:T(8,128)(2,1)} %bitcast.109, ...), custom_call_target="tpu_custom_call", output_to_operand_aliasing={{2}: (5, {}), {3}: (6, {})} | custom-call | flops 3221225472 | bytes 19136512 | tf_op jit(solution)/shard_map/pallas_call | solution.py:59
  742.3 17.6 %all-to-all-done.17 = bf16[32,16,2048]{2,1,0:T(8,128)(2,1)S(1)} async-done(((bf16[32,16,2048]{2,1,0:T(8,128)(2,1)}), bf16[32,16,2048]{2,1,0:T(8,128)(2,1)S(1)}, u32[]{:S(2)}, u32[]{:S(2)}) %all-to-all-start.17) | async-done | bytes 2097184 | tf_op jit(solution)/shard_map/all_to_all | solution.py:375
  759.9 11.8 %shard_map.170 = (bf16[3,512,768]{2,1,0:T(8,128)(2,1)}, bf16[3,512,768]{2,1,0:T(8,128)(2,1)}, bf16[3,512,2048]{2,1,0:T(8,128)(2,1)}, bf16[512,2048]{1,0:T(8,128)(2,1)}) custom-call(s32[2]{0:T(128)S(1)} %pad_add_fusion.sec, bf16[512,2048]{1,0:T(8,128)(2,1)S(1)} %bitcast.117, ...), custom_call_target="tpu_custom_call", output_to_operand_aliasing={{0}: (6, {}), {1}: (7, {}), {2}: (8, {})} | custom-call | flops 4831838208 | bytes 24117248 | tf_op jit(solution)/shard_map/pallas_call | solution.py:59
  771.7 6.0 all-to-all-start.18
  777.8 5.3 shard_map.171
  783.0 22.7 %all-to-all-done.18 = bf16[32,16,2048]{2,1,0:T(8,128)(2,1)S(1)} async-done(((bf16[32,16,2048]{2,1,0:T(8,128)(2,1)}), bf16[32,16,2048]{2,1,0:T(8,128)(2,1)S(1)}, u32[]{:S(2)}, u32[]{:S(2)}) %all-to-all-start.18) | async-done | bytes 2097184 | tf_op jit(solution)/shard_map/all_to_all | solution.py:375
  810.1 7.7 collective-permute-done.7.refs_0_.refs_7_
  821.3 4.6 shard_map.174
  825.8 7.3 all-to-all-start.19
  833.2 9.8 %shard_map.176 = (bf16[512,768]{1,0:T(8,128)(2,1)}, bf16[512,768]{1,0:T(8,128)(2,1)}, bf16[3,768,512]{2,1,0:T(8,128)(2,1)}, bf16[3,2048,512]{2,1,0:T(8,128)(2,1)}) custom-call(s32[2]{0:T(128)S(1)} %pad_add_fusion.sec, bf16[512,2048]{1,0:T(8,128)(2,1)} %bitcast.13.x_ref.refs_1_.refs_0_, ...), custom_call_target="tpu_custom_call", output_to_operand_aliasing={{2}: (4, {}), {3}: (5, {})} | custom-call | flops 3221225472 | bytes 17039360 | tf_op jit(solution)/shard_map/pallas_call | solution.py:59
  843.0 16.6 %shard_map.177 = (bf16[2048,768]{1,0:T(8,128)(2,1)}, bf16[2048,768]{1,0:T(8,128)(2,1)}, bf16[768,2048]{1,0:T(8,128)(2,1)}) custom-call(s32[2]{0:T(128)S(1)} %pad_add_fusion.sec, bf16[3,2048,512]{2,1,0:T(8,128)(2,1)} %get-tuple-element.199.xt_ref, bf16[3,512,768]{2,1,0:T(8,128)(2,1)} %get-tuple-element.201.gg_ref, ...), custom_call_target="tpu_custom_call" | custom-call | flops 9663676416 | bytes 19660800 | tf_op jit(solution)/shard_map/pallas_call | solution.py:59
  859.6 4.2 all-to-all-done.19
  863.8 16.2 %shard_map.178 = (bf16[2048,768]{1,0:T(8,128)(2,1)}, bf16[2048,768]{1,0:T(8,128)(2,1)}, bf16[768,2048]{1,0:T(8,128)(2,1)}) custom-call(s32[2]{0:T(128)S(1)} %pad_add_fusion.sec, bf16[512,2048]{1,0:T(8,128)(2,1)S(1)} %bitcast.116, bf16[2048,768]{1,0:T(8,128)(2,1)} %get-tuple-element.132.wd_ref, bf16[512,768]{1,0:T(8,128)(2,1)} %get-tuple-element.197.a1_ref, ...), custom_call_target="tpu_custom_call" | custom-call | flops 6442450944 | bytes 24903680 | tf_op jit(solution)/shard_map/pallas_call | solution.py:59
  880.0 12.2 %all-gather.3.cloned.1.call-done = bf16[1536,2048]{1,0:T(8,128)(2,1)} async-done(((bf16[48,2048]{1,0:T(8,128)(2,1)}), bf16[1536,2048]{1,0:T(8,128)(2,1)}) %all-gather.3.cloned.1.call-update) | async-done | bytes 6291472 | tf_op jit(solution)/shard_map/all_gather | solution.py:678
  (149 shorter events, 130.7 us)
Async XLA Ops:
  8.0 42.1 %copy-start.17 = (bf16[1,1,768,2048]{3,2,1,0:T(8,128)(2,1)S(1)}, bf16[1,1,768,2048]{3,2,1,0:T(8,128)(2,1)}, u32[]{:S(2)}) copy-start(bf16[1,1,768,2048]{3,2,1,0:T(8,128)(2,1)} %param.15) | copy-start | bytes 9437188
  9.3 40.8 %copy-start.3 = (bf16[1,1,2048,768]{3,2,1,0:T(8,128)(2,1)S(1)}, bf16[1,1,2048,768]{3,2,1,0:T(8,128)(2,1)}, u32[]{:S(2)}) copy-start(bf16[1,1,2048,768]{3,2,1,0:T(8,128)(2,1)} %param.14) | copy-start | bytes 9437188
  12.8 37.3 %copy-start.37 = (bf16[64,2048]{1,0:T(8,128)(2,1)}, bf16[64,2048]{1,0:T(8,128)(2,1)S(1)}, u32[]{:S(2)}) copy-start(bf16[64,2048]{1,0:T(8,128)(2,1)S(1)} %get-tuple-element.110.n_ref) | copy-start | bytes 786436
  12.8 37.3 %copy-start = (bf16[1,1,2048,768]{3,2,1,0:T(8,128)(2,1)S(1)}, bf16[1,1,2048,768]{3,2,1,0:T(8,128)(2,1)}, u32[]{:S(2)}) copy-start(bf16[1,1,2048,768]{3,2,1,0:T(8,128)(2,1)} %param.13) | copy-start | bytes 9437188
  50.1 8.1 copy-start.22
  58.2 4.2 copy-start.43
  58.2 4.5 copy-start.38
  58.2 32.2 %all-to-all-start.1 = ((bf16[32,16,2048]{2,1,0:T(8,128)(2,1)}), bf16[32,16,2048]{2,1,0:T(8,128)(2,1)S(1)}, u32[]{:S(2)}, u32[]{:S(2)}) async-start(bf16[32,16,2048]{2,1,0:T(8,128)(2,1)} %bitcast.144), calls=%async_computation.1 | async-start | bytes 4194304 | tf_op jit(solution)/shard_map/all_to_all | solution.py:375
  62.7 39.5 %copy-start.11 = (bf16[2048,32]{1,0:T(8,128)(2,1)}, bf16[2048,32]{1,0:T(8,128)(2,1)S(1)}, u32[]{:S(2)}) copy-start(bf16[2048,32]{1,0:T(8,128)(2,1)S(1)} %copy.32.router_ref) | copy-start | bytes 393220
  90.3 12.6 %copy-start.9 = (bf16[32,16,2048]{2,1,0:T(8,128)(2,1)}, bf16[32,16,2048]{2,1,0:T(8,128)(2,1)S(1)}, u32[]{:S(2)}) copy-start(bf16[32,16,2048]{2,1,0:T(8,128)(2,1)S(1)} %all-to-all-done.1) | copy-start | bytes 6291460
  92.7 6.8 collective-permute-start
  102.9 35.9 %all-to-all-start.2 = ((bf16[32,16,2048]{2,1,0:T(8,128)(2,1)}), bf16[32,16,2048]{2,1,0:T(8,128)(2,1)}, u32[]{:S(2)}, u32[]{:S(2)}) async-start(bf16[32,16,2048]{2,1,0:T(8,128)(2,1)} %bitcast.124), calls=%async_computation.2 | async-start | bytes 4194304 | tf_op jit(solution)/shard_map/all_to_all | solution.py:375
  110.9 27.9 %copy-start.1 = (bf16[1,1,2048,768]{3,2,1,0:T(8,128)(2,1)S(1)}, bf16[1,1,2048,768]{3,2,1,0:T(8,128)(2,1)}, u32[]{:S(2)}) copy-start(bf16[1,1,2048,768]{3,2,1,0:T(8,128)(2,1)} %param.13) | copy-start | bytes 9437188
  138.8 1.9 copy-start.4
  140.7 1.9 copy-start.18
  152.1 6.9 copy-start.36
  152.1 34.8 %all-to-all-start.3 = ((bf16[32,16,2048]{2,1,0:T(8,128)(2,1)}), bf16[32,16,2048]{2,1,0:T(8,128)(2,1)}, u32[]{:S(2)}, u32[]{:S(2)}) async-start(bf16[32,16,2048]{2,1,0:T(8,128)(2,1)} %bitcast.125), calls=%async_computation.3 | async-start | bytes 4194304 | tf_op jit(solution)/shard_map/all_to_all | solution.py:375
  187.0 49.6 %copy-start.19 = (bf16[1,1,768,2048]{3,2,1,0:T(8,128)(2,1)S(1)}, bf16[1,1,768,2048]{3,2,1,0:T(8,128)(2,1)}, u32[]{:S(2)}) copy-start(bf16[1,1,768,2048]{3,2,1,0:T(8,128)(2,1)} %param.15) | copy-start | bytes 9437188
  189.8 7.4 collective-permute-start.1
  199.8 36.7 %copy-start.5 = (bf16[1,1,2048,768]{3,2,1,0:T(8,128)(2,1)S(1)}, bf16[1,1,2048,768]{3,2,1,0:T(8,128)(2,1)}, u32[]{:S(2)}) copy-start(bf16[1,1,2048,768]{3,2,1,0:T(8,128)(2,1)} %param.14) | copy-start | bytes 9437188
  236.5 8.1 copy-start.16
  244.6 33.2 %all-to-all-start.5 = ((bf16[32,16,2048]{2,1,0:T(8,128)(2,1)}), bf16[32,16,2048]{2,1,0:T(8,128)(2,1)}, u32[]{:S(2)}, u32[]{:S(2)}) async-start(bf16[32,16,2048]{2,1,0:T(8,128)(2,1)} %bitcast.145), calls=%async_computation.5 | async-start | bytes 4194304 | tf_op jit(solution)/shard_map/all_to_all | solution.py:375
  277.9 49.5 %copy-start.20 = (bf16[1,1,768,2048]{3,2,1,0:T(8,128)(2,1)S(1)}, bf16[1,1,768,2048]{3,2,1,0:T(8,128)(2,1)}, u32[]{:S(2)}) copy-start(bf16[1,1,768,2048]{3,2,1,0:T(8,128)(2,1)} %param.15) | copy-start | bytes 9437188
  280.7 7.4 collective-permute-start.2
  290.7 36.7 %copy-start.6 = (bf16[1,1,2048,768]{3,2,1,0:T(8,128)(2,1)S(1)}, bf16[1,1,2048,768]{3,2,1,0:T(8,128)(2,1)}, u32[]{:S(2)}) copy-start(bf16[1,1,2048,768]{3,2,1,0:T(8,128)(2,1)} %param.14) | copy-start | bytes 9437188
  327.3 8.1 copy-start.23
  335.5 4.2 copy-start.44
  335.5 5.0 copy-start.14
  335.5 32.2 %all-to-all-start.7 = ((bf16[32,16,2048]{2,1,0:T(8,128)(2,1)}), bf16[32,16,2048]{2,1,0:T(8,128)(2,1)S(1)}, u32[]{:S(2)}, u32[]{:S(2)}) async-start(bf16[32,16,2048]{2,1,0:T(8,128)(2,1)} %bitcast.143), calls=%async_computation.7 | async-start | bytes 4194304 | tf_op jit(solution)/shard_map/all_to_all | solution.py:375
  339.7 30.3 %copy-start.31 = (bf16[2048,128]{1,0:T(8,128)(2,1)S(1)}, bf16[2048,128]{1,0:T(8,128)(2,1)}, u32[]{:S(2)}) copy-start(bf16[2048,128]{1,0:T(8,128)(2,1)} %head_ref.3) | copy-start | bytes 1572868
  342.2 27.8 %copy-start.40 = (s32[64,1]{1,0:T(8,128)S(1)}, s32[64,1]{1,0:T(8,128)}, u32[]{:S(2)}) copy-start(s32[64,1]{1,0:T(8,128)} %copy.38.label_ref) | copy-start | bytes 772
  367.6 8.6 copy-start.8
  370.0 12.2 %copy-start.27 = (bf16[64,2048]{1,0:T(8,128)(2,1)}, bf16[64,2048]{1,0:T(8,128)(2,1)S(1)}, u32[]{:S(2)}) copy-start(bf16[64,2048]{1,0:T(8,128)(2,1)S(1)} %shard_map.144.final_ref.refs_0_) | copy-start | bytes 786436
  376.2 34.0 %all-to-all-start.10 = ((bf16[32,16,2048]{2,1,0:T(8,128)(2,1)}), bf16[32,16,2048]{2,1,0:T(8,128)(2,1)S(1)}, u32[]{:S(2)}, u32[]{:S(2)}) async-start(bf16[32,16,2048]{2,1,0:T(8,128)(2,1)} %bitcast.139), calls=%async_computation.10 | async-start | bytes 4194304 | tf_op jit(solution)/shard_map/all_to_all | solution.py:375
  382.2 9.4 %collective-permute-start.3 = (bf16[64,2048]{1,0:T(8,128)(2,1)S(1)}, bf16[64,2048]{1,0:T(8,128)(2,1)S(1)}, u32[]{:S(2)}, u32[]{:S(2)}) collective-permute-start(bf16[64,2048]{1,0:T(8,128)(2,1)S(1)} %shard_map.144.final_ref.refs_0_), channel_id=1, source_target_pairs={{0,32},{32,64},{64,96},{1,33},{33,65},{65,97},{2,34},{34,66},{66,9... | collective-permute-start | bytes 786440 | tf_op jit(solution)/shard_map/ppermute | solution.py:381
  411.5 34.0 %all-to-all-start.8 = ((bf16[32,16,2048]{2,1,0:T(8,128)(2,1)}), bf16[32,16,2048]{2,1,0:T(8,128)(2,1)S(1)}, u32[]{:S(2)}, u32[]{:S(2)}) async-start(bf16[32,16,2048]{2,1,0:T(8,128)(2,1)} %bitcast.136), calls=%async_computation.8 | async-start | bytes 4194304 | tf_op jit(solution)/shard_map/all_to_all | solution.py:375
  417.6 9.7 %copy-start.30 = (bf16[32,16,2048]{2,1,0:T(8,128)(2,1)S(1)}, bf16[32,16,2048]{2,1,0:T(8,128)(2,1)}, u32[]{:S(2)}) copy-start(bf16[32,16,2048]{2,1,0:T(8,128)(2,1)} %copy-done.29) | copy-start | bytes 6291460
  446.8 7.0 copy-start.2
  446.8 35.0 %all-to-all-start.11 = ((bf16[32,16,2048]{2,1,0:T(8,128)(2,1)}), bf16[32,16,2048]{2,1,0:T(8,128)(2,1)}, u32[]{:S(2)}, u32[]{:S(2)}) async-start(bf16[32,16,2048]{2,1,0:T(8,128)(2,1)} %bitcast.141), calls=%async_computation.11 | async-start | bytes 4194304 | tf_op jit(solution)/shard_map/all_to_all | solution.py:375
  453.8 1.9 copy-start.7
  455.7 1.9 copy-start.21
  457.6 1.6 copy-start.25
  481.8 34.2 %all-to-all-start.9 = ((bf16[32,16,2048]{2,1,0:T(8,128)(2,1)}), bf16[32,16,2048]{2,1,0:T(8,128)(2,1)S(1)}, u32[]{:S(2)}, u32[]{:S(2)}) async-start(bf16[32,16,2048]{2,1,0:T(8,128)(2,1)} %bitcast.134), calls=%async_computation.9 | async-start | bytes 4194304 | tf_op jit(solution)/shard_map/all_to_all | solution.py:375
  493.2 5.9 copy-start.15
  497.0 21.4 %copy-start.32 = (bf16[2048,128]{1,0:T(8,128)(2,1)S(1)}, bf16[2048,128]{1,0:T(8,128)(2,1)}, u32[]{:S(2)}) copy-start(bf16[2048,128]{1,0:T(8,128)(2,1)} %head_ref.3) | copy-start | bytes 1572868
  497.0 23.2 %collective-permute-start.4 = (bf16[64,2048]{1,0:T(8,128)(2,1)}, bf16[64,2048]{1,0:T(8,128)(2,1)}, u32[]{:S(2)}, u32[]{:S(2)}) collective-permute-start(bf16[64,2048]{1,0:T(8,128)(2,1)} %shard_map.155), channel_id=1, source_target_pairs={{32,0},{64,32},{96,64},{33,1},{65,33},{97,65},{34,2},{66,34},{98,6... | collective-permute-start | bytes 786440 | tf_op jit(solution)/shard_map/ppermute | solution.py:381
  500.9 17.5 %copy-start.39 = (s32[64,1]{1,0:T(8,128)S(1)}, s32[64,1]{1,0:T(8,128)}, u32[]{:S(2)}) copy-start(s32[64,1]{1,0:T(8,128)} %copy.37.label_ref) | copy-start | bytes 772
  516.0 8.8 copy-start.10
  518.4 6.4 copy-start.28
  524.8 34.0 %all-to-all-start.12 = ((bf16[32,16,2048]{2,1,0:T(8,128)(2,1)}), bf16[32,16,2048]{2,1,0:T(8,128)(2,1)S(1)}, u32[]{:S(2)}, u32[]{:S(2)}) async-start(bf16[32,16,2048]{2,1,0:T(8,128)(2,1)} %bitcast.138), calls=%async_computation.12 | async-start | bytes 4194304 | tf_op jit(solution)/shard_map/all_to_all | solution.py:375
  558.8 17.7 %all-to-all-start.14 = ((bf16[32,64,128]{2,1,0:T(8,128)(2,1)}), bf16[32,64,128]{2,1,0:T(8,128)(2,1)S(1)}, u32[]{:S(2)}, u32[]{:S(2)}) async-start(bf16[32,64,128]{2,1,0:T(8,128)(2,1)} %bitcast.149), calls=%async_computation.14 | async-start | bytes 1048576 | tf_op jit(solution)/shard_map/all_to_all | solution.py:375
  576.5 35.4 %all-to-all-start.13 = ((bf16[32,16,2048]{2,1,0:T(8,128)(2,1)}), bf16[32,16,2048]{2,1,0:T(8,128)(2,1)S(1)}, u32[]{:S(2)}, u32[]{:S(2)}) async-start(bf16[32,16,2048]{2,1,0:T(8,128)(2,1)} %bitcast.132), calls=%async_computation.13 | async-start | bytes 4194304 | tf_op jit(solution)/shard_map/all_to_all | solution.py:375
  593.7 211.9 %copy-start.33 = (bf16[16,2048]{1,0:T(8,128)(2,1)}, bf16[16,2048]{1,0:T(8,128)(2,1)S(1)}, u32[]{:S(2)}) copy-start(bf16[16,2048]{1,0:T(8,128)(2,1)S(1)} %reshape.63.refs_2_.refs_6_) | copy-start | bytes 196612
  614.7 9.8 %collective-permute-start.5 = (bf16[80,2048]{1,0:T(8,128)(2,1)S(1)}, bf16[80,2048]{1,0:T(8,128)(2,1)S(1)}, u32[]{:S(2)}, u32[]{:S(2)}) collective-permute-start(bf16[80,2048]{1,0:T(8,128)(2,1)S(1)} %shard_map.162), channel_id=1, source_target_pairs={{32,0},{64,32},{96,64},{33,1},{65,33},{97,65},{34,2},{66,34},{98,6... | collective-permute-start | bytes 983048 | tf_op jit(solution)/shard_map/ppermute | solution.py:381
  628.0 35.4 %all-to-all-start.15 = ((bf16[32,16,2048]{2,1,0:T(8,128)(2,1)}), bf16[32,16,2048]{2,1,0:T(8,128)(2,1)S(1)}, u32[]{:S(2)}, u32[]{:S(2)}) async-start(bf16[32,16,2048]{2,1,0:T(8,128)(2,1)} %bitcast.142), calls=%async_computation.15 | async-start | bytes 4194304 | tf_op jit(solution)/shard_map/all_to_all | solution.py:375
  675.1 34.0 %all-to-all-start.16 = ((bf16[32,16,2048]{2,1,0:T(8,128)(2,1)}), bf16[32,16,2048]{2,1,0:T(8,128)(2,1)S(1)}, u32[]{:S(2)}, u32[]{:S(2)}) async-start(bf16[32,16,2048]{2,1,0:T(8,128)(2,1)} %bitcast.137), calls=%async_computation.16 | async-start | bytes 4194304 | tf_op jit(solution)/shard_map/all_to_all | solution.py:375
  712.0 9.3 %collective-permute-start.6 = (bf16[80,2048]{1,0:T(8,128)(2,1)S(1)}, bf16[80,2048]{1,0:T(8,128)(2,1)S(1)}, u32[]{:S(2)}, u32[]{:S(2)}) collective-permute-start(bf16[80,2048]{1,0:T(8,128)(2,1)S(1)} %shard_map.167), channel_id=1, source_target_pairs={{32,0},{64,32},{96,64},{33,1},{65,33},{97,65},{34,2},{66,34},{98,6... | collective-permute-start | bytes 983048 | tf_op jit(solution)/shard_map/ppermute | solution.py:381
  724.7 35.2 %all-to-all-start.17 = ((bf16[32,16,2048]{2,1,0:T(8,128)(2,1)}), bf16[32,16,2048]{2,1,0:T(8,128)(2,1)S(1)}, u32[]{:S(2)}, u32[]{:S(2)}) async-start(bf16[32,16,2048]{2,1,0:T(8,128)(2,1)} %bitcast.140), calls=%async_computation.17 | async-start | bytes 4194304 | tf_op jit(solution)/shard_map/all_to_all | solution.py:375
  771.7 34.0 %all-to-all-start.18 = ((bf16[32,16,2048]{2,1,0:T(8,128)(2,1)}), bf16[32,16,2048]{2,1,0:T(8,128)(2,1)S(1)}, u32[]{:S(2)}, u32[]{:S(2)}) async-start(bf16[32,16,2048]{2,1,0:T(8,128)(2,1)} %bitcast.135), calls=%async_computation.18 | async-start | bytes 4194304 | tf_op jit(solution)/shard_map/all_to_all | solution.py:375
  777.7 114.5 %all-gather.3.cloned.1.call-start = ((), (), s32[]{:S(2)}) async-start(), calls=%async_computation.20 | async-start | bytes 6488064 | tf_op jit(solution)/shard_map/all_gather | solution.py:678
  808.6 9.3 %collective-permute-start.7 = (bf16[80,2048]{1,0:T(8,128)(2,1)S(1)}, bf16[80,2048]{1,0:T(8,128)(2,1)S(1)}, u32[]{:S(2)}, u32[]{:S(2)}) collective-permute-start(bf16[80,2048]{1,0:T(8,128)(2,1)S(1)} %shard_map.172), channel_id=1, source_target_pairs={{32,0},{64,32},{96,64},{33,1},{65,33},{97,65},{34,2},{66,34},{98,6... | collective-permute-start | bytes 983048 | tf_op jit(solution)/shard_map/ppermute | solution.py:381
  817.9 3.4 copy-start.34
  825.8 37.9 %all-to-all-start.19 = ((bf16[32,16,2048]{2,1,0:T(8,128)(2,1)}), bf16[32,16,2048]{2,1,0:T(8,128)(2,1)S(1)}, u32[]{:S(2)}, u32[]{:S(2)}) async-start(bf16[32,16,2048]{2,1,0:T(8,128)(2,1)} %bitcast.133), calls=%async_computation.19 | async-start | bytes 4194304 | tf_op jit(solution)/shard_map/all_to_all | solution.py:375
  892.2 2.8 copy-start.26
  (7 other events, 7.3 us)
Sparse Core Ops, SparseCore 0:
  826.0 66.1 all-gather.2

commit v3 on v2

--- a/solution.py
+++ b/solution.py
@@ -167,12 +167,15 @@
 
 def turn_kernel(sec, wg_ref, wu_ref, wd_ref, dep_ref, gu_ref, down_ref):
     tile = wg_ref.shape[1]
-    gu_ref[:tile] = wg_ref[...].T
-    gu_ref[tile:] = wu_ref[...].T
-    down_ref[...] = wd_ref[...].T
-
-
-def combine_fwd_kernel(sec, ret_ref, h_ref, phl_ref, out_ref):
+    blocks, _, chunk = gu_ref.shape
+    for block in range(blocks):
+        gu_ref[block, :tile] = wg_ref[block * chunk : (block + 1) * chunk].T
+        gu_ref[block, tile:] = wu_ref[block * chunk : (block + 1) * chunk].T
+    down_ref[0] = wd_ref[...].T
+
+
+def combine_fwd_kernel(sec, ret_ref, h_ref, phl_ref, *refs):
+    out_ref = refs[-1]
     rows = h_ref.shape[0]
     both = nn(phl_ref[...], ret_ref[...])
     out_ref[...] = (h_ref[...].astype(F32) + (both[:rows] + both[rows:])).astype(BF)
@@ -227,7 +230,7 @@
 def route_bwd_kernel(tick, slots, n, micros, sec, g_ref, *refs):
     r_refs, h_refs, p_refs, c_refs = (refs[i * n : (i + 1) * n] for i in range(4))
     router_t_ref, acc_in_ref = refs[4 * n : 4 * n + 2]
-    carry_refs, (gn_ref, acc_ref) = refs[4 * n + 2 : -2], refs[-2:]
+    gn_ref, acc_ref = refs[-2:]
     flag = sec[0] == sec[1] - tick
     micro = tick - (sec[1] - 1 - sec[0])
     active = (micro >= 0) & (micro < micros)
@@ -241,11 +244,7 @@
     gn_ref[...] = nn(grad_route, router_t_ref[...])
     normed = normalize(pick(flag, h_refs))[2]
     total = acc_in_ref[...] + jnp.where(active, tn(grad_route, normed), 0.0)
-    if carry_refs:
-        acc_ref[:experts] = total.astype(BF)
-        acc_ref[experts:] = carried(sec, grad.shape[0], carry_refs)
-    else:
-        acc_ref[...] = total
+    acc_ref[...] = total.astype(acc_ref.dtype)
 
 
 def again_kernel(tick, n, sec, *refs):
@@ -257,8 +256,8 @@
     up = nn(packed, wu_ref[...])
     sigmoid = jax.nn.sigmoid(gate)
     silu = gate * sigmoid
-    a1_ref[...] = (up * sigmoid * (1.0 + gate * (1.0 - sigmoid))).astype(BF)
-    a2_ref[...] = silu.astype(BF)
+    a1_ref[0] = (up * sigmoid * (1.0 + gate * (1.0 - sigmoid))).astype(BF)
+    a2_ref[0] = silu.astype(BF)
     ht_ref[0] = (silu * up).astype(BF).T
 
     @pl.when(pl.program_id(0) == 0)
@@ -267,19 +266,15 @@
 
 
 def expert_bwd_kernel(first, sec, dy_ref, wd_ref, a1_ref, a2_ref, wgu_ref, *refs):
-    gg_ref, gu_ref, dys_ref, out_ref, both_ref = refs[-5:]
+    gg_ref, gu_ref, out_ref, both_ref = refs[-4:]
     step = pl.program_id(0)
-    tile = wd_ref.shape[1]
-
-    @pl.when(step == 0)
-    def _():
-        dys_ref[0] = dy_ref[...]
+    tile = wd_ref.shape[2]
 
     @pl.when(step < first)
     def _():
-        grad_hidden = nn(dy_ref[...], wd_ref[...])
-        gg = (grad_hidden * a1_ref[...].astype(F32)).astype(BF)
-        gu = (grad_hidden * a2_ref[...].astype(F32)).astype(BF)
+        grad_hidden = nn(dy_ref[...], wd_ref[0])
+        gg = (grad_hidden * a1_ref[0].astype(F32)).astype(BF)
+        gu = (grad_hidden * a2_ref[0].astype(F32)).astype(BF)
         gg_ref[0] = gg
         gu_ref[0] = gu
         at = pl.multiple_of(step * 2 * tile, tile)
@@ -288,71 +283,79 @@
 
     @pl.when(step >= first)
     def _():
-        out_ref[...] = nn(both_ref[...], wgu_ref[...]).astype(BF)
-
-
-def earlier_kernel(sec, xt_ref, gg_ref, gu_ref, ht_ref, dy_ref, gate_ref, up_ref, down_ref, dy_now):
+        out_ref[...] = nn(both_ref[...], wgu_ref[0]).astype(BF)
+
+
+def earlier_kernel(sec, xt_ref, gg_ref, gu_ref, ht_ref, *refs):
+    arrived = refs[:-4]
+    gate_ref, up_ref, down_ref, rows_ref = refs[-4:]
     done = sec[0] != 0
 
     @pl.when(pl.program_id(0) == 0)
     def _():
-        dy_now[...] = jnp.where(done, dy_ref[1], jnp.zeros((), BF))
+        for tick in range(len(arrived)):
+            if tick > 0:
+
+                @pl.when(sec[0] == sec[1] - tick)
+                def _():
+                    rows_ref[1] = arrived[tick][...]
+
+            @pl.when(sec[0] == sec[1] - 1 - tick)
+            def _():
+                rows_ref[0] = arrived[tick][...]
+
+        @pl.when(sec[0] == 0)
+        def _():
+            rows_ref[1] = jnp.zeros(rows_ref.shape[1:], BF)
 
     gg = jnp.where(done, gg_ref[1], jnp.zeros((), BF))
     gu = jnp.where(done, gu_ref[1], jnp.zeros((), BF))
     gate_ref[...] = (nn(xt_ref[0], gg_ref[0]) + nn(xt_ref[1], gg)).astype(BF)
     up_ref[...] = (nn(xt_ref[0], gu_ref[0]) + nn(xt_ref[1], gu)).astype(BF)
-    down_ref[...] = (nn(ht_ref[0], dy_ref[0]) + nn(ht_ref[1], dy_now[...])).astype(BF)
-
-
-def final_kernel(sec, dy_ref, wd_ref, a1_ref, a2_ref, xt_ref, ht_ref, *refs):
-    gate_old, up_old, down_old, gate_ref, up_ref, down_ref, dy_now = refs
+    down_ref[...] = (nn(ht_ref[0], rows_ref[0]) + nn(ht_ref[1], rows_ref[1])).astype(BF)
+
+
+def final_kernel(first, sec, dy_ref, wd_ref, a1_ref, a2_ref, ht_ref, xt_ref, *refs):
+    gate_old, up_old, down_old = refs[:3]
+    gate_ref, up_ref, down_ref, dy_now, gg_all, gu_all = refs[-6:]
     mine = sec[0] == 0
-
-    @pl.when(pl.program_id(0) == 0)
+    step = pl.program_id(0)
+    tile = wd_ref.shape[2]
+
+    @pl.when(step == 0)
     def _():
         dy_now[...] = jnp.where(mine, dy_ref[...], jnp.zeros((), BF))
 
-    grad_hidden = nn(dy_now[...], wd_ref[...])
-    gg = (grad_hidden * a1_ref[...].astype(F32)).astype(BF)
-    gu = (grad_hidden * a2_ref[...].astype(F32)).astype(BF)
-    gate_ref[...] = (gate_old[...].astype(F32) + nn(xt_ref[0], gg)).astype(BF)
-    up_ref[...] = (up_old[...].astype(F32) + nn(xt_ref[0], gu)).astype(BF)
-    down_ref[...] = (down_old[...].astype(F32) + nn(ht_ref[0], dy_now[...])).astype(BF)
-
-
-def tail_kernel(held, sec, in_ref, router_ref, head_ref, loss_ref):
-    blocks = in_ref.shape[0]
-    experts = router_ref.shape[0]
-    total = in_ref[0, :experts].astype(F32)
-    for block in range(1, blocks):
-        total = total + in_ref[block, :experts].astype(F32)
-    step = pl.program_id(0)
-
-    @pl.when(step == 0)
-    def _():
-        router_ref[...] = total
-
-    @pl.when(step > 0)
-    def _():
-        router_ref[...] += total
-
-    for block in range(blocks):
-        rest = in_ref[block, experts:].astype(F32)
+    @pl.when(step < first)
+    def _():
+        grad_hidden = nn(dy_now[...], wd_ref[0])
+        cols = pl.ds(pl.multiple_of(step * tile, tile), tile)
+        gg_all[:, cols] = (grad_hidden * a1_ref[0].astype(F32)).astype(BF)
+        gu_all[:, cols] = (grad_hidden * a2_ref[0].astype(F32)).astype(BF)
+        down_ref[...] = (down_old[...].astype(F32) + nn(ht_ref[0], dy_now[...])).astype(BF)
+
+    @pl.when(step >= first)
+    def _():
+        gate_ref[...] = (gate_old[...].astype(F32) + nn(xt_ref[0], gg_all[...])).astype(BF)
+        up_ref[...] = (up_old[...].astype(F32) + nn(xt_ref[0], gu_all[...])).astype(BF)
+
+
+def head_tail_kernel(held, sec, in_ref, head_ref, loss_ref):
+    for block in range(in_ref.shape[0]):
+        rest = in_ref[block].astype(F32)
         head_ref[block] = rest[:held] + rest[held : 2 * held]
         loss_ref[block : block + 1] = rest[2 * held : 2 * held + 1, : loss_ref.shape[1]]
 
 
-def carried(sec, rows, refs):
-    own = refs[0][...]
-    if len(refs) == 1:
-        return own
-    return jnp.where(sec[0] == sec[1] - 1, own, refs[1][rows:])
+def tail_kernel(sec, in_ref, router_ref):
+    total = in_ref[0].astype(F32)
+    for block in range(1, in_ref.shape[0]):
+        total = total + in_ref[block].astype(F32)
+    router_ref[...] = total
 
 
 def combine_bwd_kernel(tick, n, sec, ret_ref, pt_ref, gn_ref, g_ref, *refs):
-    h_refs, carry_refs, (out_ref, sum_ref) = refs[:n], refs[n:-2], refs[-2:]
-    rows = g_ref.shape[0]
+    h_refs, (out_ref, sum_ref) = refs[:n], refs[-2:]
     step = pl.program_id(0)
     chunk = ret_ref.shape[1]
     cols = pl.ds(pl.multiple_of(step * chunk, chunk), chunk)
@@ -364,11 +367,9 @@
         grad_normed = sum_ref[...] + gn_ref[...]
         normed_f = hidden_f * inv_rms
         mean = jnp.mean(grad_normed * normed_f, axis=-1, keepdims=True)
-        out_ref[:rows] = (
+        out_ref[...] = (
             g_ref[...].astype(F32) + inv_rms * (grad_normed - normed_f * mean)
         ).astype(BF)
-        if carry_refs:
-            out_ref[rows:] = carried(sec, rows, carry_refs)
 
 
 def to_owners(rows):
@@ -403,11 +404,12 @@
     buf_block = pl.BlockSpec((packed, chunk), lambda i, s: (0, i))
     in_block = pl.BlockSpec((width, tile), lambda i, s: (0, i))
     down_block = pl.BlockSpec((tile, width), lambda i, s: (i, 0))
-    act_block = pl.BlockSpec((packed, tile), lambda i, s: (0, i))
+    act_block = pl.BlockSpec((1, packed, tile), lambda i, s: (i, 0, 0))
     row_full = sds((rows, width), BF)
     buf_full = sds((packed, width), BF)
     buf_out = pltpu.HBM((packed, width), BF)
     wide_chunk = 1024
+    chunk_b = 512
     late_block = pl.BlockSpec((packed, wide_chunk), lambda i, s: (0, jnp.maximum(i - steps, 0)))
     anywhere = pl.BlockSpec(memory_space=pl.ANY)
     matmul = 2.0 * packed * width * ffe
@@ -456,28 +458,14 @@
             [whole(two), whole(wide), whole(wide)],
             cost=2 * rows * width * experts,
         )
-        if tick == 1:
-            turned_gu, turned_down = run(
-                turn_kernel,
-                (sec, *far([gate_w, up_w, down_w, outgoing])),
-                [in_block, in_block, down_block, anywhere],
-                [pltpu.HBM((2 * ffe, width), BF), pltpu.HBM((width, ffe), BF)],
-                [pl.BlockSpec((2 * tile, width), lambda i, s: (i, 0)), in_block],
-                grid=(steps,),
-                cost=matmul,
-            )
-            after = (turned_gu,)
-        else:
-            after = ()
         [results] = run(
             functools.partial(expert_fwd_kernel, steps),
-            (sec, arrived, gate_w, up_w, down_w, *far(after)),
+            (sec, arrived, gate_w, up_w, down_w),
             [
                 whole(buf_full),
                 pl.BlockSpec((width, tile), lambda i, s: (0, jnp.minimum(i, steps - 1))),
                 pl.BlockSpec((width, tile), lambda i, s: (0, jnp.minimum(i, steps - 1))),
                 pl.BlockSpec((ffe, wide_chunk), lambda i, s: (0, jnp.maximum(i - steps, 0))),
-                *[anywhere for _ in after],
             ],
             [buf_out],
             [late_block],
@@ -487,10 +475,27 @@
             room=24,
         )
         returned = to_owners(results)
+        after = ()
+        if tick == 0:
+            after = turned_gu, turned_down = run(
+                turn_kernel,
+                (sec, *far([gate_w, up_w, down_w, results])),
+                [in_block, in_block, down_block, anywhere],
+                [
+                    pltpu.HBM((width // wide_chunk, 2 * ffe, wide_chunk), BF),
+                    pltpu.HBM((steps, width, tile), BF),
+                ],
+                [
+                    pl.BlockSpec((width // wide_chunk, 2 * tile, wide_chunk), lambda i, s: (0, i, 0)),
+                    pl.BlockSpec((1, width, tile), lambda i, s: (i, 0, 0)),
+                ],
+                grid=(steps,),
+                cost=matmul,
+            )
         [layer_out] = run(
             combine_fwd_kernel,
-            (sec, returned, *far([layer_in, probs_two])),
-            [buf_block, row_block, whole(two)],
+            (sec, returned, *far([layer_in, probs_two, *after])),
+            [buf_block, row_block, whole(two), *[anywhere for _ in after]],
             [row_full],
             [row_block],
             grid=(col_steps,),
@@ -522,6 +527,7 @@
     classes = class_head.shape[1]
     router_sum = jnp.zeros((experts, width), F32)
     store = None
+    arrivals = []
     for tick in range(ticks):
         at = [
             s_num + tick - (sections - 1 - s_num)
@@ -568,8 +574,7 @@
         wide_f = sds((rows, width), F32)
         acc_full = sds((experts, width), F32)
         if last:
-            route_args = (*route_args, own, incoming)
-            acc_full = sds((experts + carry_rows, width), BF)
+            acc_full = sds((experts, width), BF)
         grad_normed, router_sum = run(
             functools.partial(route_bwd_kernel, tick, slots, count, micros),
             (sec, *far(route_args)),
@@ -578,19 +583,19 @@
             [whole(wide_f), whole(acc_full)],
             cost=2 * rows * packed * width,
         )
-        act = sds((packed, ffe), BF)
+        act = sds((steps, packed, tile), BF)
         stores = [
             sds((micros + 1, ffe, packed), BF),
             sds((micros + 1, width, packed), BF),
             sds((micros + 1, packed, ffe), BF),
             sds((micros + 1, packed, ffe), BF),
-            sds((micros + 1, packed, width), BF),
         ]
         old = [] if store is None else list(store[:2])
+        deps = far([carry]) if tick == 3 else far(earlier) if last else []
         a1, a2, hidden_t, packed_t = run(
             functools.partial(again_kernel, tick, count),
-            (sec, *far([c[0] for c in cands]), *far([gate_w, up_w]), *far(old)),
-            [whole(buf_full)] * count + [in_block, in_block] + [anywhere] * len(old),
+            (sec, *far([c[0] for c in cands]), *far([gate_w, up_w]), *far(old), *deps),
+            [whole(buf_full)] * count + [in_block, in_block] + [anywhere] * len(old + deps),
             [far_out(act), far_out(act), *[far_out(a) for a in stores[:2]]],
             [
                 act_block,
@@ -603,17 +608,86 @@
             cost=2 * matmul,
             room=28,
         )
-        if tick == 1:
+        if last:
+            break
+        old = [] if store is None else list(store[2:])
+        args = [arrived, turned_down, a1, a2, turned_gu]
+        early = lambda i: jnp.minimum(i, steps - 1)
+        got = run(
+            functools.partial(expert_bwd_kernel, steps),
+            (sec, arrived, *far([turned_down, a1, a2, turned_gu, *old])),
+            [
+                whole(buf_full),
+                pl.BlockSpec((1, width, tile), lambda i, s: (early(i), 0, 0)),
+                pl.BlockSpec((1, packed, tile), lambda i, s: (early(i), 0, 0)),
+                pl.BlockSpec((1, packed, tile), lambda i, s: (early(i), 0, 0)),
+                pl.BlockSpec((1, 2 * ffe, wide_chunk), lambda i, s: (jnp.maximum(i - steps, 0), 0, 0)),
+                *[anywhere] * len(old),
+            ],
+            [*[far_out(a) for a in stores[2:]], buf_out],
+            [
+                slot_block((packed, tile), lambda i: (0, early(i))),
+                slot_block((packed, tile), lambda i: (0, early(i))),
+                late_block,
+            ],
+            grid=(steps + width // wide_chunk,),
+            scratch=[pltpu.VMEM((packed, 2 * ffe), BF)],
+            room=32,
+            aliases={1 + len(args) + i: i for i in range(len(old))},
+            cost=3 * matmul,
+        )
+        store = (hidden_t, packed_t, *got[:2])
+        returned = to_owners(got[2])
+        arrivals.append(arrived)
+        before = []
+        if tick + 2 == ticks:
+            both_slots = lambda shape, place: pl.BlockSpec((micros, *shape), lambda i, s: (0, *place(i)))
+            up_tile = lambda i: (i, 0)
+            side_tile = lambda i: (0, i)
+            stay = lambda i: (0, 0)
+            grad_shapes = [sds((width, ffe), BF), sds((width, ffe), BF), sds((ffe, width), BF)]
+            earlier = run(
+                earlier_kernel,
+                (sec, *far([packed_t, store[2], store[3], hidden_t, *arrivals])),
+                [
+                    both_slots((width, packed), stay),
+                    both_slots((packed, tile), side_tile),
+                    both_slots((packed, tile), side_tile),
+                    both_slots((tile, packed), up_tile),
+                    *[whole(buf_full) for _ in arrivals],
+                ],
+                [far_out(a) for a in grad_shapes],
+                [in_block, in_block, down_block],
+                grid=(steps,),
+                scratch=[pltpu.VMEM((micros, packed, width), BF)],
+                cost=6 * matmul,
+                room=44,
+            )
+            before = earlier
+        [grad_in] = run(
+            functools.partial(combine_bwd_kernel, tick, count),
+            (sec, returned, places, *far([grad_normed, gsel, *[c[2] for c in cands], *before])),
+            [buf_block, place_block(micro_of), whole(wide_f), whole(row_full)]
+            + [whole(row_full)] * count
+            + [anywhere] * len(before),
+            [row_full],
+            [whole(row_full)],
+            grid=(col_steps,),
+            scratch=[pltpu.VMEM((rows, width), F32)],
+            cost=2 * rows * packed * width,
+        )
+        if tick == 2:
             head_full = sds((width, classes), BF)
             head_args = [part for final in finals for part in (final[0], final[2])]
             [head_term] = run(
                 head_sum_kernel,
-                (sec, *far(head_args), *far([a1])),
+                (sec, *far(head_args), *far([grad_normed])),
                 [*[whole(a) for a in head_args], anywhere],
                 [far_out(head_full)],
                 [whole(head_full)],
                 cost=4 * rows * width * classes,
             )
+            head_term, _ = lax.optimization_barrier((head_term, grad_in))
             pieces = to_owners(head_term)
             piece_full = sds((2 * share, classes), BF)
             [piece] = run(
@@ -626,120 +700,71 @@
             loss_pair = jnp.stack(hi_lo(sum(final[3][0, 0] for final in finals)))
             flat = jnp.concatenate([piece.reshape(-1), loss_pair])
             own = jnp.pad(flat, (0, carry_rows * width - flat.size)).reshape(carry_rows, width)
-        if last:
-            break
-        old = [] if store is None else list(store[2:])
-        args = [arrived, turned_down, a1, a2, turned_gu]
-        early = lambda i: jnp.minimum(i, steps - 1)
-        got = run(
-            functools.partial(expert_bwd_kernel, steps),
-            (sec, arrived, *far([turned_down, a1, a2, turned_gu, *old])),
-            [
-                whole(buf_full),
-                pl.BlockSpec((width, tile), lambda i, s: (0, early(i))),
-                pl.BlockSpec((packed, tile), lambda i, s: (0, early(i))),
-                pl.BlockSpec((packed, tile), lambda i, s: (0, early(i))),
-                pl.BlockSpec(
-                    (2 * ffe, wide_chunk), lambda i, s: (0, jnp.maximum(i - steps, 0))
-                ),
-                *[anywhere] * len(old),
-            ],
-            [*[far_out(a) for a in stores[2:]], buf_out],
-            [
-                slot_block((packed, tile), lambda i: (0, early(i))),
-                slot_block((packed, tile), lambda i: (0, early(i))),
-                slot_block((packed, width), lambda i: (0, 0)),
-                late_block,
-            ],
-            grid=(steps + width // wide_chunk,),
-            scratch=[pltpu.VMEM((packed, 2 * ffe), BF)],
-            room=32,
-            aliases={1 + len(args) + i: i for i in range(len(old))},
-            cost=3 * matmul,
-        )
-        store = (hidden_t, packed_t, *got[:3])
-        returned = to_owners(got[3])
-        carry = [] if tick == 0 else [own] if tick == 1 else [own, incoming]
-        grad_full = sds((rows + (carry_rows if carry else 0), width), BF)
-        [grad_in] = run(
-            functools.partial(combine_bwd_kernel, tick, count),
-            (sec, returned, places, *far([grad_normed, gsel, *[c[2] for c in cands]]), *carry),
-            [buf_block, place_block(micro_of), whole(wide_f), whole(row_full)]
-            + [whole(row_full)] * count
-            + [whole(a) for a in carry],
-            [grad_full],
-            [whole(grad_full)],
-            grid=(col_steps,),
-            scratch=[pltpu.VMEM((rows, width), F32)],
-            cost=2 * rows * packed * width,
-        )
+            others = [lax.ppermute(own, "section", [(sections - 1, t)]) for t in range(sections - 1)]
+            carry = jnp.where(section == sections - 1, own, sum(others))
+            carry_all = lax.all_gather(carry, plane, axis=0, tiled=False)
         incoming = from_behind(grad_in, "section", -1)
 
     everyone = lax.all_gather(router_sum, plane, axis=0, tiled=False)
     held = share * classes // width
     router_full, head_full = sds((experts, width), F32), sds((experts, held, width), F32)
     loss_full = sds((experts, 128), F32)
-    router_rows, head_rows, loss_rows = run(
-        functools.partial(tail_kernel, held),
-        (sec, everyone),
-        [pl.BlockSpec((8, *everyone.shape[1:]), lambda i, s: (i, 0, 0))],
-        [router_full, head_full, loss_full],
+    head_rows, loss_rows = run(
+        functools.partial(head_tail_kernel, held),
+        (sec, *far([carry_all])),
+        [pl.BlockSpec((8, *carry_all.shape[1:]), lambda i, s: (i, 0, 0))],
+        [head_full, loss_full],
         [
-            whole(router_full),
             pl.BlockSpec((8, held, width), lambda i, s: (i, 0, 0)),
             pl.BlockSpec((8, 128), lambda i, s: (i, 0)),
         ],
         grid=(experts // 8,),
     )
-    router_out = router_rows.T[None]
     head_total = head_rows.reshape(width, classes)
     mean_loss = jnp.sum(loss_rows[:, :2]) / (micros * rows * experts)
-
-    both_slots = lambda shape, place: pl.BlockSpec((micros, *shape), lambda i, s: (0, *place(i)))
+    [router_rows] = run(
+        tail_kernel,
+        (sec, *far([everyone])),
+        [pl.BlockSpec((*everyone.shape[:2], chunk_b), lambda i, s: (0, 0, i))],
+        [router_full],
+        [pl.BlockSpec((experts, chunk_b), lambda i, s: (0, i))],
+        grid=(width // chunk_b,),
+    )
+    router_out = router_rows.T[None]
+
     next_slot = lambda shape, place: pl.BlockSpec((1, *shape), lambda i, s: (1, *place(i)))
-    up_tile = lambda i: (i, 0)
-    side_tile = lambda i: (0, i)
-    stay = lambda i: (0, 0)
-    grad_shapes = [sds((width, ffe), BF), sds((width, ffe), BF), sds((ffe, width), BF)]
-    earlier = run(
-        earlier_kernel,
-        (sec, *far([packed_t, store[2], store[3], hidden_t, store[4]])),
-        [
-            both_slots((width, packed), stay),
-            both_slots((packed, tile), side_tile),
-            both_slots((packed, tile), side_tile),
-            both_slots((tile, packed), up_tile),
-            both_slots((packed, width), stay),
-        ],
-        [far_out(a) for a in grad_shapes],
-        [in_block, in_block, down_block],
-        grid=(steps,),
-        scratch=[pltpu.VMEM((packed, width), BF)],
-        cost=6 * matmul,
-        room=32,
-    )
+    early = lambda i: jnp.minimum(i, steps - 1)
+    late = lambda i: jnp.maximum(i - steps, 0)
+    down_early = pl.BlockSpec((tile, width), lambda i, s: (early(i), 0))
+    act_early = pl.BlockSpec((1, packed, tile), lambda i, s: (early(i), 0, 0))
+    in_late = pl.BlockSpec((chunk_b, ffe), lambda i, s: (late(i), 0))
     grad_gate, grad_up, grad_down = run(
-        final_kernel,
+        functools.partial(final_kernel, steps),
         (
             sec,
             arrived,
-            *far([turned_down, a1, a2, packed_t, hidden_t, *earlier]),
+            *far([turned_down, a1, a2, hidden_t, packed_t, *earlier, head_total]),
         ),
         [
             whole(buf_full),
-            in_block,
-            act_block,
-            act_block,
-            next_slot((width, packed), stay),
-            next_slot((tile, packed), up_tile),
-            in_block,
-            in_block,
-            down_block,
+            pl.BlockSpec((1, width, tile), lambda i, s: (early(i), 0, 0)),
+            act_early,
+            act_early,
+            next_slot((tile, packed), lambda i: (early(i), 0)),
+            next_slot((chunk_b, packed), lambda i: (late(i), 0)),
+            in_late,
+            in_late,
+            down_early,
+            anywhere,
         ],
         grad_shapes,
-        [in_block, in_block, down_block],
-        grid=(steps,),
-        scratch=[pltpu.VMEM((packed, width), BF)],
+        [in_late, in_late, down_early],
+        grid=(steps + width // chunk_b,),
+        scratch=[
+            pltpu.VMEM((packed, width), BF),
+            pltpu.VMEM((packed, ffe), BF),
+            pltpu.VMEM((packed, ffe), BF),
+        ],
         cost=4 * matmul,
         room=32,
     )

time: 920 us -> 904 us (0.983)
  waiting for transfers between devices: 340 us -> 301 us
  blocking collectives: 111 us -> 147 us
    all_to_all x17 -> x16, waiting for transfers between devices: 289 us -> 249 us  [to_owners(): return lax.all_to_all(rows, plane, split_axis=0, concat_axis=0, tiled=True)]
    all_to_all x3 -> x4, blocking collectives: 111 us -> 147 us  [to_owners(): return lax.all_to_all(rows, plane, split_axis=0, concat_axis=0, tiled=True)]
    all_to_all x17 -> x16, starting transfers between devices: 108 us -> 95.7 us  [to_owners(): return lax.all_to_all(rows, plane, split_axis=0, concat_axis=0, tiled=True)]
    unnamed x91 -> x93, local copies, waits for them, and re-layouts: 20.2 us -> 12.9 us
    pallas_call x52 -> x53, Pallas kernels: 282 us -> 285 us  [run(): pl.pallas_call(kernel, grid_spec=pltpu.PrefetchScalarGridSpec(num_scalar_...]
  transfers between devices with their start and end apart: 26 -> 29, of which waited for: 24 -> 24; matrix products, arithmetic and copies ran while one was open for 1% -> 1% of each run, Pallas kernels for 19% -> 21%
where the time goes in v3:
time: 904 us; the launch traced here: 893 us
  waiting for transfers between devices  301 us (33%)
  Pallas kernels  285 us (32%)
  blocking collectives  147 us (16%)
  starting transfers between devices  120 us (13%)
  local copies, waits for them, and re-layouts  20.6 us (2%)
  between operations  17.9 us (2%)
    pallas_call x53, Pallas kernels, run(): pl.pallas_call(kernel, grid_spec=pltpu.PrefetchScalarGridSpec(num_scalar_...  285 us
    all_to_all x16, waiting for transfers between devices, to_owners(): return lax.all_to_all(rows, plane, split_axis=0, concat_axis=0, tiled=True)  249 us
    all_to_all x4, blocking collectives, to_owners(): return lax.all_to_all(rows, plane, split_axis=0, concat_axis=0, tiled=True)  147 us
    all_to_all x16, starting transfers between devices, to_owners(): return lax.all_to_all(rows, plane, split_axis=0, concat_axis=0, tiled=True)  95.7 us
    ppermute x8, waiting for transfers between devices, from_behind(): return lax.ppermute(block, axis, route)  38 us
    ppermute x8, starting transfers between devices, from_behind(): return lax.ppermute(block, axis, route)  21.2 us
  transfers between devices with their start and end apart: 29, of which 24 were waited for; matrix products, arithmetic and copies ran while one was open for 1% of the time, Pallas kernels for 21%

profile of v3, /device:TPU:1, one launch (start us, length us, event | category | flops | bytes accessed | tf_op | source)
XLA Modules:
  0.0 892.5 jit_solution(7493189374972266593)
XLA Ops:
  12.8 37.3 %all_to_all.220 = bf16[32,16,2048]{2,1,0:T(8,128)(2,1)S(1)} all-to-all(bf16[32,16,2048]{2,1,0:T(8,128)(2,1)} %bitcast.154), channel_id=1, replica_groups=mesh['section'=4,'expert'=4,'dp'=8] {'expert','dp'}, dimensions={0} | all-to-all | bytes 4194304 | tf_op jit(solution)/shard_map/all_to_all | solution.py:376
  50.1 8.1 shard_map.129.dep_ref
  58.2 4.2 all-to-all-start.1
  64.5 10.1 %shard_map.131 = (bf16[2,1536,1024]{2,1,0:T(8,128)(2,1)}, bf16[3,2048,256]{2,1,0:T(8,128)(2,1)}) custom-call(s32[2]{0:T(128)S(1)} %pad_add_fusion.sec, bf16[2048,768]{1,0:T(8,128)(2,1)} %bitcast.68, bf16[2048,768]{1,0:T(8,128)(2,1)} %bitcast.79, bf16[768,2048]{1,0:T(8,128)(2,1)} %bitcast.114, bf16[512,2048]{1,0:T(8,128)(2,1)} %shard_map.129.dep_ref), custom_call_target="tpu_custom_call" | custom-call | flops 1610612736 | bytes 11534336 | tf_op jit(solution)/shard_map/pallas_call | solution.py:59
  74.6 15.8 %all-to-all-done.1 = bf16[32,16,2048]{2,1,0:T(8,128)(2,1)S(1)} async-done(((bf16[32,16,2048]{2,1,0:T(8,128)(2,1)}), bf16[32,16,2048]{2,1,0:T(8,128)(2,1)S(1)}, u32[]{:S(2)}, u32[]{:S(2)}) %all-to-all-start.1) | async-done | bytes 2097184 | tf_op jit(solution)/shard_map/all_to_all | solution.py:376
  103.2 36.6 %all_to_all.221 = bf16[32,16,2048]{2,1,0:T(8,128)(2,1)S(1)} all-to-all(bf16[32,16,2048]{2,1,0:T(8,128)(2,1)} %bitcast.153), channel_id=1, replica_groups=mesh['section'=4,'expert'=4,'dp'=8] {'expert','dp'}, dimensions={0} | all-to-all | bytes 4194304 | tf_op jit(solution)/shard_map/all_to_all | solution.py:376
  139.8 8.1 shard_map.134
  147.9 4.9 all-to-all-start.3
  155.7 25.1 %all-to-all-done.3 = bf16[32,16,2048]{2,1,0:T(8,128)(2,1)} async-done(((bf16[32,16,2048]{2,1,0:T(8,128)(2,1)}), bf16[32,16,2048]{2,1,0:T(8,128)(2,1)}, u32[]{:S(2)}, u32[]{:S(2)}) %all-to-all-start.3) | async-done | bytes 2097184 | tf_op jit(solution)/shard_map/all_to_all | solution.py:376
  193.7 36.7 %all_to_all.222 = bf16[32,16,2048]{2,1,0:T(8,128)(2,1)S(1)} all-to-all(bf16[32,16,2048]{2,1,0:T(8,128)(2,1)} %bitcast.155), channel_id=1, replica_groups=mesh['section'=4,'expert'=4,'dp'=8] {'expert','dp'}, dimensions={0} | all-to-all | bytes 4194304 | tf_op jit(solution)/shard_map/all_to_all | solution.py:376
  230.4 8.1 shard_map.138
  238.5 5.1 all-to-all-start.5
  246.4 24.9 %all-to-all-done.5 = bf16[32,16,2048]{2,1,0:T(8,128)(2,1)} async-done(((bf16[32,16,2048]{2,1,0:T(8,128)(2,1)}), bf16[32,16,2048]{2,1,0:T(8,128)(2,1)}, u32[]{:S(2)}, u32[]{:S(2)}) %all-to-all-start.5) | async-done | bytes 2097184 | tf_op jit(solution)/shard_map/all_to_all | solution.py:376
  274.2 4.1 collective-permute-start.2
  284.3 36.7 %all_to_all.223 = bf16[32,16,2048]{2,1,0:T(8,128)(2,1)S(1)} all-to-all(bf16[32,16,2048]{2,1,0:T(8,128)(2,1)} %bitcast.156), channel_id=1, replica_groups=mesh['section'=4,'expert'=4,'dp'=8] {'expert','dp'}, dimensions={0} | all-to-all | bytes 4194304 | tf_op jit(solution)/shard_map/all_to_all | solution.py:376
  320.9 8.1 shard_map.142
  329.0 4.2 all-to-all-start.7
  335.8 25.4 %all-to-all-done.7 = bf16[32,16,2048]{2,1,0:T(8,128)(2,1)S(1)} async-done(((bf16[32,16,2048]{2,1,0:T(8,128)(2,1)}), bf16[32,16,2048]{2,1,0:T(8,128)(2,1)S(1)}, u32[]{:S(2)}, u32[]{:S(2)}) %all-to-all-start.7) | async-done | bytes 2097184 | tf_op jit(solution)/shard_map/all_to_all | solution.py:376
  369.7 6.0 all-to-all-start.10
  379.9 5.3 collective-permute-done.3.refs_0_
  387.9 15.9 %all-to-all-done.10 = bf16[32,16,2048]{2,1,0:T(8,128)(2,1)S(1)} async-done(((bf16[32,16,2048]{2,1,0:T(8,128)(2,1)}), bf16[32,16,2048]{2,1,0:T(8,128)(2,1)S(1)}, u32[]{:S(2)}, u32[]{:S(2)}) %all-to-all-start.10) | async-done | bytes 2097184 | tf_op jit(solution)/shard_map/all_to_all | solution.py:376
  405.0 6.0 all-to-all-start.8
  411.1 9.7 %shard_map.152 = (bf16[3,512,256]{2,1,0:T(8,128)(2,1)}, bf16[3,512,256]{2,1,0:T(8,128)(2,1)}, bf16[3,768,512]{2,1,0:T(8,128)(2,1)}, bf16[3,2048,512]{2,1,0:T(8,128)(2,1)}) custom-call(s32[2]{0:T(128)S(1)} %pad_add_fusion.sec, bf16[512,2048]{1,0:T(8,128)(2,1)} %bitcast.109, bf16[2048,768]{1,0:T(8,128)(2,1)} %bitcast.69, bf16[2048,768]{1,0:T(8,128)(2,1)} %bitcast.80), custom_call_target="tpu_custom_call" | custom-call | flops 3221225472 | bytes 8388608 | tf_op jit(solution)/shard_map/pallas_call | solution.py:59
  420.8 11.0 %shard_map.153 = (bf16[3,512,768]{2,1,0:T(8,128)(2,1)}, bf16[3,512,768]{2,1,0:T(8,128)(2,1)}, bf16[512,2048]{1,0:T(8,128)(2,1)}) custom-call(s32[2]{0:T(128)S(1)} %pad_add_fusion.sec, bf16[512,2048]{1,0:T(8,128)(2,1)S(1)} %bitcast.121, bf16[3,2048,256]{2,1,0:T(8,128)(2,1)} %get-tuple-element.109.refs_1_.wd_ref, ...), custom_call_target="tpu_custom_call" | custom-call | flops 4831838208 | bytes 13107200 | tf_op jit(solution)/shard_map/pallas_call | solution.py:59
  431.8 7.2 all-to-all-done.8
  440.4 7.0 all-to-all-start.11
  452.7 8.2 shard_map.147
  460.9 14.4 %all-to-all-done.11 = bf16[32,16,2048]{2,1,0:T(8,128)(2,1)} async-done(((bf16[32,16,2048]{2,1,0:T(8,128)(2,1)}), bf16[32,16,2048]{2,1,0:T(8,128)(2,1)}, u32[]{:S(2)}, u32[]{:S(2)}) %all-to-all-start.11) | async-done | bytes 2097184 | tf_op jit(solution)/shard_map/all_to_all | solution.py:376
  475.3 6.3 all-to-all-start.9
  482.3 4.4 shard_map.154
  494.5 15.1 %all-to-all-done.9 = bf16[32,16,2048]{2,1,0:T(8,128)(2,1)S(1)} async-done(((bf16[32,16,2048]{2,1,0:T(8,128)(2,1)}), bf16[32,16,2048]{2,1,0:T(8,128)(2,1)S(1)}, u32[]{:S(2)}, u32[]{:S(2)}) %all-to-all-start.9) | async-done | bytes 2097184 | tf_op jit(solution)/shard_map/all_to_all | solution.py:376
  518.4 6.0 all-to-all-start.12
  524.5 10.3 %shard_map.157 = (bf16[3,512,256]{2,1,0:T(8,128)(2,1)}, bf16[3,512,256]{2,1,0:T(8,128)(2,1)}, bf16[3,768,512]{2,1,0:T(8,128)(2,1)}, bf16[3,2048,512]{2,1,0:T(8,128)(2,1)}) custom-call(s32[2]{0:T(128)S(1)} %pad_add_fusion.sec, bf16[512,2048]{1,0:T(8,128)(2,1)} %bitcast.111, ...), custom_call_target="tpu_custom_call", output_to_operand_aliasing={{2}: (5, {}), {3}: (6, {})} | custom-call | flops 3221225472 | bytes 19136512 | tf_op jit(solution)/shard_map/pallas_call | solution.py:59
  534.8 17.6 %all-to-all-done.12 = bf16[32,16,2048]{2,1,0:T(8,128)(2,1)S(1)} async-done(((bf16[32,16,2048]{2,1,0:T(8,128)(2,1)}), bf16[32,16,2048]{2,1,0:T(8,128)(2,1)S(1)}, u32[]{:S(2)}, u32[]{:S(2)}) %all-to-all-start.12) | async-done | bytes 2097184 | tf_op jit(solution)/shard_map/all_to_all | solution.py:376
  552.4 11.1 %shard_map.158 = (bf16[3,512,768]{2,1,0:T(8,128)(2,1)}, bf16[3,512,768]{2,1,0:T(8,128)(2,1)}, bf16[512,2048]{1,0:T(8,128)(2,1)}) custom-call(s32[2]{0:T(128)S(1)} %pad_add_fusion.sec, bf16[512,2048]{1,0:T(8,128)(2,1)S(1)} %bitcast.122, bf16[3,2048,256]{2,1,0:T(8,128)(2,1)} %get-tuple-element.109.refs_1_.wd_ref, ...), custom_call_target="tpu_custom_call", output_to_operand_aliasing={{0}: (6, {}), {1}: (7, {})} | custom-call | flops 4831838208 | bytes 17825792 | tf_op jit(solution)/shard_map/pallas_call | solution.py:59
  563.5 6.0 all-to-all-start.13
  569.5 5.3 shard_map.159
  574.8 22.7 %all-to-all-done.13 = bf16[32,16,2048]{2,1,0:T(8,128)(2,1)S(1)} async-done(((bf16[32,16,2048]{2,1,0:T(8,128)(2,1)}), bf16[32,16,2048]{2,1,0:T(8,128)(2,1)S(1)}, u32[]{:S(2)}, u32[]{:S(2)}) %all-to-all-start.13) | async-done | bytes 2097184 | tf_op jit(solution)/shard_map/all_to_all | solution.py:376
  601.7 7.1 collective-permute-done.5.refs_0_
  612.2 7.8 all-to-all-start.14
  620.0 10.3 %shard_map.164 = (bf16[3,512,256]{2,1,0:T(8,128)(2,1)}, bf16[3,512,256]{2,1,0:T(8,128)(2,1)}, bf16[3,768,512]{2,1,0:T(8,128)(2,1)}, bf16[3,2048,512]{2,1,0:T(8,128)(2,1)}) custom-call(s32[2]{0:T(128)S(1)} %pad_add_fusion.sec, bf16[512,2048]{1,0:T(8,128)(2,1)} %bitcast.110, bf16[512,2048]{1,0:T(8,128)(2,1)} %bitcast.98, ...), custom_call_target="tpu_custom_call", output_to_operand_aliasing={{2}: (5, {}), {3}: (6, {})} | custom-call | flops 3221225472 | bytes 19136512 | tf_op jit(solution)/shard_map/pallas_call | solution.py:59
  630.3 17.4 %all-to-all-done.14 = bf16[32,16,2048]{2,1,0:T(8,128)(2,1)S(1)} async-done(((bf16[32,16,2048]{2,1,0:T(8,128)(2,1)}), bf16[32,16,2048]{2,1,0:T(8,128)(2,1)S(1)}, u32[]{:S(2)}, u32[]{:S(2)}) %all-to-all-start.14) | async-done | bytes 2097184 | tf_op jit(solution)/shard_map/all_to_all | solution.py:376
  647.8 11.1 %shard_map.165 = (bf16[3,512,768]{2,1,0:T(8,128)(2,1)}, bf16[3,512,768]{2,1,0:T(8,128)(2,1)}, bf16[512,2048]{1,0:T(8,128)(2,1)}) custom-call(s32[2]{0:T(128)S(1)} %pad_add_fusion.sec, bf16[512,2048]{1,0:T(8,128)(2,1)S(1)} %bitcast.124, bf16[3,2048,256]{2,1,0:T(8,128)(2,1)} %get-tuple-element.109.refs_1_.wd_ref, ...), custom_call_target="tpu_custom_call", output_to_operand_aliasing={{0}: (6, {}), {1}: (7, {})} | custom-call | flops 4831838208 | bytes 17825792 | tf_op jit(solution)/shard_map/pallas_call | solution.py:59
  658.8 6.0 all-to-all-start.15
  664.9 5.2 shard_map.162
  672.9 19.9 %all-to-all-done.15 = bf16[32,16,2048]{2,1,0:T(8,128)(2,1)S(1)} async-done(((bf16[32,16,2048]{2,1,0:T(8,128)(2,1)}), bf16[32,16,2048]{2,1,0:T(8,128)(2,1)S(1)}, u32[]{:S(2)}, u32[]{:S(2)}) %all-to-all-start.15) | async-done | bytes 2097184 | tf_op jit(solution)/shard_map/all_to_all | solution.py:376
  695.7 5.9 all-to-all-start.16
  702.9 8.7 collective-permute-done.9.refs_0_
  715.1 8.0 all-to-all-start.17
  734.9 10.3 %shard_map.170 = (bf16[3,512,256]{2,1,0:T(8,128)(2,1)}, bf16[3,512,256]{2,1,0:T(8,128)(2,1)}, bf16[3,768,512]{2,1,0:T(8,128)(2,1)}, bf16[3,2048,512]{2,1,0:T(8,128)(2,1)}) custom-call(s32[2]{0:T(128)S(1)} %pad_add_fusion.sec, bf16[512,2048]{1,0:T(8,128)(2,1)} %bitcast.102, ...), custom_call_target="tpu_custom_call", output_to_operand_aliasing={{2}: (5, {}), {3}: (6, {})} | custom-call | flops 3221225472 | bytes 19202048 | tf_op jit(solution)/shard_map/pallas_call | solution.py:59
  745.3 5.7 all-to-all-done.17
  751.0 11.1 %shard_map.171 = (bf16[3,512,768]{2,1,0:T(8,128)(2,1)}, bf16[3,512,768]{2,1,0:T(8,128)(2,1)}, bf16[512,2048]{1,0:T(8,128)(2,1)}) custom-call(s32[2]{0:T(128)S(1)} %pad_add_fusion.sec, bf16[512,2048]{1,0:T(8,128)(2,1)S(1)} %bitcast.126, bf16[3,2048,256]{2,1,0:T(8,128)(2,1)} %get-tuple-element.109.refs_1_.wd_ref, ...), custom_call_target="tpu_custom_call", output_to_operand_aliasing={{0}: (6, {}), {1}: (7, {})} | custom-call | flops 4831838208 | bytes 17825792 | tf_op jit(solution)/shard_map/pallas_call | solution.py:59
  762.0 6.1 all-to-all-start.18
  768.3 5.3 shard_map.172
  773.6 18.1 %shard_map.173 = (bf16[2048,768]{1,0:T(8,128)(2,1)}, bf16[2048,768]{1,0:T(8,128)(2,1)}, bf16[768,2048]{1,0:T(8,128)(2,1)}) custom-call(s32[2]{0:T(128)S(1)} %pad_add_fusion.sec, bf16[3,2048,512]{2,1,0:T(8,128)(2,1)} %get-tuple-element.184.xt_ref.refs_4_, bf16[3,512,768]{2,1,0:T(8,128)(2,1)} %get-tuple-element.185.gg_ref, ...), custom_call_target="tpu_custom_call" | custom-call | flops 9663676416 | bytes 21757952 | tf_op jit(solution)/shard_map/pallas_call | solution.py:59
  791.7 8.7 all-to-all-done.18
  804.6 7.1 collective-permute-done.10.refs_0_
  815.1 4.4 shard_map.176
  819.5 6.2 all-to-all-start.19
  825.7 9.6 %shard_map.178 = (bf16[3,512,256]{2,1,0:T(8,128)(2,1)}, bf16[3,512,256]{2,1,0:T(8,128)(2,1)}, bf16[3,768,512]{2,1,0:T(8,128)(2,1)}, bf16[3,2048,512]{2,1,0:T(8,128)(2,1)}) custom-call(s32[2]{0:T(128)S(1)} %pad_add_fusion.sec, bf16[512,2048]{1,0:T(8,128)(2,1)} %bitcast.99, bf16[2048,768]{1,0:T(8,128)(2,1)} %bitcast.73, ...), custom_call_target="tpu_custom_call", output_to_operand_aliasing={{2}: (4, {}), {3}: (5, {})} | custom-call | flops 3221225472 | bytes 26476544 | tf_op jit(solution)/shard_map/pallas_call | solution.py:59
  841.1 13.6 %all-to-all-done.19 = bf16[32,16,2048]{2,1,0:T(8,128)(2,1)S(1)} async-done(((bf16[32,16,2048]{2,1,0:T(8,128)(2,1)}), bf16[32,16,2048]{2,1,0:T(8,128)(2,1)S(1)}, u32[]{:S(2)}, u32[]{:S(2)}) %all-to-all-start.19) | async-done | bytes 2097184 | tf_op jit(solution)/shard_map/all_to_all | solution.py:376
  854.7 15.4 %shard_map.179 = (bf16[2048,768]{1,0:T(8,128)(2,1)}, bf16[2048,768]{1,0:T(8,128)(2,1)}, bf16[768,2048]{1,0:T(8,128)(2,1)}) custom-call(s32[2]{0:T(128)S(1)} %pad_add_fusion.sec, bf16[512,2048]{1,0:T(8,128)(2,1)S(1)} %bitcast.113, bf16[3,2048,256]{2,1,0:T(8,128)(2,1)} %get-tuple-element.109.refs_1_.wd_ref, bf16[3,512,256]{2,1,0:T(8,128)(2,1)} %get-tuple-element.195.a1_ref, ...), custom_call_target="tpu_custom_call" | custom-call | flops 6442450944 | bytes 25952256 | tf_op jit(solution)/shard_map/pallas_call | solution.py:59
  870.1 9.6 %all-gather.7.cloned.1.call-done = bf16[1024,2048]{1,0:T(8,128)(2,1)} async-done(((bf16[32,2048]{1,0:T(8,128)(2,1)}), bf16[1024,2048]{1,0:T(8,128)(2,1)}) %all-gather.7.cloned.1.call-update) | async-done | bytes 4194320 | tf_op jit(solution)/shard_map/all_gather | solution.py:708
  879.7 4.6 shard_map.177
  (161 shorter events, 132.3 us)
Async XLA Ops:
  8.0 42.1 %copy-start.22 = (bf16[1,1,768,2048]{3,2,1,0:T(8,128)(2,1)S(1)}, bf16[1,1,768,2048]{3,2,1,0:T(8,128)(2,1)}, u32[]{:S(2)}) copy-start(bf16[1,1,768,2048]{3,2,1,0:T(8,128)(2,1)} %param.15) | copy-start | bytes 9437188
  9.3 40.8 %copy-start.3 = (bf16[1,1,2048,768]{3,2,1,0:T(8,128)(2,1)S(1)}, bf16[1,1,2048,768]{3,2,1,0:T(8,128)(2,1)}, u32[]{:S(2)}) copy-start(bf16[1,1,2048,768]{3,2,1,0:T(8,128)(2,1)} %param.14) | copy-start | bytes 9437188
  12.8 37.3 %copy-start.36 = (bf16[64,2048]{1,0:T(8,128)(2,1)}, bf16[64,2048]{1,0:T(8,128)(2,1)S(1)}, u32[]{:S(2)}) copy-start(bf16[64,2048]{1,0:T(8,128)(2,1)S(1)} %get-tuple-element.106.n_ref) | copy-start | bytes 786436
  12.8 37.3 %copy-start = (bf16[1,1,2048,768]{3,2,1,0:T(8,128)(2,1)S(1)}, bf16[1,1,2048,768]{3,2,1,0:T(8,128)(2,1)}, u32[]{:S(2)}) copy-start(bf16[1,1,2048,768]{3,2,1,0:T(8,128)(2,1)} %param.13) | copy-start | bytes 9437188
  50.1 8.1 copy-start.18
  58.2 4.2 copy-start.44
  58.2 4.5 copy-start.37
  58.2 32.2 %all-to-all-start.1 = ((bf16[32,16,2048]{2,1,0:T(8,128)(2,1)}), bf16[32,16,2048]{2,1,0:T(8,128)(2,1)S(1)}, u32[]{:S(2)}, u32[]{:S(2)}) async-start(bf16[32,16,2048]{2,1,0:T(8,128)(2,1)} %bitcast.131), calls=%async_computation.1 | async-start | bytes 4194304 | tf_op jit(solution)/shard_map/all_to_all | solution.py:376
  62.7 11.9 %copy-start.10 = (bf16[2048,32]{1,0:T(8,128)(2,1)}, bf16[2048,32]{1,0:T(8,128)(2,1)S(1)}, u32[]{:S(2)}) copy-start(bf16[2048,32]{1,0:T(8,128)(2,1)S(1)} %copy.29.router_ref) | copy-start | bytes 393220
  90.3 49.5 %copy-start.4 = (bf16[1,1,2048,768]{3,2,1,0:T(8,128)(2,1)S(1)}, bf16[1,1,2048,768]{3,2,1,0:T(8,128)(2,1)}, u32[]{:S(2)}) copy-start(bf16[1,1,2048,768]{3,2,1,0:T(8,128)(2,1)} %param.14) | copy-start | bytes 9437188
  90.3 49.5 %copy-start.23 = (bf16[1,1,768,2048]{3,2,1,0:T(8,128)(2,1)S(1)}, bf16[1,1,768,2048]{3,2,1,0:T(8,128)(2,1)}, u32[]{:S(2)}) copy-start(bf16[1,1,768,2048]{3,2,1,0:T(8,128)(2,1)} %param.15) | copy-start | bytes 9437188
  93.7 6.8 collective-permute-start
  103.2 36.6 %copy-start.38 = (bf16[64,2048]{1,0:T(8,128)(2,1)}, bf16[64,2048]{1,0:T(8,128)(2,1)S(1)}, u32[]{:S(2)}) copy-start(bf16[64,2048]{1,0:T(8,128)(2,1)S(1)} %get-tuple-element.112.n_ref) | copy-start | bytes 786436
  103.2 36.7 %copy-start.1 = (bf16[1,1,2048,768]{3,2,1,0:T(8,128)(2,1)S(1)}, bf16[1,1,2048,768]{3,2,1,0:T(8,128)(2,1)}, u32[]{:S(2)}) copy-start(bf16[1,1,2048,768]{3,2,1,0:T(8,128)(2,1)} %param.13) | copy-start | bytes 9437188
  139.8 8.1 copy-start.16
  147.9 4.9 copy-start.39
  147.9 32.9 %all-to-all-start.3 = ((bf16[32,16,2048]{2,1,0:T(8,128)(2,1)}), bf16[32,16,2048]{2,1,0:T(8,128)(2,1)}, u32[]{:S(2)}, u32[]{:S(2)}) async-start(bf16[32,16,2048]{2,1,0:T(8,128)(2,1)} %bitcast.151), calls=%async_computation.3 | async-start | bytes 4194304 | tf_op jit(solution)/shard_map/all_to_all | solution.py:376
  180.8 49.6 %copy-start.24 = (bf16[1,1,768,2048]{3,2,1,0:T(8,128)(2,1)S(1)}, bf16[1,1,768,2048]{3,2,1,0:T(8,128)(2,1)}, u32[]{:S(2)}) copy-start(bf16[1,1,768,2048]{3,2,1,0:T(8,128)(2,1)} %param.15) | copy-start | bytes 9437188
  183.6 7.4 collective-permute-start.1
  193.6 36.7 %copy-start.5 = (bf16[1,1,2048,768]{3,2,1,0:T(8,128)(2,1)S(1)}, bf16[1,1,2048,768]{3,2,1,0:T(8,128)(2,1)}, u32[]{:S(2)}) copy-start(bf16[1,1,2048,768]{3,2,1,0:T(8,128)(2,1)} %param.14) | copy-start | bytes 9437188
  230.4 8.1 copy-start.17
  238.5 32.9 %all-to-all-start.5 = ((bf16[32,16,2048]{2,1,0:T(8,128)(2,1)}), bf16[32,16,2048]{2,1,0:T(8,128)(2,1)}, u32[]{:S(2)}, u32[]{:S(2)}) async-start(bf16[32,16,2048]{2,1,0:T(8,128)(2,1)} %bitcast.152), calls=%async_computation.5 | async-start | bytes 4194304 | tf_op jit(solution)/shard_map/all_to_all | solution.py:376
  271.4 49.5 %copy-start.25 = (bf16[1,1,768,2048]{3,2,1,0:T(8,128)(2,1)S(1)}, bf16[1,1,768,2048]{3,2,1,0:T(8,128)(2,1)}, u32[]{:S(2)}) copy-start(bf16[1,1,768,2048]{3,2,1,0:T(8,128)(2,1)} %param.15) | copy-start | bytes 9437188
  274.2 7.4 collective-permute-start.2
  284.3 36.7 %copy-start.6 = (bf16[1,1,2048,768]{3,2,1,0:T(8,128)(2,1)S(1)}, bf16[1,1,2048,768]{3,2,1,0:T(8,128)(2,1)}, u32[]{:S(2)}) copy-start(bf16[1,1,2048,768]{3,2,1,0:T(8,128)(2,1)} %param.14) | copy-start | bytes 9437188
  320.9 8.1 copy-start.19
  329.0 4.9 copy-start.13
  329.0 32.2 %all-to-all-start.7 = ((bf16[32,16,2048]{2,1,0:T(8,128)(2,1)}), bf16[32,16,2048]{2,1,0:T(8,128)(2,1)S(1)}, u32[]{:S(2)}, u32[]{:S(2)}) async-start(bf16[32,16,2048]{2,1,0:T(8,128)(2,1)} %bitcast.150), calls=%async_computation.7 | async-start | bytes 4194304 | tf_op jit(solution)/shard_map/all_to_all | solution.py:376
  333.2 30.3 %copy-start.34 = (bf16[2048,128]{1,0:T(8,128)(2,1)S(1)}, bf16[2048,128]{1,0:T(8,128)(2,1)}, u32[]{:S(2)}) copy-start(bf16[2048,128]{1,0:T(8,128)(2,1)} %head_ref.3) | copy-start | bytes 1572868
  335.8 27.8 %copy-start.41 = (s32[64,1]{1,0:T(8,128)S(1)}, s32[64,1]{1,0:T(8,128)}, u32[]{:S(2)}) copy-start(s32[64,1]{1,0:T(8,128)} %copy.33.label_ref) | copy-start | bytes 772
  361.2 8.6 copy-start.8
  363.6 12.2 %copy-start.27 = (bf16[64,2048]{1,0:T(8,128)(2,1)}, bf16[64,2048]{1,0:T(8,128)(2,1)S(1)}, u32[]{:S(2)}) copy-start(bf16[64,2048]{1,0:T(8,128)(2,1)S(1)} %shard_map.144.final_ref.refs_0_) | copy-start | bytes 786436
  369.7 34.0 %all-to-all-start.10 = ((bf16[32,16,2048]{2,1,0:T(8,128)(2,1)}), bf16[32,16,2048]{2,1,0:T(8,128)(2,1)S(1)}, u32[]{:S(2)}, u32[]{:S(2)}) async-start(bf16[32,16,2048]{2,1,0:T(8,128)(2,1)} %bitcast.146), calls=%async_computation.10 | async-start | bytes 4194304 | tf_op jit(solution)/shard_map/all_to_all | solution.py:376
  375.8 9.4 %collective-permute-start.3 = (bf16[64,2048]{1,0:T(8,128)(2,1)S(1)}, bf16[64,2048]{1,0:T(8,128)(2,1)S(1)}, u32[]{:S(2)}, u32[]{:S(2)}) collective-permute-start(bf16[64,2048]{1,0:T(8,128)(2,1)S(1)} %shard_map.144.final_ref.refs_0_), channel_id=1, source_target_pairs={{0,32},{32,64},{64,96},{1,33},{33,65},{65,97},{2,34},{34,66},{66,9... | collective-permute-start | bytes 786440 | tf_op jit(solution)/shard_map/ppermute | solution.py:382
  405.0 34.0 %all-to-all-start.8 = ((bf16[32,16,2048]{2,1,0:T(8,128)(2,1)}), bf16[32,16,2048]{2,1,0:T(8,128)(2,1)S(1)}, u32[]{:S(2)}, u32[]{:S(2)}) async-start(bf16[32,16,2048]{2,1,0:T(8,128)(2,1)} %bitcast.144), calls=%async_computation.8 | async-start | bytes 4194304 | tf_op jit(solution)/shard_map/all_to_all | solution.py:376
  411.1 9.7 %copy-start.30 = (bf16[32,16,2048]{2,1,0:T(8,128)(2,1)S(1)}, bf16[32,16,2048]{2,1,0:T(8,128)(2,1)}, u32[]{:S(2)}) copy-start(bf16[32,16,2048]{2,1,0:T(8,128)(2,1)} %copy-done.29) | copy-start | bytes 6291460
  440.4 7.0 copy-start.2
  440.4 35.0 %all-to-all-start.11 = ((bf16[32,16,2048]{2,1,0:T(8,128)(2,1)}), bf16[32,16,2048]{2,1,0:T(8,128)(2,1)}, u32[]{:S(2)}, u32[]{:S(2)}) async-start(bf16[32,16,2048]{2,1,0:T(8,128)(2,1)} %bitcast.149), calls=%async_computation.11 | async-start | bytes 4194304 | tf_op jit(solution)/shard_map/all_to_all | solution.py:376
  475.3 34.2 %all-to-all-start.9 = ((bf16[32,16,2048]{2,1,0:T(8,128)(2,1)}), bf16[32,16,2048]{2,1,0:T(8,128)(2,1)S(1)}, u32[]{:S(2)}, u32[]{:S(2)}) async-start(bf16[32,16,2048]{2,1,0:T(8,128)(2,1)} %bitcast.142), calls=%async_computation.9 | async-start | bytes 4194304 | tf_op jit(solution)/shard_map/all_to_all | solution.py:376
  486.8 5.9 copy-start.14
  490.5 21.4 %copy-start.35 = (bf16[2048,128]{1,0:T(8,128)(2,1)S(1)}, bf16[2048,128]{1,0:T(8,128)(2,1)}, u32[]{:S(2)}) copy-start(bf16[2048,128]{1,0:T(8,128)(2,1)} %head_ref.3) | copy-start | bytes 1572868
  490.5 23.3 %collective-permute-start.4 = (bf16[64,2048]{1,0:T(8,128)(2,1)}, bf16[64,2048]{1,0:T(8,128)(2,1)}, u32[]{:S(2)}, u32[]{:S(2)}) collective-permute-start(bf16[64,2048]{1,0:T(8,128)(2,1)} %shard_map.155), channel_id=1, source_target_pairs={{32,0},{64,32},{96,64},{33,1},{65,33},{97,65},{34,2},{66,34},{98,6... | collective-permute-start | bytes 786440 | tf_op jit(solution)/shard_map/ppermute | solution.py:382
  494.5 17.5 %copy-start.40 = (s32[64,1]{1,0:T(8,128)S(1)}, s32[64,1]{1,0:T(8,128)}, u32[]{:S(2)}) copy-start(s32[64,1]{1,0:T(8,128)} %copy.35.label_ref) | copy-start | bytes 772
  509.6 8.9 copy-start.9
  512.0 6.5 copy-start.28
  518.4 34.0 %all-to-all-start.12 = ((bf16[32,16,2048]{2,1,0:T(8,128)(2,1)}), bf16[32,16,2048]{2,1,0:T(8,128)(2,1)S(1)}, u32[]{:S(2)}, u32[]{:S(2)}) async-start(bf16[32,16,2048]{2,1,0:T(8,128)(2,1)} %bitcast.147), calls=%async_computation.12 | async-start | bytes 4194304 | tf_op jit(solution)/shard_map/all_to_all | solution.py:376
  552.4 11.1 %copy-start.31 = (bf16[32,16,2048]{2,1,0:T(8,128)(2,1)}, bf16[32,16,2048]{2,1,0:T(8,128)(2,1)S(1)}, u32[]{:S(2)}) copy-start(bf16[32,16,2048]{2,1,0:T(8,128)(2,1)S(1)} %all-to-all-done.12) | copy-start | bytes 6291460
  563.5 34.0 %all-to-all-start.13 = ((bf16[32,16,2048]{2,1,0:T(8,128)(2,1)}), bf16[32,16,2048]{2,1,0:T(8,128)(2,1)S(1)}, u32[]{:S(2)}, u32[]{:S(2)}) async-start(bf16[32,16,2048]{2,1,0:T(8,128)(2,1)} %bitcast.145), calls=%async_computation.13 | async-start | bytes 4194304 | tf_op jit(solution)/shard_map/all_to_all | solution.py:376
  600.4 8.4 collective-permute-start.5
  612.2 35.6 %all-to-all-start.14 = ((bf16[32,16,2048]{2,1,0:T(8,128)(2,1)}), bf16[32,16,2048]{2,1,0:T(8,128)(2,1)S(1)}, u32[]{:S(2)}, u32[]{:S(2)}) async-start(bf16[32,16,2048]{2,1,0:T(8,128)(2,1)} %bitcast.148), calls=%async_computation.14 | async-start | bytes 4194304 | tf_op jit(solution)/shard_map/all_to_all | solution.py:376
  647.8 11.1 %copy-start.32 = (bf16[32,16,2048]{2,1,0:T(8,128)(2,1)}, bf16[32,16,2048]{2,1,0:T(8,128)(2,1)S(1)}, u32[]{:S(2)}) copy-start(bf16[32,16,2048]{2,1,0:T(8,128)(2,1)S(1)} %all-to-all-done.14) | copy-start | bytes 6291460
  658.8 34.0 %all-to-all-start.15 = ((bf16[32,16,2048]{2,1,0:T(8,128)(2,1)}), bf16[32,16,2048]{2,1,0:T(8,128)(2,1)S(1)}, u32[]{:S(2)}, u32[]{:S(2)}) async-start(bf16[32,16,2048]{2,1,0:T(8,128)(2,1)} %bitcast.143), calls=%async_computation.15 | async-start | bytes 4194304 | tf_op jit(solution)/shard_map/all_to_all | solution.py:376
  695.7 19.4 %all-to-all-start.16 = ((bf16[32,64,128]{2,1,0:T(8,128)(2,1)}), bf16[32,64,128]{2,1,0:T(8,128)(2,1)S(1)}, u32[]{:S(2)}, u32[]{:S(2)}) async-start(bf16[32,64,128]{2,1,0:T(8,128)(2,1)} %bitcast.44), calls=%async_computation.16 | async-start | bytes 1048576 | tf_op jit(solution)/shard_map/all_to_all | solution.py:376
  701.6 10.0 %collective-permute-start.9 = (bf16[64,2048]{1,0:T(8,128)(2,1)S(1)}, bf16[64,2048]{1,0:T(8,128)(2,1)S(1)}, u32[]{:S(2)}, u32[]{:S(2)}) collective-permute-start(bf16[64,2048]{1,0:T(8,128)(2,1)S(1)} %shard_map.166), channel_id=1, source_target_pairs={{32,0},{64,32},{96,64},{33,1},{65,33},{97,65},{34,2},{66,34},{98,6... | collective-permute-start | bytes 786440 | tf_op jit(solution)/shard_map/ppermute | solution.py:382
  715.1 35.9 %all-to-all-start.17 = ((bf16[32,16,2048]{2,1,0:T(8,128)(2,1)}), bf16[32,16,2048]{2,1,0:T(8,128)(2,1)S(1)}, u32[]{:S(2)}, u32[]{:S(2)}) async-start(bf16[32,16,2048]{2,1,0:T(8,128)(2,1)} %bitcast.139), calls=%async_computation.17 | async-start | bytes 4194304 | tf_op jit(solution)/shard_map/all_to_all | solution.py:376
  723.1 112.2 %all-gather.5.cloned.1.call-start = ((), (), s32[]{:S(2)}) async-start(), calls=%async_computation.20 | async-start | bytes 2162688 | tf_op jit(solution)/shard_map/all_gather | solution.py:705
  727.7 6.6 collective-permute-start.6
  729.0 5.3 collective-permute-start.7
  729.6 4.6 collective-permute-start.8
  751.0 11.1 %copy-start.33 = (bf16[32,16,2048]{2,1,0:T(8,128)(2,1)}, bf16[32,16,2048]{2,1,0:T(8,128)(2,1)S(1)}, u32[]{:S(2)}) copy-start(bf16[32,16,2048]{2,1,0:T(8,128)(2,1)S(1)} %all-to-all-done.17) | copy-start | bytes 6291460
  762.0 38.4 %all-to-all-start.18 = ((bf16[32,16,2048]{2,1,0:T(8,128)(2,1)}), bf16[32,16,2048]{2,1,0:T(8,128)(2,1)S(1)}, u32[]{:S(2)}, u32[]{:S(2)}) async-start(bf16[32,16,2048]{2,1,0:T(8,128)(2,1)} %bitcast.141), calls=%async_computation.18 | async-start | bytes 4194304 | tf_op jit(solution)/shard_map/all_to_all | solution.py:376
  768.1 111.6 %all-gather.7.cloned.1.call-start = ((), (), s32[]{:S(2)}) async-start(), calls=%async_computation.21 | async-start | bytes 4325376 | tf_op jit(solution)/shard_map/all_gather | solution.py:708
  803.3 8.4 collective-permute-start.10
  819.5 35.2 %all-to-all-start.19 = ((bf16[32,16,2048]{2,1,0:T(8,128)(2,1)}), bf16[32,16,2048]{2,1,0:T(8,128)(2,1)S(1)}, u32[]{:S(2)}, u32[]{:S(2)}) async-start(bf16[32,16,2048]{2,1,0:T(8,128)(2,1)} %bitcast.140), calls=%async_computation.19 | async-start | bytes 4194304 | tf_op jit(solution)/shard_map/all_to_all | solution.py:376
  (11 other events, 19.5 us)
Sparse Core Ops, SparseCore 0:
  735.0 60.0 all-gather.4
  819.6 60.0 all-gather.6

commit v4 on v3

--- a/solution.py
+++ b/solution.py
@@ -212,7 +212,7 @@
 
 
 def prep_bwd_kernel(tick, n_g, n_p, sec, *refs):
-    g_refs, phl_refs, (g_ref, out_ref) = refs[:n_g], refs[n_g : n_g + n_p], refs[n_g + n_p :]
+    g_refs, phl_refs, (g_ref, out_ref) = refs[:n_g], refs[n_g : n_g + n_p], refs[-2:]
     flag = sec[0] == sec[1] - tick
     step = pl.program_id(0)
     chunk = out_ref.shape[1]
@@ -552,18 +552,22 @@
             return pl.BlockSpec((1, *shape), index)
 
         count = len(cands)
-        gsel, outgoing = run(
-            functools.partial(prep_bwd_kernel, tick, len(grads), count),
-            (sec, *grads, *far([c[3] for c in cands])),
-            [whole(a) for a in grads] + [whole(c[3]) for c in cands],
-            [far_out(row_full), buf_out],
-            [whole(row_full), buf_block],
-            grid=(col_steps,),
-            cost=4 * rows * packed * width,
-        )
-        arrived = to_owners(outgoing)
+        def prep(*order):
+            return run(
+                functools.partial(prep_bwd_kernel, tick, len(grads), count),
+                (sec, *grads, *far([*[c[3] for c in cands], *order])),
+                [whole(a) for a in grads]
+                + [whole(c[3]) for c in cands]
+                + [anywhere] * len(order),
+                [far_out(row_full), buf_out],
+                [whole(row_full), buf_block],
+                grid=(col_steps,),
+                cost=4 * rows * packed * width,
+            )
+
+        if not last:
+            gsel, outgoing = prep()
         route_args = (
-            gsel,
             *[c[1] for c in cands],
             *[c[2] for c in cands],
             *[c[4] for c in cands],
@@ -577,12 +581,15 @@
             acc_full = sds((experts, width), BF)
         grad_normed, router_sum = run(
             functools.partial(route_bwd_kernel, tick, slots, count, micros),
-            (sec, *far(route_args)),
-            [whole(a) for a in route_args],
+            (sec, grads[0] if last else Far(gsel), *far(route_args)),
+            [whole(row_full)] + [whole(a) for a in route_args],
             [far_out(wide_f), far_out(acc_full)],
             [whole(wide_f), whole(acc_full)],
             cost=2 * rows * packed * width,
         )
+        if last:
+            _, outgoing = prep(router_sum)
+        arrived = to_owners(outgoing)
         act = sds((steps, packed, tile), BF)
         stores = [
             sds((micros + 1, ffe, packed), BF),

time: 904 us -> 901 us (level)
  no operation moved by 1% of the time
where the time goes in v4:
time: 901 us; the launch traced here: 890 us
  waiting for transfers between devices  298 us (33%)
  Pallas kernels  285 us (32%)
  blocking collectives  147 us (16%)
  starting transfers between devices  120 us (13%)
  local copies, waits for them, and re-layouts  20.6 us (2%)
  between operations  17.9 us (2%)
    pallas_call x53, Pallas kernels, run(): pl.pallas_call(kernel, grid_spec=pltpu.PrefetchScalarGridSpec(num_scalar_...  285 us
    all_to_all x16, waiting for transfers between devices, to_owners(): return lax.all_to_all(rows, plane, split_axis=0, concat_axis=0, tiled=True)  250 us
    all_to_all x4, blocking collectives, to_owners(): return lax.all_to_all(rows, plane, split_axis=0, concat_axis=0, tiled=True)  147 us
    all_to_all x16, starting transfers between devices, to_owners(): return lax.all_to_all(rows, plane, split_axis=0, concat_axis=0, tiled=True)  95.7 us
    ppermute x8, waiting for transfers between devices, from_behind(): return lax.ppermute(block, axis, route)  38 us
    ppermute x8, starting transfers between devices, from_behind(): return lax.ppermute(block, axis, route)  21.2 us
  transfers between devices with their start and end apart: 29, of which 24 were waited for; matrix products, arithmetic and copies ran while one was open for 1% of the time, Pallas kernels for 21%

profile of v4, /device:TPU:1, one launch (start us, length us, event | category | flops | bytes accessed | tf_op | source)
XLA Modules:
  0.0 889.5 jit_solution(14273388801030453520)
XLA Ops:
  12.8 37.3 %all_to_all.220 = bf16[32,16,2048]{2,1,0:T(8,128)(2,1)S(1)} all-to-all(bf16[32,16,2048]{2,1,0:T(8,128)(2,1)} %bitcast.154), channel_id=1, replica_groups=mesh['section'=4,'expert'=4,'dp'=8] {'expert','dp'}, dimensions={0} | all-to-all | bytes 4194304 | tf_op jit(solution)/shard_map/all_to_all | solution.py:376
  50.1 8.1 shard_map.129.dep_ref
  58.2 4.2 all-to-all-start.1
  64.5 10.1 %shard_map.131 = (bf16[2,1536,1024]{2,1,0:T(8,128)(2,1)}, bf16[3,2048,256]{2,1,0:T(8,128)(2,1)}) custom-call(s32[2]{0:T(128)S(1)} %pad_add_fusion.sec, bf16[2048,768]{1,0:T(8,128)(2,1)} %bitcast.68, bf16[2048,768]{1,0:T(8,128)(2,1)} %bitcast.79, bf16[768,2048]{1,0:T(8,128)(2,1)} %bitcast.114, bf16[512,2048]{1,0:T(8,128)(2,1)} %shard_map.129.dep_ref), custom_call_target="tpu_custom_call" | custom-call | flops 1610612736 | bytes 11534336 | tf_op jit(solution)/shard_map/pallas_call | solution.py:59
  74.6 15.8 %all-to-all-done.1 = bf16[32,16,2048]{2,1,0:T(8,128)(2,1)S(1)} async-done(((bf16[32,16,2048]{2,1,0:T(8,128)(2,1)}), bf16[32,16,2048]{2,1,0:T(8,128)(2,1)S(1)}, u32[]{:S(2)}, u32[]{:S(2)}) %all-to-all-start.1) | async-done | bytes 2097184 | tf_op jit(solution)/shard_map/all_to_all | solution.py:376
  103.2 36.6 %all_to_all.221 = bf16[32,16,2048]{2,1,0:T(8,128)(2,1)S(1)} all-to-all(bf16[32,16,2048]{2,1,0:T(8,128)(2,1)} %bitcast.153), channel_id=1, replica_groups=mesh['section'=4,'expert'=4,'dp'=8] {'expert','dp'}, dimensions={0} | all-to-all | bytes 4194304 | tf_op jit(solution)/shard_map/all_to_all | solution.py:376
  139.8 8.1 shard_map.134
  147.9 4.9 all-to-all-start.3
  155.7 25.1 %all-to-all-done.3 = bf16[32,16,2048]{2,1,0:T(8,128)(2,1)} async-done(((bf16[32,16,2048]{2,1,0:T(8,128)(2,1)}), bf16[32,16,2048]{2,1,0:T(8,128)(2,1)}, u32[]{:S(2)}, u32[]{:S(2)}) %all-to-all-start.3) | async-done | bytes 2097184 | tf_op jit(solution)/shard_map/all_to_all | solution.py:376
  193.7 36.7 %all_to_all.222 = bf16[32,16,2048]{2,1,0:T(8,128)(2,1)S(1)} all-to-all(bf16[32,16,2048]{2,1,0:T(8,128)(2,1)} %bitcast.155), channel_id=1, replica_groups=mesh['section'=4,'expert'=4,'dp'=8] {'expert','dp'}, dimensions={0} | all-to-all | bytes 4194304 | tf_op jit(solution)/shard_map/all_to_all | solution.py:376
  230.4 8.1 shard_map.138
  238.5 5.1 all-to-all-start.5
  246.4 24.9 %all-to-all-done.5 = bf16[32,16,2048]{2,1,0:T(8,128)(2,1)} async-done(((bf16[32,16,2048]{2,1,0:T(8,128)(2,1)}), bf16[32,16,2048]{2,1,0:T(8,128)(2,1)}, u32[]{:S(2)}, u32[]{:S(2)}) %all-to-all-start.5) | async-done | bytes 2097184 | tf_op jit(solution)/shard_map/all_to_all | solution.py:376
  274.2 4.1 collective-permute-start.2
  284.3 36.7 %all_to_all.223 = bf16[32,16,2048]{2,1,0:T(8,128)(2,1)S(1)} all-to-all(bf16[32,16,2048]{2,1,0:T(8,128)(2,1)} %bitcast.156), channel_id=1, replica_groups=mesh['section'=4,'expert'=4,'dp'=8] {'expert','dp'}, dimensions={0} | all-to-all | bytes 4194304 | tf_op jit(solution)/shard_map/all_to_all | solution.py:376
  320.9 8.1 shard_map.142
  329.0 4.2 all-to-all-start.7
  335.8 25.4 %all-to-all-done.7 = bf16[32,16,2048]{2,1,0:T(8,128)(2,1)S(1)} async-done(((bf16[32,16,2048]{2,1,0:T(8,128)(2,1)}), bf16[32,16,2048]{2,1,0:T(8,128)(2,1)S(1)}, u32[]{:S(2)}, u32[]{:S(2)}) %all-to-all-start.7) | async-done | bytes 2097184 | tf_op jit(solution)/shard_map/all_to_all | solution.py:376
  369.7 6.0 all-to-all-start.10
  379.9 5.3 collective-permute-done.3.refs_0_
  387.9 15.9 %all-to-all-done.10 = bf16[32,16,2048]{2,1,0:T(8,128)(2,1)S(1)} async-done(((bf16[32,16,2048]{2,1,0:T(8,128)(2,1)}), bf16[32,16,2048]{2,1,0:T(8,128)(2,1)S(1)}, u32[]{:S(2)}, u32[]{:S(2)}) %all-to-all-start.10) | async-done | bytes 2097184 | tf_op jit(solution)/shard_map/all_to_all | solution.py:376
  405.0 6.0 all-to-all-start.8
  411.1 9.7 %shard_map.152 = (bf16[3,512,256]{2,1,0:T(8,128)(2,1)}, bf16[3,512,256]{2,1,0:T(8,128)(2,1)}, bf16[3,768,512]{2,1,0:T(8,128)(2,1)}, bf16[3,2048,512]{2,1,0:T(8,128)(2,1)}) custom-call(s32[2]{0:T(128)S(1)} %pad_add_fusion.sec, bf16[512,2048]{1,0:T(8,128)(2,1)} %bitcast.109, bf16[2048,768]{1,0:T(8,128)(2,1)} %bitcast.69, bf16[2048,768]{1,0:T(8,128)(2,1)} %bitcast.80), custom_call_target="tpu_custom_call" | custom-call | flops 3221225472 | bytes 8388608 | tf_op jit(solution)/shard_map/pallas_call | solution.py:59
  420.8 11.0 %shard_map.153 = (bf16[3,512,768]{2,1,0:T(8,128)(2,1)}, bf16[3,512,768]{2,1,0:T(8,128)(2,1)}, bf16[512,2048]{1,0:T(8,128)(2,1)}) custom-call(s32[2]{0:T(128)S(1)} %pad_add_fusion.sec, bf16[512,2048]{1,0:T(8,128)(2,1)S(1)} %bitcast.121, bf16[3,2048,256]{2,1,0:T(8,128)(2,1)} %get-tuple-element.108.refs_1_.wd_ref, ...), custom_call_target="tpu_custom_call" | custom-call | flops 4831838208 | bytes 13107200 | tf_op jit(solution)/shard_map/pallas_call | solution.py:59
  431.8 7.2 all-to-all-done.8
  440.4 7.0 all-to-all-start.11
  452.7 8.2 shard_map.147
  460.9 14.4 %all-to-all-done.11 = bf16[32,16,2048]{2,1,0:T(8,128)(2,1)} async-done(((bf16[32,16,2048]{2,1,0:T(8,128)(2,1)}), bf16[32,16,2048]{2,1,0:T(8,128)(2,1)}, u32[]{:S(2)}, u32[]{:S(2)}) %all-to-all-start.11) | async-done | bytes 2097184 | tf_op jit(solution)/shard_map/all_to_all | solution.py:376
  475.3 6.3 all-to-all-start.9
  482.3 4.4 shard_map.154
  494.5 15.1 %all-to-all-done.9 = bf16[32,16,2048]{2,1,0:T(8,128)(2,1)S(1)} async-done(((bf16[32,16,2048]{2,1,0:T(8,128)(2,1)}), bf16[32,16,2048]{2,1,0:T(8,128)(2,1)S(1)}, u32[]{:S(2)}, u32[]{:S(2)}) %all-to-all-start.9) | async-done | bytes 2097184 | tf_op jit(solution)/shard_map/all_to_all | solution.py:376
  518.4 6.0 all-to-all-start.12
  524.5 10.3 %shard_map.157 = (bf16[3,512,256]{2,1,0:T(8,128)(2,1)}, bf16[3,512,256]{2,1,0:T(8,128)(2,1)}, bf16[3,768,512]{2,1,0:T(8,128)(2,1)}, bf16[3,2048,512]{2,1,0:T(8,128)(2,1)}) custom-call(s32[2]{0:T(128)S(1)} %pad_add_fusion.sec, bf16[512,2048]{1,0:T(8,128)(2,1)} %bitcast.111, ...), custom_call_target="tpu_custom_call", output_to_operand_aliasing={{2}: (5, {}), {3}: (6, {})} | custom-call | flops 3221225472 | bytes 19136512 | tf_op jit(solution)/shard_map/pallas_call | solution.py:59
  534.8 17.6 %all-to-all-done.12 = bf16[32,16,2048]{2,1,0:T(8,128)(2,1)S(1)} async-done(((bf16[32,16,2048]{2,1,0:T(8,128)(2,1)}), bf16[32,16,2048]{2,1,0:T(8,128)(2,1)S(1)}, u32[]{:S(2)}, u32[]{:S(2)}) %all-to-all-start.12) | async-done | bytes 2097184 | tf_op jit(solution)/shard_map/all_to_all | solution.py:376
  552.4 11.1 %shard_map.158 = (bf16[3,512,768]{2,1,0:T(8,128)(2,1)}, bf16[3,512,768]{2,1,0:T(8,128)(2,1)}, bf16[512,2048]{1,0:T(8,128)(2,1)}) custom-call(s32[2]{0:T(128)S(1)} %pad_add_fusion.sec, bf16[512,2048]{1,0:T(8,128)(2,1)S(1)} %bitcast.122, bf16[3,2048,256]{2,1,0:T(8,128)(2,1)} %get-tuple-element.108.refs_1_.wd_ref, ...), custom_call_target="tpu_custom_call", output_to_operand_aliasing={{0}: (6, {}), {1}: (7, {})} | custom-call | flops 4831838208 | bytes 17825792 | tf_op jit(solution)/shard_map/pallas_call | solution.py:59
  563.5 6.0 all-to-all-start.13
  569.5 5.3 shard_map.159
  574.8 22.7 %all-to-all-done.13 = bf16[32,16,2048]{2,1,0:T(8,128)(2,1)S(1)} async-done(((bf16[32,16,2048]{2,1,0:T(8,128)(2,1)}), bf16[32,16,2048]{2,1,0:T(8,128)(2,1)S(1)}, u32[]{:S(2)}, u32[]{:S(2)}) %all-to-all-start.13) | async-done | bytes 2097184 | tf_op jit(solution)/shard_map/all_to_all | solution.py:376
  601.7 7.1 collective-permute-done.5.refs_0_
  612.2 7.8 all-to-all-start.14
  620.0 10.3 %shard_map.164 = (bf16[3,512,256]{2,1,0:T(8,128)(2,1)}, bf16[3,512,256]{2,1,0:T(8,128)(2,1)}, bf16[3,768,512]{2,1,0:T(8,128)(2,1)}, bf16[3,2048,512]{2,1,0:T(8,128)(2,1)}) custom-call(s32[2]{0:T(128)S(1)} %pad_add_fusion.sec, bf16[512,2048]{1,0:T(8,128)(2,1)} %bitcast.110, bf16[512,2048]{1,0:T(8,128)(2,1)} %bitcast.98, ...), custom_call_target="tpu_custom_call", output_to_operand_aliasing={{2}: (5, {}), {3}: (6, {})} | custom-call | flops 3221225472 | bytes 19136512 | tf_op jit(solution)/shard_map/pallas_call | solution.py:59
  630.3 17.4 %all-to-all-done.14 = bf16[32,16,2048]{2,1,0:T(8,128)(2,1)S(1)} async-done(((bf16[32,16,2048]{2,1,0:T(8,128)(2,1)}), bf16[32,16,2048]{2,1,0:T(8,128)(2,1)S(1)}, u32[]{:S(2)}, u32[]{:S(2)}) %all-to-all-start.14) | async-done | bytes 2097184 | tf_op jit(solution)/shard_map/all_to_all | solution.py:376
  647.8 11.1 %shard_map.165 = (bf16[3,512,768]{2,1,0:T(8,128)(2,1)}, bf16[3,512,768]{2,1,0:T(8,128)(2,1)}, bf16[512,2048]{1,0:T(8,128)(2,1)}) custom-call(s32[2]{0:T(128)S(1)} %pad_add_fusion.sec, bf16[512,2048]{1,0:T(8,128)(2,1)S(1)} %bitcast.124, bf16[3,2048,256]{2,1,0:T(8,128)(2,1)} %get-tuple-element.108.refs_1_.wd_ref, ...), custom_call_target="tpu_custom_call", output_to_operand_aliasing={{0}: (6, {}), {1}: (7, {})} | custom-call | flops 4831838208 | bytes 17825792 | tf_op jit(solution)/shard_map/pallas_call | solution.py:59
  658.8 6.0 all-to-all-start.15
  664.9 5.2 shard_map.162
  672.9 19.9 %all-to-all-done.15 = bf16[32,16,2048]{2,1,0:T(8,128)(2,1)S(1)} async-done(((bf16[32,16,2048]{2,1,0:T(8,128)(2,1)}), bf16[32,16,2048]{2,1,0:T(8,128)(2,1)S(1)}, u32[]{:S(2)}, u32[]{:S(2)}) %all-to-all-start.15) | async-done | bytes 2097184 | tf_op jit(solution)/shard_map/all_to_all | solution.py:376
  695.7 5.9 all-to-all-start.16
  702.9 8.7 collective-permute-done.9.refs_0_
  715.1 8.0 all-to-all-start.17
  734.9 10.3 %shard_map.170 = (bf16[3,512,256]{2,1,0:T(8,128)(2,1)}, bf16[3,512,256]{2,1,0:T(8,128)(2,1)}, bf16[3,768,512]{2,1,0:T(8,128)(2,1)}, bf16[3,2048,512]{2,1,0:T(8,128)(2,1)}) custom-call(s32[2]{0:T(128)S(1)} %pad_add_fusion.sec, bf16[512,2048]{1,0:T(8,128)(2,1)} %bitcast.102, ...), custom_call_target="tpu_custom_call", output_to_operand_aliasing={{2}: (5, {}), {3}: (6, {})} | custom-call | flops 3221225472 | bytes 19202048 | tf_op jit(solution)/shard_map/pallas_call | solution.py:59
  745.3 5.7 all-to-all-done.17
  751.0 11.1 %shard_map.171 = (bf16[3,512,768]{2,1,0:T(8,128)(2,1)}, bf16[3,512,768]{2,1,0:T(8,128)(2,1)}, bf16[512,2048]{1,0:T(8,128)(2,1)}) custom-call(s32[2]{0:T(128)S(1)} %pad_add_fusion.sec, bf16[512,2048]{1,0:T(8,128)(2,1)S(1)} %bitcast.126, bf16[3,2048,256]{2,1,0:T(8,128)(2,1)} %get-tuple-element.108.refs_1_.wd_ref, ...), custom_call_target="tpu_custom_call", output_to_operand_aliasing={{0}: (6, {}), {1}: (7, {})} | custom-call | flops 4831838208 | bytes 17825792 | tf_op jit(solution)/shard_map/pallas_call | solution.py:59
  762.0 6.1 all-to-all-start.18
  768.3 5.3 shard_map.172
  773.6 18.1 %shard_map.173 = (bf16[2048,768]{1,0:T(8,128)(2,1)}, bf16[2048,768]{1,0:T(8,128)(2,1)}, bf16[768,2048]{1,0:T(8,128)(2,1)}) custom-call(s32[2]{0:T(128)S(1)} %pad_add_fusion.sec, bf16[3,2048,512]{2,1,0:T(8,128)(2,1)} %get-tuple-element.183.xt_ref.refs_4_, bf16[3,512,768]{2,1,0:T(8,128)(2,1)} %get-tuple-element.184.gg_ref, ...), custom_call_target="tpu_custom_call" | custom-call | flops 9663676416 | bytes 21757952 | tf_op jit(solution)/shard_map/pallas_call | solution.py:59
  791.7 8.7 all-to-all-done.18
  804.6 7.1 collective-permute-done.10.g_ref.refs_0_
  811.7 4.3 shard_map.175
  819.5 6.1 all-to-all-start.19
  825.6 9.7 %shard_map.178 = (bf16[3,512,256]{2,1,0:T(8,128)(2,1)}, bf16[3,512,256]{2,1,0:T(8,128)(2,1)}, bf16[3,768,512]{2,1,0:T(8,128)(2,1)}, bf16[3,2048,512]{2,1,0:T(8,128)(2,1)}) custom-call(s32[2]{0:T(128)S(1)} %pad_add_fusion.sec, bf16[512,2048]{1,0:T(8,128)(2,1)} %bitcast.99, bf16[2048,768]{1,0:T(8,128)(2,1)} %bitcast.73, ...), custom_call_target="tpu_custom_call", output_to_operand_aliasing={{2}: (4, {}), {3}: (5, {})} | custom-call | flops 3221225472 | bytes 26476544 | tf_op jit(solution)/shard_map/pallas_call | solution.py:59
  841.1 13.7 %all-to-all-done.19 = bf16[32,16,2048]{2,1,0:T(8,128)(2,1)S(1)} async-done(((bf16[32,16,2048]{2,1,0:T(8,128)(2,1)}), bf16[32,16,2048]{2,1,0:T(8,128)(2,1)S(1)}, u32[]{:S(2)}, u32[]{:S(2)}) %all-to-all-start.19) | async-done | bytes 2097184 | tf_op jit(solution)/shard_map/all_to_all | solution.py:376
  854.8 16.0 %shard_map.179 = (bf16[2048,768]{1,0:T(8,128)(2,1)}, bf16[2048,768]{1,0:T(8,128)(2,1)}, bf16[768,2048]{1,0:T(8,128)(2,1)}) custom-call(s32[2]{0:T(128)S(1)} %pad_add_fusion.sec, bf16[512,2048]{1,0:T(8,128)(2,1)S(1)} %bitcast.113, bf16[3,2048,256]{2,1,0:T(8,128)(2,1)} %get-tuple-element.108.refs_1_.wd_ref, bf16[3,512,256]{2,1,0:T(8,128)(2,1)} %get-tuple-element.193.a1_ref, ...), custom_call_target="tpu_custom_call" | custom-call | flops 6442450944 | bytes 25952256 | tf_op jit(solution)/shard_map/pallas_call | solution.py:59
  870.8 5.9 all-gather.7.cloned.1.call-done
  876.7 4.6 shard_map.176
  (161 shorter events, 132.3 us)
Async XLA Ops:
  8.0 42.1 %copy-start.22 = (bf16[1,1,768,2048]{3,2,1,0:T(8,128)(2,1)S(1)}, bf16[1,1,768,2048]{3,2,1,0:T(8,128)(2,1)}, u32[]{:S(2)}) copy-start(bf16[1,1,768,2048]{3,2,1,0:T(8,128)(2,1)} %param.15) | copy-start | bytes 9437188
  9.3 40.8 %copy-start.3 = (bf16[1,1,2048,768]{3,2,1,0:T(8,128)(2,1)S(1)}, bf16[1,1,2048,768]{3,2,1,0:T(8,128)(2,1)}, u32[]{:S(2)}) copy-start(bf16[1,1,2048,768]{3,2,1,0:T(8,128)(2,1)} %param.14) | copy-start | bytes 9437188
  12.8 37.3 %copy-start.36 = (bf16[64,2048]{1,0:T(8,128)(2,1)}, bf16[64,2048]{1,0:T(8,128)(2,1)S(1)}, u32[]{:S(2)}) copy-start(bf16[64,2048]{1,0:T(8,128)(2,1)S(1)} %get-tuple-element.105.n_ref) | copy-start | bytes 786436
  12.8 37.3 %copy-start = (bf16[1,1,2048,768]{3,2,1,0:T(8,128)(2,1)S(1)}, bf16[1,1,2048,768]{3,2,1,0:T(8,128)(2,1)}, u32[]{:S(2)}) copy-start(bf16[1,1,2048,768]{3,2,1,0:T(8,128)(2,1)} %param.13) | copy-start | bytes 9437188
  50.1 8.1 copy-start.18
  58.2 4.2 copy-start.44
  58.2 4.5 copy-start.37
  58.2 32.2 %all-to-all-start.1 = ((bf16[32,16,2048]{2,1,0:T(8,128)(2,1)}), bf16[32,16,2048]{2,1,0:T(8,128)(2,1)S(1)}, u32[]{:S(2)}, u32[]{:S(2)}) async-start(bf16[32,16,2048]{2,1,0:T(8,128)(2,1)} %bitcast.131), calls=%async_computation.1 | async-start | bytes 4194304 | tf_op jit(solution)/shard_map/all_to_all | solution.py:376
  62.7 11.9 %copy-start.10 = (bf16[2048,32]{1,0:T(8,128)(2,1)}, bf16[2048,32]{1,0:T(8,128)(2,1)S(1)}, u32[]{:S(2)}) copy-start(bf16[2048,32]{1,0:T(8,128)(2,1)S(1)} %copy.29.router_ref) | copy-start | bytes 393220
  90.3 49.5 %copy-start.4 = (bf16[1,1,2048,768]{3,2,1,0:T(8,128)(2,1)S(1)}, bf16[1,1,2048,768]{3,2,1,0:T(8,128)(2,1)}, u32[]{:S(2)}) copy-start(bf16[1,1,2048,768]{3,2,1,0:T(8,128)(2,1)} %param.14) | copy-start | bytes 9437188
  90.3 49.5 %copy-start.23 = (bf16[1,1,768,2048]{3,2,1,0:T(8,128)(2,1)S(1)}, bf16[1,1,768,2048]{3,2,1,0:T(8,128)(2,1)}, u32[]{:S(2)}) copy-start(bf16[1,1,768,2048]{3,2,1,0:T(8,128)(2,1)} %param.15) | copy-start | bytes 9437188
  93.7 6.8 collective-permute-start
  103.2 36.6 %copy-start.38 = (bf16[64,2048]{1,0:T(8,128)(2,1)}, bf16[64,2048]{1,0:T(8,128)(2,1)S(1)}, u32[]{:S(2)}) copy-start(bf16[64,2048]{1,0:T(8,128)(2,1)S(1)} %get-tuple-element.111.n_ref) | copy-start | bytes 786436
  103.2 36.7 %copy-start.1 = (bf16[1,1,2048,768]{3,2,1,0:T(8,128)(2,1)S(1)}, bf16[1,1,2048,768]{3,2,1,0:T(8,128)(2,1)}, u32[]{:S(2)}) copy-start(bf16[1,1,2048,768]{3,2,1,0:T(8,128)(2,1)} %param.13) | copy-start | bytes 9437188
  139.8 8.1 copy-start.16
  147.9 4.9 copy-start.39
  147.9 32.9 %all-to-all-start.3 = ((bf16[32,16,2048]{2,1,0:T(8,128)(2,1)}), bf16[32,16,2048]{2,1,0:T(8,128)(2,1)}, u32[]{:S(2)}, u32[]{:S(2)}) async-start(bf16[32,16,2048]{2,1,0:T(8,128)(2,1)} %bitcast.151), calls=%async_computation.3 | async-start | bytes 4194304 | tf_op jit(solution)/shard_map/all_to_all | solution.py:376
  180.8 49.6 %copy-start.24 = (bf16[1,1,768,2048]{3,2,1,0:T(8,128)(2,1)S(1)}, bf16[1,1,768,2048]{3,2,1,0:T(8,128)(2,1)}, u32[]{:S(2)}) copy-start(bf16[1,1,768,2048]{3,2,1,0:T(8,128)(2,1)} %param.15) | copy-start | bytes 9437188
  183.6 7.4 collective-permute-start.1
  193.6 36.7 %copy-start.5 = (bf16[1,1,2048,768]{3,2,1,0:T(8,128)(2,1)S(1)}, bf16[1,1,2048,768]{3,2,1,0:T(8,128)(2,1)}, u32[]{:S(2)}) copy-start(bf16[1,1,2048,768]{3,2,1,0:T(8,128)(2,1)} %param.14) | copy-start | bytes 9437188
  230.4 8.1 copy-start.17
  238.5 32.9 %all-to-all-start.5 = ((bf16[32,16,2048]{2,1,0:T(8,128)(2,1)}), bf16[32,16,2048]{2,1,0:T(8,128)(2,1)}, u32[]{:S(2)}, u32[]{:S(2)}) async-start(bf16[32,16,2048]{2,1,0:T(8,128)(2,1)} %bitcast.152), calls=%async_computation.5 | async-start | bytes 4194304 | tf_op jit(solution)/shard_map/all_to_all | solution.py:376
  271.4 49.5 %copy-start.25 = (bf16[1,1,768,2048]{3,2,1,0:T(8,128)(2,1)S(1)}, bf16[1,1,768,2048]{3,2,1,0:T(8,128)(2,1)}, u32[]{:S(2)}) copy-start(bf16[1,1,768,2048]{3,2,1,0:T(8,128)(2,1)} %param.15) | copy-start | bytes 9437188
  274.2 7.4 collective-permute-start.2
  284.3 36.7 %copy-start.6 = (bf16[1,1,2048,768]{3,2,1,0:T(8,128)(2,1)S(1)}, bf16[1,1,2048,768]{3,2,1,0:T(8,128)(2,1)}, u32[]{:S(2)}) copy-start(bf16[1,1,2048,768]{3,2,1,0:T(8,128)(2,1)} %param.14) | copy-start | bytes 9437188
  320.9 8.1 copy-start.19
  329.0 4.9 copy-start.13
  329.0 32.2 %all-to-all-start.7 = ((bf16[32,16,2048]{2,1,0:T(8,128)(2,1)}), bf16[32,16,2048]{2,1,0:T(8,128)(2,1)S(1)}, u32[]{:S(2)}, u32[]{:S(2)}) async-start(bf16[32,16,2048]{2,1,0:T(8,128)(2,1)} %bitcast.150), calls=%async_computation.7 | async-start | bytes 4194304 | tf_op jit(solution)/shard_map/all_to_all | solution.py:376
  333.2 30.3 %copy-start.34 = (bf16[2048,128]{1,0:T(8,128)(2,1)S(1)}, bf16[2048,128]{1,0:T(8,128)(2,1)}, u32[]{:S(2)}) copy-start(bf16[2048,128]{1,0:T(8,128)(2,1)} %head_ref.3) | copy-start | bytes 1572868
  335.8 27.8 %copy-start.41 = (s32[64,1]{1,0:T(8,128)S(1)}, s32[64,1]{1,0:T(8,128)}, u32[]{:S(2)}) copy-start(s32[64,1]{1,0:T(8,128)} %copy.33.label_ref) | copy-start | bytes 772
  361.2 8.6 copy-start.8
  363.6 12.2 %copy-start.27 = (bf16[64,2048]{1,0:T(8,128)(2,1)}, bf16[64,2048]{1,0:T(8,128)(2,1)S(1)}, u32[]{:S(2)}) copy-start(bf16[64,2048]{1,0:T(8,128)(2,1)S(1)} %shard_map.144.final_ref.refs_0_) | copy-start | bytes 786436
  369.7 34.0 %all-to-all-start.10 = ((bf16[32,16,2048]{2,1,0:T(8,128)(2,1)}), bf16[32,16,2048]{2,1,0:T(8,128)(2,1)S(1)}, u32[]{:S(2)}, u32[]{:S(2)}) async-start(bf16[32,16,2048]{2,1,0:T(8,128)(2,1)} %bitcast.146), calls=%async_computation.10 | async-start | bytes 4194304 | tf_op jit(solution)/shard_map/all_to_all | solution.py:376
  375.8 9.4 %collective-permute-start.3 = (bf16[64,2048]{1,0:T(8,128)(2,1)S(1)}, bf16[64,2048]{1,0:T(8,128)(2,1)S(1)}, u32[]{:S(2)}, u32[]{:S(2)}) collective-permute-start(bf16[64,2048]{1,0:T(8,128)(2,1)S(1)} %shard_map.144.final_ref.refs_0_), channel_id=1, source_target_pairs={{0,32},{32,64},{64,96},{1,33},{33,65},{65,97},{2,34},{34,66},{66,9... | collective-permute-start | bytes 786440 | tf_op jit(solution)/shard_map/ppermute | solution.py:382
  405.0 34.0 %all-to-all-start.8 = ((bf16[32,16,2048]{2,1,0:T(8,128)(2,1)}), bf16[32,16,2048]{2,1,0:T(8,128)(2,1)S(1)}, u32[]{:S(2)}, u32[]{:S(2)}) async-start(bf16[32,16,2048]{2,1,0:T(8,128)(2,1)} %bitcast.144), calls=%async_computation.8 | async-start | bytes 4194304 | tf_op jit(solution)/shard_map/all_to_all | solution.py:376
  411.1 9.7 %copy-start.30 = (bf16[32,16,2048]{2,1,0:T(8,128)(2,1)S(1)}, bf16[32,16,2048]{2,1,0:T(8,128)(2,1)}, u32[]{:S(2)}) copy-start(bf16[32,16,2048]{2,1,0:T(8,128)(2,1)} %copy-done.29) | copy-start | bytes 6291460
  440.4 7.0 copy-start.2
  440.4 35.0 %all-to-all-start.11 = ((bf16[32,16,2048]{2,1,0:T(8,128)(2,1)}), bf16[32,16,2048]{2,1,0:T(8,128)(2,1)}, u32[]{:S(2)}, u32[]{:S(2)}) async-start(bf16[32,16,2048]{2,1,0:T(8,128)(2,1)} %bitcast.149), calls=%async_computation.11 | async-start | bytes 4194304 | tf_op jit(solution)/shard_map/all_to_all | solution.py:376
  475.3 34.2 %all-to-all-start.9 = ((bf16[32,16,2048]{2,1,0:T(8,128)(2,1)}), bf16[32,16,2048]{2,1,0:T(8,128)(2,1)S(1)}, u32[]{:S(2)}, u32[]{:S(2)}) async-start(bf16[32,16,2048]{2,1,0:T(8,128)(2,1)} %bitcast.141), calls=%async_computation.9 | async-start | bytes 4194304 | tf_op jit(solution)/shard_map/all_to_all | solution.py:376
  486.8 5.9 copy-start.14
  490.5 21.4 %copy-start.35 = (bf16[2048,128]{1,0:T(8,128)(2,1)S(1)}, bf16[2048,128]{1,0:T(8,128)(2,1)}, u32[]{:S(2)}) copy-start(bf16[2048,128]{1,0:T(8,128)(2,1)} %head_ref.3) | copy-start | bytes 1572868
  490.5 23.3 %collective-permute-start.4 = (bf16[64,2048]{1,0:T(8,128)(2,1)}, bf16[64,2048]{1,0:T(8,128)(2,1)}, u32[]{:S(2)}, u32[]{:S(2)}) collective-permute-start(bf16[64,2048]{1,0:T(8,128)(2,1)} %shard_map.155), channel_id=1, source_target_pairs={{32,0},{64,32},{96,64},{33,1},{65,33},{97,65},{34,2},{66,34},{98,6... | collective-permute-start | bytes 786440 | tf_op jit(solution)/shard_map/ppermute | solution.py:382
  494.5 17.5 %copy-start.40 = (s32[64,1]{1,0:T(8,128)S(1)}, s32[64,1]{1,0:T(8,128)}, u32[]{:S(2)}) copy-start(s32[64,1]{1,0:T(8,128)} %copy.35.label_ref) | copy-start | bytes 772
  509.6 8.9 copy-start.9
  512.0 6.5 copy-start.28
  518.4 34.0 %all-to-all-start.12 = ((bf16[32,16,2048]{2,1,0:T(8,128)(2,1)}), bf16[32,16,2048]{2,1,0:T(8,128)(2,1)S(1)}, u32[]{:S(2)}, u32[]{:S(2)}) async-start(bf16[32,16,2048]{2,1,0:T(8,128)(2,1)} %bitcast.147), calls=%async_computation.12 | async-start | bytes 4194304 | tf_op jit(solution)/shard_map/all_to_all | solution.py:376
  552.4 11.1 %copy-start.31 = (bf16[32,16,2048]{2,1,0:T(8,128)(2,1)}, bf16[32,16,2048]{2,1,0:T(8,128)(2,1)S(1)}, u32[]{:S(2)}) copy-start(bf16[32,16,2048]{2,1,0:T(8,128)(2,1)S(1)} %all-to-all-done.12) | copy-start | bytes 6291460
  563.5 34.0 %all-to-all-start.13 = ((bf16[32,16,2048]{2,1,0:T(8,128)(2,1)}), bf16[32,16,2048]{2,1,0:T(8,128)(2,1)S(1)}, u32[]{:S(2)}, u32[]{:S(2)}) async-start(bf16[32,16,2048]{2,1,0:T(8,128)(2,1)} %bitcast.145), calls=%async_computation.13 | async-start | bytes 4194304 | tf_op jit(solution)/shard_map/all_to_all | solution.py:376
  600.4 8.4 collective-permute-start.5
  612.2 35.6 %all-to-all-start.14 = ((bf16[32,16,2048]{2,1,0:T(8,128)(2,1)}), bf16[32,16,2048]{2,1,0:T(8,128)(2,1)S(1)}, u32[]{:S(2)}, u32[]{:S(2)}) async-start(bf16[32,16,2048]{2,1,0:T(8,128)(2,1)} %bitcast.148), calls=%async_computation.14 | async-start | bytes 4194304 | tf_op jit(solution)/shard_map/all_to_all | solution.py:376
  647.8 11.1 %copy-start.32 = (bf16[32,16,2048]{2,1,0:T(8,128)(2,1)}, bf16[32,16,2048]{2,1,0:T(8,128)(2,1)S(1)}, u32[]{:S(2)}) copy-start(bf16[32,16,2048]{2,1,0:T(8,128)(2,1)S(1)} %all-to-all-done.14) | copy-start | bytes 6291460
  658.8 34.0 %all-to-all-start.15 = ((bf16[32,16,2048]{2,1,0:T(8,128)(2,1)}), bf16[32,16,2048]{2,1,0:T(8,128)(2,1)S(1)}, u32[]{:S(2)}, u32[]{:S(2)}) async-start(bf16[32,16,2048]{2,1,0:T(8,128)(2,1)} %bitcast.143), calls=%async_computation.15 | async-start | bytes 4194304 | tf_op jit(solution)/shard_map/all_to_all | solution.py:376
  695.7 19.4 %all-to-all-start.16 = ((bf16[32,64,128]{2,1,0:T(8,128)(2,1)}), bf16[32,64,128]{2,1,0:T(8,128)(2,1)S(1)}, u32[]{:S(2)}, u32[]{:S(2)}) async-start(bf16[32,64,128]{2,1,0:T(8,128)(2,1)} %bitcast.44), calls=%async_computation.16 | async-start | bytes 1048576 | tf_op jit(solution)/shard_map/all_to_all | solution.py:376
  701.6 10.0 %collective-permute-start.9 = (bf16[64,2048]{1,0:T(8,128)(2,1)S(1)}, bf16[64,2048]{1,0:T(8,128)(2,1)S(1)}, u32[]{:S(2)}, u32[]{:S(2)}) collective-permute-start(bf16[64,2048]{1,0:T(8,128)(2,1)S(1)} %shard_map.166), channel_id=1, source_target_pairs={{32,0},{64,32},{96,64},{33,1},{65,33},{97,65},{34,2},{66,34},{98,6... | collective-permute-start | bytes 786440 | tf_op jit(solution)/shard_map/ppermute | solution.py:382
  715.1 35.9 %all-to-all-start.17 = ((bf16[32,16,2048]{2,1,0:T(8,128)(2,1)}), bf16[32,16,2048]{2,1,0:T(8,128)(2,1)S(1)}, u32[]{:S(2)}, u32[]{:S(2)}) async-start(bf16[32,16,2048]{2,1,0:T(8,128)(2,1)} %bitcast.139), calls=%async_computation.17 | async-start | bytes 4194304 | tf_op jit(solution)/shard_map/all_to_all | solution.py:376
  723.1 112.2 %all-gather.5.cloned.1.call-start = ((), (), s32[]{:S(2)}) async-start(), calls=%async_computation.20 | async-start | bytes 2162688 | tf_op jit(solution)/shard_map/all_gather | solution.py:712
  727.7 6.6 collective-permute-start.6
  729.0 5.3 collective-permute-start.7
  729.6 4.6 collective-permute-start.8
  751.0 11.1 %copy-start.33 = (bf16[32,16,2048]{2,1,0:T(8,128)(2,1)}, bf16[32,16,2048]{2,1,0:T(8,128)(2,1)S(1)}, u32[]{:S(2)}) copy-start(bf16[32,16,2048]{2,1,0:T(8,128)(2,1)S(1)} %all-to-all-done.17) | copy-start | bytes 6291460
  762.0 38.4 %all-to-all-start.18 = ((bf16[32,16,2048]{2,1,0:T(8,128)(2,1)}), bf16[32,16,2048]{2,1,0:T(8,128)(2,1)S(1)}, u32[]{:S(2)}, u32[]{:S(2)}) async-start(bf16[32,16,2048]{2,1,0:T(8,128)(2,1)} %bitcast.140), calls=%async_computation.18 | async-start | bytes 4194304 | tf_op jit(solution)/shard_map/all_to_all | solution.py:376
  768.1 108.6 %all-gather.7.cloned.1.call-start = ((), (), s32[]{:S(2)}) async-start(), calls=%async_computation.21 | async-start | bytes 4325376 | tf_op jit(solution)/shard_map/all_gather | solution.py:715
  803.3 8.4 collective-permute-start.10
  819.5 35.3 %all-to-all-start.19 = ((bf16[32,16,2048]{2,1,0:T(8,128)(2,1)}), bf16[32,16,2048]{2,1,0:T(8,128)(2,1)S(1)}, u32[]{:S(2)}, u32[]{:S(2)}) async-start(bf16[32,16,2048]{2,1,0:T(8,128)(2,1)} %bitcast.142), calls=%async_computation.19 | async-start | bytes 4194304 | tf_op jit(solution)/shard_map/all_to_all | solution.py:376
  (11 other events, 19.5 us)
Sparse Core Ops, SparseCore 0:
  735.0 60.0 all-gather.4
  816.2 60.4 all-gather.6
